TPU v7x, 32 devices: a whole 2x2x4 slice. The times are simulated.
32 devices in a mesh: lat: 16 (over z, y, x), obs: 2 (over core).
Axes of the slice: x: 2, y: 2, z: 4, core: 2. Of those that a mesh axis runs over, the one named last changes fastest.
Arguments:
- control: bfloat16 [2, 64, 128, 3072], P(None, 'obs', 'lat'), may hold values from -8 to 8
- zonal_scales: float32 [4], replicated, may hold values from 1.5 to 360, as said below
- zonal_heights: float32 [4], replicated, may hold values from 0.25 to 0.75
- meridional_scales: float32 [4], replicated, may hold values from 0.8 to 180, as said below
- meridional_heights: float32 [4], replicated, may hold values from 0.25 to 0.75
- vertical_map: bfloat16 [2, 64, 64], replicated, may hold values from -0.75 to 0.75
- send_blocks: int32 [16, 2, 2, 2], P('lat', 'obs'), may hold values from 0 to 15
- report_slot: int32 [16, 2, 2048], P('lat', 'obs'), may hold values from 0 to 3
- report_level: int32 [16, 2, 2048], P('lat', 'obs'), may hold values from 0 to 127
- report_corner: int32 [16, 2, 4, 2048], P('lat', 'obs'), may hold values from 0 to 767, as said below
- report_weight: float32 [16, 2, 4, 2048], P('lat', 'obs'), may hold values from 0 to 1, as said below
- innovation: float32 [16, 2, 2048], P('lat', 'obs'), may hold values from -6 to 6
- report_precision: float32 [16, 2, 2048], P('lat', 'obs'), may hold values from 1 to 4
Outputs:
- weighted_departure: float32 [16, 2, 2048], P('lat', 'obs')
- control_gradient: float32 [2, 64, 128, 3072], P(None, 'obs', 'lat')
Inputs may be any that keep to these rules, and one draw needn't show every extreme that they name: `report_corner`: the corners of an observation are q, q + 1, q + 192, q + 193 in this order, with q // 192 < 3 and q % 192 < 191. `report_weight`: nonnegative bilinear weights whose four values sum to one, in the corner order of report_corner. `zonal_scales`: positive length scales. `meridional_scales`: positive length scales.
All inputs are finite; a program needn't handle non-finite values.
Results may differ from a plain program's by a relative error of at most 0.009.
Values may be sent and summed in bfloat16 or wider, within the bound.
A program may use at most 128 MiB of HBM per device.

v0:
```python
import math

import jax
import jax.numpy as jnp
from jax import lax
from jax.sharding import PartitionSpec as P

SLOTS = 2
BR = 4


def profile(distance, scales, heights):
    total = jnp.zeros(distance.shape, jnp.float32)
    for member in range(4):
        scale = scales[member]
        total = total + heights[member] * jnp.exp(
            -distance * distance / (2.0 * scale * scale)
        ) / jnp.sqrt(math.sqrt(math.pi) * scale)
    return total


def zonal_apply(source, pattern, out_shape, out_type, scales, heights):
    width = out_shape[-1]
    stride = math.gcd(width, 512)
    result = jnp.zeros(out_shape, out_type)
    column_ids = jnp.arange(width)[:, None]

    def one_block(counter, acc_field):
        start = counter * stride
        target = start + jnp.arange(stride)[None, :]
        offset = jnp.abs(column_ids - target)
        distance = jnp.minimum(offset, width - offset).astype(jnp.float32)
        kernel = profile(distance, scales, heights).astype(jnp.bfloat16)
        part_out = jnp.einsum(pattern, source, kernel, preferred_element_type=jnp.float32).astype(
            out_type
        )
        return lax.dynamic_update_slice_in_dim(acc_field, part_out, start, len(out_shape) - 1)

    return lax.fori_loop(0, width // stride, one_block, result)


def on_device(
    control,
    zonal_scales,
    zonal_heights,
    meridional_scales,
    meridional_heights,
    vertical_map,
    send_blocks,
    report_slot,
    report_level,
    report_corner,
    report_weight,
    innovation,
    report_precision,
):
    lat_count = lax.axis_size("lat")
    owner_count = lax.axis_size("obs")
    variables, level_share, band_rows, width = control.shape
    strip = width // lat_count
    all_rows = band_rows * lat_count
    levels = level_share * owner_count
    column_rows = all_rows // owner_count
    block_count = column_rows // BR
    slot_count = owner_count * SLOTS
    places = jnp.arange(all_rows)
    apart = jnp.abs(places[:, None] - places[None, :]).astype(jnp.float32)
    meridional = profile(apart, meridional_scales, meridional_heights).astype(jnp.bfloat16)
    smoothed = zonal_apply(
        control,
        "vlyx,xz->vylz",
        (variables, band_rows, level_share, width),
        jnp.bfloat16,
        zonal_scales,
        zonal_heights,
    )
    smoothed = smoothed.reshape(variables, band_rows, level_share, lat_count, strip)
    lines = lax.all_to_all(smoothed, "lat", split_axis=3, concat_axis=1, tiled=True)
    items = lines.shape[0]
    flat = lines.reshape(items, all_rows, level_share * strip)
    mixed = jnp.einsum("ay,vyc->vac", meridional, flat, preferred_element_type=jnp.float32).astype(
        jnp.bfloat16
    )
    lined = mixed.reshape(items, all_rows, level_share, strip)
    columns = lax.all_to_all(lined, "obs", split_axis=1, concat_axis=2, tiled=True)
    increment = jnp.einsum(
        "vlk,vykx->vylx", vertical_map, columns, preferred_element_type=jnp.float32
    )
    sends = send_blocks.reshape(slot_count)
    blocks = increment.reshape(variables, block_count, BR, levels, strip)
    selector = (sends[:, None] == jnp.arange(block_count)[None, :]).astype(jnp.float32)
    outgoing = jnp.einsum("sb,vbrlx->vsrlx", selector, blocks, precision=lax.Precision.HIGHEST)
    incoming = lax.all_to_all(
        outgoing.astype(jnp.bfloat16), "obs", split_axis=1, concat_axis=1, tiled=True
    ).astype(outgoing.dtype)
    slot = report_slot.reshape(1, -1)
    level_code = report_level.reshape(1, -1)
    corner = report_corner.reshape(4, -1)
    position = (
        ((level_code // levels * slot_count + slot) * BR + corner // strip) * levels
        + level_code % levels
    ) * strip + corner % strip
    values = jnp.take(incoming.reshape(-1), position)
    stencil = report_weight.reshape(4, -1)
    model_value = jnp.sum(stencil * values, axis=0).reshape(report_slot.shape)
    departure = report_precision * (model_value - innovation)
    pushes = stencil * departure.reshape(1, -1)
    spread = (
        jnp.zeros((incoming.size,), jnp.float32).at[position.reshape(-1)].add(pushes.reshape(-1))
    )
    returned = lax.all_to_all(
        spread.reshape(incoming.shape).astype(jnp.bfloat16),
        "obs",
        split_axis=1,
        concat_axis=1,
        tiled=True,
    ).astype(jnp.float32)
    adjoint = jnp.einsum(
        "sb,vsrlx->vbrlx", selector, returned, precision=lax.Precision.HIGHEST
    ).reshape(increment.shape)
    lifted = jnp.einsum(
        "vlk,vylx->vykx", vertical_map.astype(jnp.float32), adjoint, precision=lax.Precision.HIGHEST
    ).astype(jnp.bfloat16)
    lines = lax.all_to_all(lifted, "obs", split_axis=2, concat_axis=1, tiled=True)
    items = lines.shape[0]
    flat = lines.reshape(items, all_rows, level_share * strip)
    mixed = jnp.einsum("ya,vyc->vac", meridional, flat, preferred_element_type=jnp.float32).astype(
        jnp.bfloat16
    )
    returned_lines = mixed.reshape(items, all_rows, level_share, 1, strip)
    lines = lax.all_to_all(returned_lines, "lat", split_axis=1, concat_axis=3, tiled=True)
    items = lines.shape[0]
    flat = lines.reshape(items, band_rows, level_share, width)
    gradient = zonal_apply(
        flat,
        "vylx,xz->vlyz",
        (items, level_share, band_rows, width),
        jnp.float32,
        zonal_scales,
        zonal_heights,
    )
    return (departure, gradient)


def solution(mesh):
    in_specs = (
        P(None, "obs", "lat", None),
        P(),
        P(),
        P(),
        P(),
        P(),
        P("lat", "obs", None, None),
        P("lat", "obs", None),
        P("lat", "obs", None),
        P("lat", "obs", None, None),
        P("lat", "obs", None, None),
        P("lat", "obs", None),
        P("lat", "obs", None),
    )
    out_specs = (P("lat", "obs", None), P(None, "obs", "lat", None))
    return jax.shard_map(
        on_device, mesh=mesh, in_specs=in_specs, out_specs=out_specs, check_vma=False
    )
```

profile of v0, /device:TPU:12, one launch (start us, length us, event | category | flops | bytes accessed | tf_op | source)
XLA Modules:
  0.0 608.8 jit_solution(12811473287838067633)
XLA Ops:
  9.9 5.3 copy.72
  15.6 81.6 %while.32 = (s32[]{:T(128)}, bf16[2,8,32,3072]{3,2,1,0:T(8,128)(2,1)S(1)}, f32[4]{0:T(128)S(1)}, f32[]{:T(128)}, f32[]{:T(128)}, /*index=5*/f32[]{:T(128)}, f32[...) while((s32[]{:T(128)}, ...), condition=%wide.region_1.0_spmd.clone, body=%wide.region_0.0_spmd.clone.sunk | while | flops 1647051264 | bytes 3674395 | solution.py:39
  16.2 12.9 %fusion.166 = bf16[2,8,32,3072]{3,2,1,0:T(8,128)(2,1)S(1)} fusion(bf16[2,8,32,3072]{3,2,1,0:T(8,128)(2,1)S(1)} %get-tuple-element.763, s32[]{:T(128)S(6)} %select_n.204, bf16[2,32,8,3072]{3,1,2,0:T(8,128)(2,1)} %get-tuple-element.789, f32[]{:T(128)} %get-tuple-element.788, f32[]{:T(128)} %get-tuple-element.787, f32[]{:T(128)} %bitcast.216, ...), kind=kOutput, calls=%fused_computation.47.clone.1 | convolution fusion | flops 1647050752 | bytes 3672116 | tf_op jit(solution)/shard_map/while/body/eval_jaxpr/vlyx,xz->vylz/dot_general | solution.py:34
  29.8 12.9 %fusion.166 = bf16[2,8,32,3072]{3,2,1,0:T(8,128)(2,1)S(1)} fusion(bf16[2,8,32,3072]{3,2,1,0:T(8,128)(2,1)S(1)} %get-tuple-element.763, s32[]{:T(128)S(6)} %select_n.204, bf16[2,32,8,3072]{3,1,2,0:T(8,128)(2,1)} %get-tuple-element.789, f32[]{:T(128)} %get-tuple-element.788, f32[]{:T(128)} %get-tuple-element.787, f32[]{:T(128)} %bitcast.216, ...), kind=kOutput, calls=%fused_computation.47.clone.1 | convolution fusion | flops 1647050752 | bytes 3672116 | tf_op jit(solution)/shard_map/while/body/eval_jaxpr/vlyx,xz->vylz/dot_general | solution.py:34
  43.4 12.9 %fusion.166 = bf16[2,8,32,3072]{3,2,1,0:T(8,128)(2,1)S(1)} fusion(bf16[2,8,32,3072]{3,2,1,0:T(8,128)(2,1)S(1)} %get-tuple-element.763, s32[]{:T(128)S(6)} %select_n.204, bf16[2,32,8,3072]{3,1,2,0:T(8,128)(2,1)} %get-tuple-element.789, f32[]{:T(128)} %get-tuple-element.788, f32[]{:T(128)} %get-tuple-element.787, f32[]{:T(128)} %bitcast.216, ...), kind=kOutput, calls=%fused_computation.47.clone.1 | convolution fusion | flops 1647050752 | bytes 3672116 | tf_op jit(solution)/shard_map/while/body/eval_jaxpr/vlyx,xz->vylz/dot_general | solution.py:34
  57.0 12.9 %fusion.166 = bf16[2,8,32,3072]{3,2,1,0:T(8,128)(2,1)S(1)} fusion(bf16[2,8,32,3072]{3,2,1,0:T(8,128)(2,1)S(1)} %get-tuple-element.763, s32[]{:T(128)S(6)} %select_n.204, bf16[2,32,8,3072]{3,1,2,0:T(8,128)(2,1)} %get-tuple-element.789, f32[]{:T(128)} %get-tuple-element.788, f32[]{:T(128)} %get-tuple-element.787, f32[]{:T(128)} %bitcast.216, ...), kind=kOutput, calls=%fused_computation.47.clone.1 | convolution fusion | flops 1647050752 | bytes 3672116 | tf_op jit(solution)/shard_map/while/body/eval_jaxpr/vlyx,xz->vylz/dot_general | solution.py:34
  70.6 12.9 %fusion.166 = bf16[2,8,32,3072]{3,2,1,0:T(8,128)(2,1)S(1)} fusion(bf16[2,8,32,3072]{3,2,1,0:T(8,128)(2,1)S(1)} %get-tuple-element.763, s32[]{:T(128)S(6)} %select_n.204, bf16[2,32,8,3072]{3,1,2,0:T(8,128)(2,1)} %get-tuple-element.789, f32[]{:T(128)} %get-tuple-element.788, f32[]{:T(128)} %get-tuple-element.787, f32[]{:T(128)} %bitcast.216, ...), kind=kOutput, calls=%fused_computation.47.clone.1 | convolution fusion | flops 1647050752 | bytes 3672116 | tf_op jit(solution)/shard_map/while/body/eval_jaxpr/vlyx,xz->vylz/dot_general | solution.py:34
  84.2 12.9 %fusion.166 = bf16[2,8,32,3072]{3,2,1,0:T(8,128)(2,1)S(1)} fusion(bf16[2,8,32,3072]{3,2,1,0:T(8,128)(2,1)S(1)} %get-tuple-element.763, s32[]{:T(128)S(6)} %select_n.204, bf16[2,32,8,3072]{3,1,2,0:T(8,128)(2,1)} %get-tuple-element.789, f32[]{:T(128)} %get-tuple-element.788, f32[]{:T(128)} %get-tuple-element.787, f32[]{:T(128)} %bitcast.216, ...), kind=kOutput, calls=%fused_computation.47.clone.1 | convolution fusion | flops 1647050752 | bytes 3672116 | tf_op jit(solution)/shard_map/while/body/eval_jaxpr/vlyx,xz->vylz/dot_general | solution.py:34
  97.1 5.6 reshape.424
  102.7 5.7 copy.73
  108.4 7.9 %all-to-all-start = ((bf16[2,8,32,16,192]{4,2,1,0,3:T(8,128)(2,1)}), bf16[2,8,32,16,192]{4,2,1,0,3:T(8,128)(2,1)}, u32[]{:S(2)}, u32[]{:S(2)}) async-start(bf16[2,8,32,16,192]{4,2,1,0,3:T(8,128)(2,1)} %copy.73), calls=%async_computation | async-start | bytes 8388608 | tf_op jit(solution)/shard_map/all_to_all | solution.py:78
  126.2 84.2 %all-to-all-done = bf16[2,8,32,16,192]{4,2,1,0,3:T(8,128)(2,1)} async-done(((bf16[2,8,32,16,192]{4,2,1,0,3:T(8,128)(2,1)}), bf16[2,8,32,16,192]{4,2,1,0,3:T(8,128)(2,1)}, u32[]{:S(2)}, u32[]{:S(2)}) %all-to-all-start) | async-done | bytes 3145760 | tf_op jit(solution)/shard_map/all_to_all | solution.py:78
  210.4 4.9 copy.74
  215.3 6.5 %reshape.425 = bf16[2,128,6144]{2,1,0:T(8,128)(2,1)S(1)} reshape(bf16[2,16,8,32,1,192]{5,3,2,1,0,4:T(8,128)(2,1)} %copy.74) | data formatting | bytes 6291456 | tf_op jit(solution)/shard_map/reshape | solution.py:80
  221.8 5.2 convolution_convert_fusion.1
  227.0 7.6 %copy.76 = bf16[2,128,32,192]{3,2,0,1:T(8,128)(2,1)} copy(bf16[2,128,32,192]{1,3,2,0:T(8,128)(2,1)} %bitcast.235) | data formatting | bytes 6291456 | tf_op jit(solution)/shard_map/reshape | solution.py:84
  234.6 8.5 %all_to_all.73 = bf16[2,128,32,192]{3,2,0,1:T(8,128)(2,1)S(1)} all-to-all(bf16[2,128,32,192]{3,2,0,1:T(8,128)(2,1)} %copy.76), channel_id=1, replica_groups=mesh['lat'=16,'obs'=2] {'obs'}, dimensions={1} | all-to-all | bytes 6291456 | tf_op jit(solution)/shard_map/all_to_all | solution.py:85
  244.9 6.2 %fusion.101 = bf16[2,4,4,64,192]{4,1,3,2,0:T(4,128)(2,1)S(1)} fusion(f32[2,16,4,64,192]{4,3,2,1,0:T(8,128)S(1)} %bitcast.227, s32[4]{0:T(128)S(1)} %eq.19), kind=kOutput, calls=%fused_computation.103 | convolution fusion | flops 75890752 | bytes 7077904 | tf_op jit(solution)/shard_map/sb,vbrlx->vsrlx/dot_general | solution.py:92
  251.2 4.6 all_to_all.74
  257.4 2.4 reshape.437
  259.8 45.5 %gather_fusion = f32[8192]{0:T(1024)S(1)} fusion(f32[393216]{0:T(1024)S(1)} %reshape.437, s32[8192]{0:T(1024)S(1)} %broadcast_clamp_fusion), kind=kCustom, calls=%fused_computation | custom fusion | bytes 98304 | tf_op jit(solution)/shard_map/jit(_take)/gather | solution.py:103
  306.2 43.6 %scatter_custom_fusion = f32[393216]{0:T(1024)S(1)} fusion(s32[8192]{0:T(1024)S(1)} %bitcast.246, f32[8192]{0:T(1024)S(1)} %mul.590, f32[]{:T(128)} %constant.182.clone.1), kind=kCustom, calls=%fused_computation.105 | custom fusion | flops 8192 | bytes 1572868 | tf_op jit(solution)/shard_map/scatter-add | solution.py:109
  350.6 4.7 all_to_all.75
  356.7 4.9 copy.84
  361.5 4.8 convert_bitcast_fusion
  366.3 2.4 copy.86
  368.7 7.3 %all_to_all.76 = bf16[2,64,64,192]{3,1,0,2:T(8,128)(2,1)S(1)} all-to-all(bf16[2,64,64,192]{3,1,0,2:T(8,128)(2,1)S(1)} %copy.86), channel_id=1, replica_groups=mesh['lat'=16,'obs'=2] {'obs'}, dimensions={2} | all-to-all | bytes 6291456 | tf_op jit(solution)/shard_map/all_to_all | solution.py:124
  376.0 4.5 copy.124
  380.5 6.5 %reshape.433 = bf16[2,128,6144]{2,1,0:T(8,128)(2,1)S(1)} reshape(bf16[2,2,64,32,192]{4,3,2,1,0:T(8,128)(2,1)} %bitcast.230) | data formatting | bytes 6291456 | tf_op jit(solution)/shard_map/reshape | solution.py:126
  387.0 5.2 convolution_convert_fusion
  392.2 7.6 %copy.89 = bf16[2,128,32,1,192]{4,2,0,3,1:T(8,128)(2,1)} copy(bf16[2,128,32,1,192]{1,4,2,0,3:T(8,128)(2,1)} %bitcast.234) | data formatting | bytes 6291456 | tf_op jit(solution)/shard_map/reshape | solution.py:130
  399.9 5.4 all-to-all-start.5
  405.2 94.9 %all-to-all-done.5 = bf16[2,128,32,1,192]{4,2,0,3,1:T(8,128)(2,1)} async-done(((bf16[2,128,32,1,192]{4,2,0,3,1:T(8,128)(2,1)}), bf16[2,128,32,1,192]{4,2,0,3,1:T(8,128)(2,1)}, u32[]{:S(2)}, u32[]{:S(2)}) %all-to-all-start.5) | async-done | bytes 3145760 | tf_op jit(solution)/shard_map/all_to_all | solution.py:131
  500.1 2.6 copy.90
  502.8 4.9 copy.91
  507.7 7.7 %reshape.435 = bf16[2,8,32,3072]{3,2,1,0:T(8,128)(2,1)} reshape(bf16[2,8,32,16,1,192]{5,3,2,1,0,4:T(8,128)(2,1)} %copy.91) | data formatting | bytes 6291456 | tf_op jit(solution)/shard_map/reshape | solution.py:133
  515.4 3.5 broadcast_in_dim.29.clone
  518.9 88.7 %while.33 = (s32[]{:T(128)}, f32[2,32,8,3072]{3,2,1,0:T(8,128)}, f32[4]{0:T(128)S(1)}, f32[]{:T(128)}, f32[]{:T(128)}, /*index=5*/f32[]{:T(128)}, f32[]{:T(128)}...) while((s32[]{:T(128)}, f32[2,32,8,3072]{3,2,1,0:T(8,128)}, ...), condition=%wide.region_5.6_spmd.clone, body=%wide.region_4.5_spmd.clone.sunk | while | flops 1646789120 | bytes 6295835 | solution.py:39
  519.7 12.5 %fusion.170 = f32[2,32,8,512]{3,1,2,0:T(8,128)S(1)} fusion(bf16[2,8,32,3072]{3,2,1,0:T(8,128)(2,1)} %get-tuple-element.837, f32[]{:T(128)} %get-tuple-element.836, f32[]{:T(128)} %get-tuple-element.835, f32[]{:T(128)} %bitcast.223, f32[]{:T(128)} %get-tuple-element.834, f32[]{:T(128)} %get-tuple-element.833, f32[]{:T(128)} %bitcast.224, ...), kind=kOutput, calls=%fused_computation.91.clone.1 | convolution fusion | flops 1646788608 | bytes 4196400 | tf_op jit(solution)/shard_map/while/body/eval_jaxpr/vylx,xz->vlyz/dot_general | solution.py:34
  532.3 1.6 copy_dynamic-update-slice_fusion.2
  534.5 12.5 %fusion.170 = f32[2,32,8,512]{3,1,2,0:T(8,128)S(1)} fusion(bf16[2,8,32,3072]{3,2,1,0:T(8,128)(2,1)} %get-tuple-element.837, f32[]{:T(128)} %get-tuple-element.836, f32[]{:T(128)} %get-tuple-element.835, f32[]{:T(128)} %bitcast.223, f32[]{:T(128)} %get-tuple-element.834, f32[]{:T(128)} %get-tuple-element.833, f32[]{:T(128)} %bitcast.224, ...), kind=kOutput, calls=%fused_computation.91.clone.1 | convolution fusion | flops 1646788608 | bytes 4196400 | tf_op jit(solution)/shard_map/while/body/eval_jaxpr/vylx,xz->vlyz/dot_general | solution.py:34
  547.0 1.6 copy_dynamic-update-slice_fusion.2
  549.2 12.5 %fusion.170 = f32[2,32,8,512]{3,1,2,0:T(8,128)S(1)} fusion(bf16[2,8,32,3072]{3,2,1,0:T(8,128)(2,1)} %get-tuple-element.837, f32[]{:T(128)} %get-tuple-element.836, f32[]{:T(128)} %get-tuple-element.835, f32[]{:T(128)} %bitcast.223, f32[]{:T(128)} %get-tuple-element.834, f32[]{:T(128)} %get-tuple-element.833, f32[]{:T(128)} %bitcast.224, ...), kind=kOutput, calls=%fused_computation.91.clone.1 | convolution fusion | flops 1646788608 | bytes 4196400 | tf_op jit(solution)/shard_map/while/body/eval_jaxpr/vylx,xz->vlyz/dot_general | solution.py:34
  561.7 1.6 copy_dynamic-update-slice_fusion.2
  563.9 12.5 %fusion.170 = f32[2,32,8,512]{3,1,2,0:T(8,128)S(1)} fusion(bf16[2,8,32,3072]{3,2,1,0:T(8,128)(2,1)} %get-tuple-element.837, f32[]{:T(128)} %get-tuple-element.836, f32[]{:T(128)} %get-tuple-element.835, f32[]{:T(128)} %bitcast.223, f32[]{:T(128)} %get-tuple-element.834, f32[]{:T(128)} %get-tuple-element.833, f32[]{:T(128)} %bitcast.224, ...), kind=kOutput, calls=%fused_computation.91.clone.1 | convolution fusion | flops 1646788608 | bytes 4196400 | tf_op jit(solution)/shard_map/while/body/eval_jaxpr/vylx,xz->vlyz/dot_general | solution.py:34
  576.5 1.6 copy_dynamic-update-slice_fusion.2
  578.7 12.5 %fusion.170 = f32[2,32,8,512]{3,1,2,0:T(8,128)S(1)} fusion(bf16[2,8,32,3072]{3,2,1,0:T(8,128)(2,1)} %get-tuple-element.837, f32[]{:T(128)} %get-tuple-element.836, f32[]{:T(128)} %get-tuple-element.835, f32[]{:T(128)} %bitcast.223, f32[]{:T(128)} %get-tuple-element.834, f32[]{:T(128)} %get-tuple-element.833, f32[]{:T(128)} %bitcast.224, ...), kind=kOutput, calls=%fused_computation.91.clone.1 | convolution fusion | flops 1646788608 | bytes 4196400 | tf_op jit(solution)/shard_map/while/body/eval_jaxpr/vylx,xz->vlyz/dot_general | solution.py:34
  593.4 12.5 %fusion.170 = f32[2,32,8,512]{3,1,2,0:T(8,128)S(1)} fusion(bf16[2,8,32,3072]{3,2,1,0:T(8,128)(2,1)} %get-tuple-element.837, f32[]{:T(128)} %get-tuple-element.836, f32[]{:T(128)} %get-tuple-element.835, f32[]{:T(128)} %bitcast.223, f32[]{:T(128)} %get-tuple-element.834, f32[]{:T(128)} %get-tuple-element.833, f32[]{:T(128)} %bitcast.224, ...), kind=kOutput, calls=%fused_computation.91.clone.1 | convolution fusion | flops 1646788608 | bytes 4196400 | tf_op jit(solution)/shard_map/while/body/eval_jaxpr/vylx,xz->vlyz/dot_general | solution.py:34
  (85 shorter events, 21.7 us)
Async XLA Ops:
  0.6 243.0 %copy-start = (bf16[2,64,64]{2,1,0:T(8,128)(2,1)S(1)}, bf16[2,64,64]{2,1,0:T(8,128)(2,1)}, u32[]{:S(2)}) copy-start(bf16[2,64,64]{2,1,0:T(8,128)(2,1)} %param.22) | copy-start | bytes 49156
  0.6 14.9 %copy-start.2 = (f32[4]{0:T(128)S(1)}, f32[4]{0:T(128)}, u32[]{:S(2)}) copy-start(f32[4]{0:T(128)} %param.19) | copy-start | bytes 52
  108.4 8.0 %copy-start.6 = (f32[4]{0:T(128)S(1)}, f32[4]{0:T(128)}, u32[]{:S(2)}) copy-start(f32[4]{0:T(128)} %param.20) | copy-start | bytes 52
  108.4 16.4 %copy-start.12 = (s32[1,1,2,2]{3,2,1,0:T(2,128)S(1)}, s32[1,1,2,2]{3,2,1,0:T(2,128)}, u32[]{:S(2)}) copy-start(s32[1,1,2,2]{3,2,1,0:T(2,128)} %param.23) | copy-start | bytes 52
  108.4 16.5 %copy-start.8 = (s32[1,1,2048]{2,1,0:T(1,128)S(1)}, s32[1,1,2048]{2,1,0:T(1,128)}, u32[]{:S(2)}) copy-start(s32[1,1,2048]{2,1,0:T(1,128)} %param.24) | copy-start | bytes 24580
  108.4 16.5 %copy-start.9 = (s32[1,1,2048]{2,1,0:T(1,128)S(1)}, s32[1,1,2048]{2,1,0:T(1,128)}, u32[]{:S(2)}) copy-start(s32[1,1,2048]{2,1,0:T(1,128)} %param.25) | copy-start | bytes 24580
  108.4 16.5 %copy-start.3 = (s32[1,1,4,2048]{3,2,1,0:T(4,128)S(1)}, s32[1,1,4,2048]{3,2,1,0:T(4,128)}, u32[]{:S(2)}) copy-start(s32[1,1,4,2048]{3,2,1,0:T(4,128)} %param.26) | copy-start | bytes 98308
  108.4 16.6 %copy-start.4 = (f32[1,1,4,2048]{3,2,1,0:T(4,128)S(1)}, f32[1,1,4,2048]{3,2,1,0:T(4,128)}, u32[]{:S(2)}) copy-start(f32[1,1,4,2048]{3,2,1,0:T(4,128)} %param.27) | copy-start | bytes 98308
  108.4 16.9 %copy-start.7 = (f32[4]{0:T(128)S(1)}, f32[4]{0:T(128)}, u32[]{:S(2)}) copy-start(f32[4]{0:T(128)} %param.21) | copy-start | bytes 52
  108.4 102.0 %all-to-all-start = ((bf16[2,8,32,16,192]{4,2,1,0,3:T(8,128)(2,1)}), bf16[2,8,32,16,192]{4,2,1,0,3:T(8,128)(2,1)}, u32[]{:S(2)}, u32[]{:S(2)}) async-start(bf16[2,8,32,16,192]{4,2,1,0,3:T(8,128)(2,1)} %copy.73), calls=%async_computation | async-start | bytes 8388608 | tf_op jit(solution)/shard_map/all_to_all | solution.py:78
  259.8 45.7 %copy-start.10 = (f32[1,1,2048]{2,1,0:T(1,128)S(1)}, f32[1,1,2048]{2,1,0:T(1,128)}, u32[]{:S(2)}) copy-start(f32[1,1,2048]{2,1,0:T(1,128)} %param.29) | copy-start | bytes 24580
  259.8 45.7 %copy-start.11 = (f32[1,1,2048]{2,1,0:T(1,128)S(1)}, f32[1,1,2048]{2,1,0:T(1,128)}, u32[]{:S(2)}) copy-start(f32[1,1,2048]{2,1,0:T(1,128)} %param.28) | copy-start | bytes 24580
  305.5 0.6 copy-start.5
  399.9 100.3 %all-to-all-start.5 = ((bf16[2,128,32,1,192]{4,2,0,3,1:T(8,128)(2,1)}), bf16[2,128,32,1,192]{4,2,0,3,1:T(8,128)(2,1)}, u32[]{:S(2)}, u32[]{:S(2)}) async-start(bf16[2,128,32,1,192]{4,2,0,3,1:T(8,128)(2,1)} %copy.89), calls=%async_computation.5 | async-start | bytes 8388608 | tf_op jit(solution)/shard_map/all_to_all | solution.py:131
  607.6 0.8 copy-start.1
where the time goes:
time: 618 us; the launch traced here: 609 us
  waiting for transfers between devices  179 us (29%)
  matrix products  177 us (29%)
  local copies, waits for them, and re-layouts  153 us (25%)
  other arithmetic  44.2 us (7%)
  blocking collectives  25.1 us (4%)
  between operations  17.1 us (3%)
  starting transfers between devices  13.3 us (2%)
    dot_general x12, matrix products, one_block(): jnp.einsum(pattern, source, kernel, preferred_element_type=jnp.float32)  153 us
    all_to_all x1, waiting for transfers between devices, on_device(): lax.all_to_all(returned_lines, 'lat', split_axis=1, concat_axis=3, tiled=...  94.9 us
    all_to_all x1, waiting for transfers between devices, on_device(): lax.all_to_all(smoothed, 'lat', split_axis=3, concat_axis=1, tiled=True)  84.2 us
    gather x2, local copies, waits for them, and re-layouts, on_device(): values = jnp.take(incoming.reshape(-1), position)  45.6 us
    scatter-add x1, other arithmetic, on_device(): jnp.zeros((incoming.size,), jnp.float32).at[position.reshape(-1)]  43.6 us
    reshape x2, local copies, waits for them, and re-layouts, on_device(): flat = lines.reshape(items, all_rows, level_share * strip)  13 us
  transfers between devices with their start and end apart: 2, of which 2 were waited for; matrix products, arithmetic and copies ran while one was open for 0% of the time, Pallas kernels for 0%

commit v1 on v0

v1 whole, which is shorter than its diff:
```python
import functools
import math

import jax
import jax.numpy as jnp
from jax import lax
from jax.experimental import pallas as pl
from jax.experimental.pallas import tpu as pltpu
from jax.sharding import PartitionSpec as P

SLOTS = 2
BR = 4
TILE = 256
F32 = jnp.float32
BF16 = jnp.bfloat16


def coefficients(scales, heights):
    rate = -1.0 / (2.0 * scales * scales)
    gain = heights / jnp.sqrt(math.sqrt(math.pi) * scales)
    return jnp.concatenate([rate, gain]).astype(F32)


def gaussians(distance, coef):
    square = distance * distance
    total = coef[4] * jnp.exp(square * coef[0])
    for member in range(1, 4):
        total = total + coef[4 + member] * jnp.exp(square * coef[member])
    return total


def params(mib=48):
    return pltpu.CompilerParams(vmem_limit_bytes=mib * 1024 * 1024)


def cost(flops, nbytes):
    return pl.CostEstimate(flops=int(flops), bytes_accessed=int(nbytes), transcendentals=0)


def wide_table_kernel(width, coef, out):
    step = 512

    def piece(at, carry):
        start = pl.multiple_of(at * step, step)
        lane = lax.broadcasted_iota(jnp.int32, (TILE, step), 1) + start
        row = lax.broadcasted_iota(jnp.int32, (TILE, step), 0)
        offset = jnp.abs(lane - row)
        distance = jnp.minimum(offset, width - offset).astype(F32)
        value = gaussians(distance, coef).astype(BF16)
        out[:, pl.ds(start, step)] = value
        out[:, pl.ds(start + width, step)] = value
        return carry

    lax.fori_loop(0, width // step, piece, 0)


def tall_table_kernel(width, coef, out):
    step = 512

    def piece(at, carry):
        start = pl.multiple_of(at * step, step)
        row = lax.broadcasted_iota(jnp.int32, (step, TILE), 0) + start
        lane = lax.broadcasted_iota(jnp.int32, (step, TILE), 1)
        offset = jnp.abs(lane - row)
        distance = jnp.minimum(offset, width - offset).astype(F32)
        value = gaussians(distance, coef).astype(BF16)
        out[pl.ds(start, step), :] = value
        out[pl.ds(start + width, step), :] = value
        return carry

    lax.fori_loop(0, width // step, piece, 0)


def table(kernel, shape, width, coef):
    return pl.pallas_call(
        functools.partial(kernel, width),
        out_shape=jax.ShapeDtypeStruct(shape, BF16),
        in_specs=[pl.BlockSpec(memory_space=pltpu.SMEM)],
        out_specs=pl.BlockSpec(memory_space=pltpu.VMEM),
        compiler_params=params(),
        cost_estimate=cost(shape[0] * shape[1] * 30, shape[0] * shape[1] * 2),
    )(coef)


def zonal_forward_kernel(width, control, wide, out, turned):
    at = pl.program_id(0)

    @pl.when(at == 0)
    def _():
        for part in range(width // TILE):
            cells = slice(part * TILE, (part + 1) * TILE)
            turned[cells, :] = control[0, :, cells].T

    start = pl.multiple_of(width - at * TILE, TILE)
    out[...] = jnp.dot(
        wide[:, pl.ds(start, width)], turned[...], preferred_element_type=F32
    ).astype(BF16)


def zonal_forward(control, wide, variable):
    _, rows, width = control.shape
    return pl.pallas_call(
        functools.partial(zonal_forward_kernel, width),
        out_shape=jax.ShapeDtypeStruct((width, rows), BF16),
        grid=(width // TILE,),
        in_specs=[
            pl.BlockSpec((1, rows, width), lambda at: (variable, 0, 0)),
            pl.BlockSpec((TILE, 2 * width), lambda at: (0, 0)),
        ],
        out_specs=pl.BlockSpec((TILE, rows), lambda at: (at, 0)),
        scratch_shapes=[pltpu.VMEM((width, rows), BF16)],
        compiler_params=params(),
        cost_estimate=cost(2 * rows * width * width, 10 * rows * width),
    )(control, wide)


def zonal_backward_kernel(width, lines, tall, *rest):
    out, turned = rest[-2:]
    at = pl.program_id(0)

    @pl.when(at == 0)
    def _():
        for part in range(width // TILE):
            cells = slice(part * TILE, (part + 1) * TILE)
            turned[:, cells] = lines[cells, :].T

    start = pl.multiple_of(width - at * TILE, TILE)
    out[0] = jnp.dot(turned[...], tall[pl.ds(start, width), :], preferred_element_type=F32)


def zonal_backward(lines, tall, variables, variable, gradient):
    width, rows = lines.shape
    operands = [lines, tall]
    in_specs = [
        pl.BlockSpec((width, rows), lambda at: (0, 0)),
        pl.BlockSpec((2 * width, TILE), lambda at: (0, 0)),
    ]
    aliases = {}
    if gradient is not None:
        operands.append(gradient)
        in_specs.append(pl.BlockSpec(memory_space=pl.ANY))
        aliases = {2: 0}
    return pl.pallas_call(
        functools.partial(zonal_backward_kernel, width),
        out_shape=jax.ShapeDtypeStruct((variables, rows, width), F32),
        grid=(width // TILE,),
        in_specs=in_specs,
        out_specs=pl.BlockSpec((1, rows, TILE), lambda at: (variable, 0, at)),
        scratch_shapes=[pltpu.VMEM((rows, width), BF16)],
        input_output_aliases=aliases,
        compiler_params=params(),
        cost_estimate=cost(2 * rows * width * width, 12 * rows * width),
    )(*operands)


def band_matrix(spread, levels, dtype):
    rows, columns = spread.shape
    full = jnp.broadcast_to(spread[None], (levels, rows, columns))
    level = lax.broadcasted_iota(jnp.int32, full.shape, 0)
    lane = lax.broadcasted_iota(jnp.int32, full.shape, 2)
    full = jnp.where(lane % levels == level, full, 0.0)
    return full.reshape(levels * rows, columns).astype(dtype)


def meridional_forward_kernel(levels, owners, lines, spread, out, total):
    at = pl.program_id(0)
    product = jnp.dot(
        lines[0], band_matrix(spread[...], levels, BF16), preferred_element_type=F32
    )

    @pl.when(at == 0)
    def _():
        total[...] = product

    @pl.when(at > 0)
    def _():
        total[...] += product

    @pl.when(at == pl.num_programs(0) - 1)
    def _():
        share = total.shape[1] // owners
        for owner in range(owners):
            out[owner] = total[:, owner * share : (owner + 1) * share].astype(BF16)


def meridional_forward(lines, spread, levels, owners):
    bands, strip, rows = lines.shape
    columns = spread.shape[1]
    band_rows = rows // levels
    return pl.pallas_call(
        functools.partial(meridional_forward_kernel, levels, owners),
        out_shape=jax.ShapeDtypeStruct((owners, strip, columns // owners), BF16),
        grid=(bands,),
        in_specs=[
            pl.BlockSpec((1, strip, rows), lambda at: (at, 0, 0)),
            pl.BlockSpec((band_rows, columns), lambda at: (at, 0)),
        ],
        out_specs=pl.BlockSpec((owners, strip, columns // owners), lambda at: (0, 0, 0)),
        scratch_shapes=[pltpu.VMEM((strip, columns), F32)],
        compiler_params=params(),
        cost_estimate=cost(2 * bands * strip * rows * columns, 2 * bands * strip * rows),
    )(lines, spread)


def meridional_backward_kernel(levels, owners, lifted, spread, out):
    matrix = band_matrix(spread[...], levels, BF16)
    share = matrix.shape[1] // owners
    total = None
    for owner in range(owners):
        part = lax.dot_general(
            lifted[owner],
            matrix[:, owner * share : (owner + 1) * share],
            (((1,), (1,)), ((), ())),
            preferred_element_type=F32,
        )
        total = part if total is None else total + part
    out[0] = total.astype(BF16)


def meridional_backward(lifted, spread, levels, bands):
    owners, strip, share = lifted.shape
    all_rows, columns = spread.shape
    band_rows = all_rows // bands
    rows = levels * band_rows
    return pl.pallas_call(
        functools.partial(meridional_backward_kernel, levels, owners),
        out_shape=jax.ShapeDtypeStruct((bands, strip, rows), BF16),
        grid=(bands,),
        in_specs=[
            pl.BlockSpec((owners, strip, share), lambda at: (0, 0, 0)),
            pl.BlockSpec((band_rows, columns), lambda at: (at, 0)),
        ],
        out_specs=pl.BlockSpec((1, strip, rows), lambda at: (at, 0, 0)),
        compiler_params=params(),
        cost_estimate=cost(2 * bands * strip * rows * columns, 2 * bands * strip * rows),
    )(lifted, spread)


def stencil_kernel(places, weights, out):
    cells = lax.broadcasted_iota(jnp.int32, out.shape, 1)
    value = jnp.zeros(out.shape, F32)
    for corner in range(4):
        hit = cells == places[:, corner : corner + 1]
        value = jnp.where(hit, weights[:, corner : corner + 1], value)
    out[...] = value.astype(BF16)


def stencil(places, weights, points):
    reports = places.shape[0]
    block = min(reports, 256)
    return pl.pallas_call(
        stencil_kernel,
        out_shape=jax.ShapeDtypeStruct((reports, points), BF16),
        grid=(reports // block,),
        in_specs=[
            pl.BlockSpec((block, 4), lambda at: (at, 0)),
            pl.BlockSpec((block, 4), lambda at: (at, 0)),
        ],
        out_specs=pl.BlockSpec((block, points), lambda at: (at, 0)),
        compiler_params=params(),
        cost_estimate=cost(10 * reports * points, 2 * reports * points),
    )(places, weights)


def turned_stencil_kernel(places, weights, out):
    base = pl.program_id(0) * out.shape[0]
    cells = lax.broadcasted_iota(jnp.int32, out.shape, 0) + base
    value = jnp.zeros(out.shape, F32)
    for corner in range(4):
        hit = cells == places[corner : corner + 1, :]
        value = jnp.where(hit, weights[corner : corner + 1, :], value)
    out[...] = value.astype(BF16)


def turned_stencil(places, weights, points):
    reports = places.shape[1]
    block = math.gcd(points, 256)
    return pl.pallas_call(
        turned_stencil_kernel,
        out_shape=jax.ShapeDtypeStruct((points, reports), BF16),
        grid=(points // block,),
        in_specs=[
            pl.BlockSpec((4, reports), lambda at: (0, 0)),
            pl.BlockSpec((4, reports), lambda at: (0, 0)),
        ],
        out_specs=pl.BlockSpec((block, reports), lambda at: (at, 0)),
        compiler_params=params(),
        cost_estimate=cost(10 * reports * points, 2 * reports * points),
    )(places, weights)


def observe_kernel(matrix, field, mapping, innovation, precision, departure, pushes):
    values = jnp.dot(matrix[...], field[...], preferred_element_type=F32)
    mapped = mapping[...]
    model = jnp.sum(values * mapped, axis=1, keepdims=True)
    result = precision[...] * (model - innovation[...])
    departure[...] = result
    pushes[...] = (mapped * result).astype(BF16)


def observe(matrix, field, mapping, innovation, precision):
    reports, points = matrix.shape
    levels = field.shape[1]
    block = min(reports, 256)
    column = pl.BlockSpec((block, 1), lambda at: (at, 0))
    return pl.pallas_call(
        observe_kernel,
        out_shape=(
            jax.ShapeDtypeStruct((reports, 1), F32),
            jax.ShapeDtypeStruct((reports, levels), BF16),
        ),
        grid=(reports // block,),
        in_specs=[
            pl.BlockSpec((block, points), lambda at: (at, 0)),
            pl.BlockSpec((points, levels), lambda at: (0, 0)),
            pl.BlockSpec((block, levels), lambda at: (at, 0)),
            column,
            column,
        ],
        out_specs=(column, pl.BlockSpec((block, levels), lambda at: (at, 0))),
        compiler_params=params(),
        cost_estimate=cost(4 * reports * points * 128, 2 * reports * points),
    )(matrix, field, mapping, innovation, precision)


def spread_kernel(matrix, pushes, out):
    out[...] = jnp.dot(matrix[...], pushes[...], preferred_element_type=F32).astype(BF16)


def spread_reports(matrix, pushes):
    points, reports = matrix.shape
    levels = pushes.shape[1]
    block = math.gcd(points, 768)
    return pl.pallas_call(
        spread_kernel,
        out_shape=jax.ShapeDtypeStruct((points, levels), BF16),
        grid=(points // block,),
        in_specs=[
            pl.BlockSpec((block, reports), lambda at: (at, 0)),
            pl.BlockSpec((reports, levels), lambda at: (0, 0)),
        ],
        out_specs=pl.BlockSpec((block, levels), lambda at: (at, 0)),
        compiler_params=params(),
        cost_estimate=cost(4 * reports * points * 128, 2 * reports * points),
    )(matrix, pushes)


def on_device(
    control,
    zonal_scales,
    zonal_heights,
    meridional_scales,
    meridional_heights,
    vertical_map,
    send_blocks,
    report_slot,
    report_level,
    report_corner,
    report_weight,
    innovation,
    report_precision,
):
    lat_count = lax.axis_size("lat")
    owners = lax.axis_size("obs")
    variables, share, band_rows, width = control.shape
    strip = width // lat_count
    all_rows = band_rows * lat_count
    levels = share * owners
    slots = owners * SLOTS
    kept = slots * BR
    points = strip * kept
    reports = report_slot.shape[-1]

    zonal = coefficients(zonal_scales, zonal_heights)
    wide = table(wide_table_kernel, (TILE, 2 * width), width, zonal)
    fields = control.reshape(variables, share * band_rows, width)
    sent = []
    for variable in range(variables):
        smooth = zonal_forward(fields, wide, variable).reshape(lat_count, strip, -1)
        sent.append(lax.all_to_all(smooth, "lat", split_axis=0, concat_axis=0, tiled=True))

    tall = table(tall_table_kernel, (2 * width, TILE), width, zonal)

    blocks = lax.all_gather(send_blocks.reshape(owners, SLOTS), "obs", axis=0)
    source = jnp.arange(owners)[:, None, None]
    starts = jnp.transpose(source * (all_rows // owners) + blocks * BR, (1, 0, 2))
    rows = starts[..., None] + jnp.arange(BR)
    lanes = jnp.repeat(rows.reshape(-1), share)
    apart = jnp.abs(jnp.arange(all_rows)[:, None] - lanes[None, :]).astype(F32)
    meridional = coefficients(meridional_scales, meridional_heights)
    spread = gaussians(apart, meridional).astype(BF16).astype(F32)

    slot = report_slot.reshape(1, reports)
    code = report_level.reshape(reports)
    corner = report_corner.reshape(4, reports)
    weight = report_weight.reshape(4, reports)
    places = (corner % strip) * kept + slot * BR + corner // strip
    matrix = stencil(places.T, weight.T, points)
    turned = turned_stencil(places, weight, points)
    chosen = (code[:, None] == jnp.arange(variables * levels)[None, :]).astype(BF16)
    innovations = innovation.reshape(reports, 1)
    precisions = report_precision.reshape(reports, 1)

    departures = []
    lines = []
    for variable in range(variables):
        mapping = jnp.dot(
            chosen[:, variable * levels : (variable + 1) * levels],
            vertical_map[variable],
            preferred_element_type=F32,
        )
        mixed = meridional_forward(sent[variable], spread, share, owners)
        taken = lax.all_to_all(mixed, "obs", split_axis=0, concat_axis=0, tiled=True)
        field = taken.reshape(owners, points, share).transpose(1, 0, 2).reshape(points, levels)
        departure, pushes = observe(matrix, field, mapping, innovations, precisions)
        departures.append(departure.reshape(reports))
        adjoint = spread_reports(turned, pushes)
        parts = adjoint.reshape(points, owners, share).transpose(1, 0, 2)
        lifted = lax.all_to_all(
            parts.reshape(owners, strip, kept * share), "obs", split_axis=0, concat_axis=0, tiled=True
        )
        back = meridional_backward(lifted, spread, share, lat_count)
        lines.append(lax.all_to_all(back, "lat", split_axis=0, concat_axis=0, tiled=True))

    gradient = None
    for variable in range(variables):
        gradient = zonal_backward(
            lines[variable].reshape(width, -1), tall, variables, variable, gradient
        )
    departure = departures[0]
    for variable in range(1, variables):
        departure = jnp.where(code >= variable * levels, departures[variable], departure)
    return (departure.reshape(report_slot.shape), gradient.reshape(control.shape))


def solution(mesh):
    in_specs = (
        P(None, "obs", "lat", None),
        P(),
        P(),
        P(),
        P(),
        P(),
        P("lat", "obs", None, None),
        P("lat", "obs", None),
        P("lat", "obs", None),
        P("lat", "obs", None, None),
        P("lat", "obs", None, None),
        P("lat", "obs", None),
        P("lat", "obs", None),
    )
    out_specs = (P("lat", "obs", None), P(None, "obs", "lat", None))
    return jax.shard_map(
        on_device, mesh=mesh, in_specs=in_specs, out_specs=out_specs, check_vma=False
    )
```

time: 618 us -> 312 us (0.50); the launches traced: 609 us -> 310 us
  matrix products: 177 us -> 1.74 us
  Pallas kernels: 0 us -> 145 us
  waiting for transfers between devices: 179 us -> 65.2 us
  local copies, waits for them, and re-layouts: 153 us -> 43.4 us
  other arithmetic: 44.2 us -> 10.6 us
  between operations: 17.1 us -> 0.96 us
  starting transfers between devices: 13.3 us -> 27.6 us
  blocking collectives: 25.1 us -> 15.4 us
    dot_general x18 -> x2, matrix products: 177 us -> 1.74 us  [on_device(): jnp.dot(chosen[:, variable * levels:(variable + 1) * levels], vertical_ma...]
    pallas_call x0 -> x16, Pallas kernels: none -> 145 us  [the longest x2 21 us: zonal_forward(): pl.pallas_call(functools.partial(zonal_forward_kernel, width), out_shape=...]
    all_to_all x2 -> x5, waiting for transfers between devices: 179 us -> 65.2 us  [the longest x2 48.8 us: on_device(): lax.all_to_all(back, 'lat', split_axis=0, concat_axis=0, tiled=True)]
    gather x2 -> x0, local copies, waits for them, and re-layouts: 45.6 us -> none  [on_device(): values = jnp.take(incoming.reshape(-1), position)]
    scatter-add x1 -> x0, other arithmetic: 43.6 us -> none  [on_device(): jnp.zeros((incoming.size,), jnp.float32).at[position.reshape(-1)]]
    reshape x9 -> x8, local copies, waits for them, and re-layouts: 51.1 us -> 15.7 us  [the longest x4 10.1 us: on_device(): taken.reshape(owners, points, share).transpose(1, 0, 2)]
    all_to_all x5 -> x0, local copies, waits for them, and re-layouts: 17.4 us -> none  [the longest x2 7.53 us: on_device(): lax.all_to_all(returned_lines, 'lat', split_axis=1, concat_axis=3, tiled=...]
    all_to_all x2 -> x5, starting transfers between devices: 13.3 us -> 27.6 us  [the longest x2 12.1 us: on_device(): lax.all_to_all(back, 'lat', split_axis=0, concat_axis=0, tiled=True)]
  transfers between devices with their start and end apart: 2 -> 5, of which waited for: 2 -> 3; matrix products, arithmetic and copies ran while one was open for 0% -> 7% of each run, Pallas kernels for 0% -> 23%
where the time goes in v1:
time: 312 us; the launch traced here: 310 us
  Pallas kernels  145 us (46%)
  waiting for transfers between devices  65.2 us (21%)
  local copies, waits for them, and re-layouts  43.4 us (14%)
  starting transfers between devices  27.6 us (9%)
  blocking collectives  15.4 us (5%)
  other arithmetic  10.6 us (3%)
    all_to_all x2, waiting for transfers between devices, on_device(): lax.all_to_all(back, 'lat', split_axis=0, concat_axis=0, tiled=True)  48.8 us
    pallas_call x2, Pallas kernels, zonal_forward(): pl.pallas_call(functools.partial(zonal_forward_kernel, width), out_shape=...  21 us
    pallas_call x1, Pallas kernels, stencil(): pl.pallas_call(stencil_kernel, out_shape=jax.ShapeDtypeStruct((reports, p...  20.6 us
    pallas_call x2, Pallas kernels, observe(): pl.pallas_call(observe_kernel, out_shape=(jax.ShapeDtypeStruct((reports,...  19.4 us
    pallas_call x2, Pallas kernels, zonal_backward(): pl.pallas_call(functools.partial(zonal_backward_kernel, width), out_shape...  18.9 us
    all_to_all x2, waiting for transfers between devices, on_device(): lax.all_to_all(smooth, 'lat', split_axis=0, concat_axis=0, tiled=True)  16.4 us
    pallas_call x2, Pallas kernels, meridional_backward(): pl.pallas_call(functools.partial(meridional_backward_kernel, levels, owne...  16.4 us
    pallas_call x2, Pallas kernels, meridional_forward(): pl.pallas_call(functools.partial(meridional_forward_kernel, levels, owner...  16.1 us
  transfers between devices with their start and end apart: 5, of which 3 were waited for; matrix products, arithmetic and copies ran while one was open for 7% of the time, Pallas kernels for 23%

profile of v1, /device:TPU:12, one launch (start us, length us, event | category | flops | bytes accessed | tf_op | source)
XLA Modules:
  0.0 309.5 jit_solution(12903027375939398260)
XLA Ops:
  1.4 3.6 %shard_map.141.wide = bf16[256,6144]{1,0:T(8,128)(2,1)S(1)} custom-call(f32[8]{0:T(128)S(1)} %pad_maximum_fusion.coef), custom_call_target="tpu_custom_call" | custom-call | flops 47185920 | bytes 3145728 | tf_op jit(solution)/shard_map/pallas_call | solution.py:75
  5.0 1.7 copy-done.4
  6.7 10.4 %shard_map.142 = bf16[3072,256]{1,0:T(8,128)(2,1)} custom-call(bf16[2,256,3072]{2,1,0:T(8,128)(2,1)S(1)} %bitcast.74, bf16[256,6144]{1,0:T(8,128)(2,1)} %copy-done.4), custom_call_target="tpu_custom_call" | custom-call | flops 4831838208 | bytes 7864320 | tf_op jit(solution)/shard_map/pallas_call | solution.py:102
  17.1 7.3 %all-to-all-start = ((bf16[16,192,256]{2,1,0:T(8,128)(2,1)}), bf16[16,192,256]{2,1,0:T(8,128)(2,1)S(1)}, u32[]{:S(2)}, u32[]{:S(2)}) async-start(bf16[16,192,256]{2,1,0:T(8,128)(2,1)} %bitcast.8), calls=%async_computation | async-start | bytes 3145728 | tf_op jit(solution)/shard_map/all_to_all | solution.py:380
  24.4 1.8 all-gather
  27.3 5.4 %fusion.4.spread = f32[128,1024]{1,0:T(8,128)S(1)} fusion(f32[]{:T(128)} %bitcast.18, f32[]{:T(128)} %bitcast.17, f32[]{:T(128)} %bitcast.16, f32[]{:T(128)} %bitcast.15, f32[]{:T(128)} %bitcast.14, f32[]{:T(128)} %bitcast.13, f32[]{:T(128)} %bitcast.12, s32[1024]{0:T(1024)S(1)} %sub.23, f32[]{:T(128)} %bitcast.9), kind=kLoop, calls=%fused_computation.6 | loop fusion | flops 2228224 | bytes 528416 | tf_op jit(solution)/shard_map/convert_element_type | solution.py:391
  32.7 1.9 copy-done.12
  34.6 10.6 %shard_map.145 = bf16[3072,256]{1,0:T(8,128)(2,1)} custom-call(bf16[2,256,3072]{2,1,0:T(8,128)(2,1)S(1)} %bitcast.75, bf16[256,6144]{1,0:T(8,128)(2,1)} %copy-done.4), custom_call_target="tpu_custom_call" | custom-call | flops 4831838208 | bytes 7864320 | tf_op jit(solution)/shard_map/pallas_call | solution.py:102
  45.2 16.4 %all-to-all-done.lines = bf16[16,192,256]{2,1,0:T(8,128)(2,1)S(1)} async-done(((bf16[16,192,256]{2,1,0:T(8,128)(2,1)}), bf16[16,192,256]{2,1,0:T(8,128)(2,1)S(1)}, u32[]{:S(2)}, u32[]{:S(2)}) %all-to-all-start) | async-done | bytes 1572896 | tf_op jit(solution)/shard_map/all_to_all | solution.py:380
  61.6 5.7 %shard_map.143 = bf16[2,192,512]{2,1,0:T(8,128)(2,1)S(1)} custom-call(bf16[16,192,256]{2,1,0:T(8,128)(2,1)S(1)} %all-to-all-done.lines, f32[128,1024]{1,0:T(8,128)S(1)} %fusion.4.spread), custom_call_target="tpu_custom_call" | custom-call | flops 1610612736 | bytes 1572864 | tf_op jit(solution)/shard_map/pallas_call | solution.py:190
  67.3 4.8 %all_to_all.40 = bf16[2,192,512]{2,1,0:T(8,128)(2,1)} all-to-all(bf16[2,192,512]{2,1,0:T(8,128)(2,1)S(1)} %shard_map.143), channel_id=1, replica_groups=mesh['lat'=16,'obs'=2] {'obs'}, dimensions={0} | all-to-all | bytes 786432 | tf_op jit(solution)/shard_map/all_to_all | solution.py:413
  72.1 4.8 %all-to-all-start.2 = ((bf16[16,192,256]{2,1,0:T(8,128)(2,1)}), bf16[16,192,256]{2,1,0:T(8,128)(2,1)}, u32[]{:S(2)}, u32[]{:S(2)}) async-start(bf16[16,192,256]{2,1,0:T(8,128)(2,1)} %bitcast.25), calls=%async_computation.2 | async-start | bytes 3145728 | tf_op jit(solution)/shard_map/all_to_all | solution.py:380
  77.3 1.3 copy.43.weights
  79.5 1.2 copy-done
  80.7 20.6 %shard_map.140.matrix = bf16[2048,3072]{1,0:T(8,128)(2,1)} custom-call(s32[2048,4]{1,0:T(8,128)S(1)} %copy.42.places, f32[2048,4]{1,0:T(8,128)S(1)} %copy-done), custom_call_target="tpu_custom_call" | custom-call | flops 62914560 | bytes 12582912 | tf_op jit(solution)/shard_map/pallas_call | solution.py:251
  101.3 11.2 %shard_map.148.matrix = bf16[3072,2048]{1,0:T(8,128)(2,1)} custom-call(s32[4,2048]{1,0:T(4,128)S(1)} %fusion.7.places, f32[4,2048]{1,0:T(4,128)S(1)} %bitcast.73), custom_call_target="tpu_custom_call" | custom-call | flops 62914560 | bytes 12582912 | tf_op jit(solution)/shard_map/pallas_call | solution.py:278
  112.9 1.5 fusion.2.mapping
  114.6 2.9 reshape.98
  117.5 2.3 copy.45
  119.8 2.2 copy.46.field
  123.1 10.4 %shard_map.146 = bf16[2,192,512]{2,1,0:T(8,128)(2,1)S(1)} custom-call(bf16[16,192,256]{2,1,0:T(8,128)(2,1)} %all-to-all-done.2.lines, f32[128,1024]{1,0:T(8,128)S(1)} %copy-done.14), custom_call_target="tpu_custom_call" | custom-call | flops 1610612736 | bytes 1572864 | tf_op jit(solution)/shard_map/pallas_call | solution.py:190
  133.5 4.8 %all_to_all.41 = bf16[2,192,512]{2,1,0:T(8,128)(2,1)} all-to-all(bf16[2,192,512]{2,1,0:T(8,128)(2,1)S(1)} %shard_map.146), channel_id=1, replica_groups=mesh['lat'=16,'obs'=2] {'obs'}, dimensions={0} | all-to-all | bytes 786432 | tf_op jit(solution)/shard_map/all_to_all | solution.py:413
  138.3 2.9 reshape.104
  141.1 2.3 copy.50
  143.5 2.2 copy.51.field
  145.6 1.2 copy-done.1
  148.0 9.7 %shard_map.144 = (f32[2048,1]{1,0:T(8,128)S(1)}, bf16[2048,64]{1,0:T(8,128)(2,1)S(1)}) custom-call(bf16[2048,3072]{1,0:T(8,128)(2,1)} %shard_map.140.matrix, bf16[3072,64]{1,0:T(8,128)(2,1)S(1)} %copy-done.3, f32[2048,64]{1,0:T(8,128)S(1)} %copy-done.1, f32[2048,1]{1,0:T(8,128)S(1)} %copy.48.innovation, f32[2048,1]{1,0:T(8,128)S(1)} %copy.49.precision), custom_call_target="tpu_custom_call" | custom-call | flops 3221225472 | bytes 12582912 | tf_op jit(solution)/shard_map/pallas_call | solution.py:306
  158.7 7.0 %shard_map.149 = bf16[3072,64]{1,0:T(8,128)(2,1)S(1)} custom-call(bf16[3072,2048]{1,0:T(8,128)(2,1)} %shard_map.148.matrix, bf16[2048,64]{1,0:T(8,128)(2,1)S(1)} %get-tuple-element.8.pushes), custom_call_target="tpu_custom_call" | custom-call | flops 3221225472 | bytes 12582912 | tf_op jit(solution)/shard_map/pallas_call | solution.py:334
  166.6 2.1 copy.55
  168.7 2.4 copy.56
  171.1 3.4 %reshape.108 = bf16[2,192,512]{2,1,0:T(8,128)(2,1)} reshape(bf16[2,3072,32]{2,1,0:T(8,128)(2,1)} %copy.56) | data formatting | bytes 786432 | tf_op jit(solution)/shard_map/reshape | solution.py:420
  175.6 9.7 %shard_map.147 = (f32[2048,1]{1,0:T(8,128)S(1)}, bf16[2048,64]{1,0:T(8,128)(2,1)S(1)}) custom-call(bf16[2048,3072]{1,0:T(8,128)(2,1)} %shard_map.140.matrix, bf16[3072,64]{1,0:T(8,128)(2,1)S(1)} %copy-done.2, f32[2048,64]{1,0:T(8,128)S(1)} %fusion.mapping, f32[2048,1]{1,0:T(8,128)S(1)} %copy.48.innovation, f32[2048,1]{1,0:T(8,128)S(1)} %copy.49.precision), custom_call_target="tpu_custom_call" | custom-call | flops 3221225472 | bytes 12582912 | tf_op jit(solution)/shard_map/pallas_call | solution.py:306
  186.3 7.0 %shard_map.152 = bf16[3072,64]{1,0:T(8,128)(2,1)S(1)} custom-call(bf16[3072,2048]{1,0:T(8,128)(2,1)} %shard_map.148.matrix, bf16[2048,64]{1,0:T(8,128)(2,1)S(1)} %get-tuple-element.9.pushes), custom_call_target="tpu_custom_call" | custom-call | flops 3221225472 | bytes 12582912 | tf_op jit(solution)/shard_map/pallas_call | solution.py:334
  194.4 1.5 reshape.111
  195.9 4.0 %all_to_all.42.lifted = bf16[2,192,512]{2,1,0:T(8,128)(2,1)S(1)} all-to-all(bf16[2,192,512]{2,1,0:T(8,128)(2,1)S(1)} %reshape.111), channel_id=1, replica_groups=mesh['lat'=16,'obs'=2] {'obs'}, dimensions={0} | all-to-all | bytes 786432 | tf_op jit(solution)/shard_map/all_to_all | solution.py:419
  199.9 3.5 %all-to-all-start.4 = ((bf16[2,192,512]{2,1,0:T(8,128)(2,1)}), bf16[2,192,512]{2,1,0:T(8,128)(2,1)S(1)}, u32[]{:S(2)}, u32[]{:S(2)}) async-start(bf16[2,192,512]{2,1,0:T(8,128)(2,1)} %reshape.108), calls=%async_computation.4 | async-start | bytes 786432 | tf_op jit(solution)/shard_map/all_to_all | solution.py:419
  203.4 8.2 %shard_map.153 = bf16[16,192,256]{2,1,0:T(8,128)(2,1)} custom-call(bf16[2,192,512]{2,1,0:T(8,128)(2,1)S(1)} %all_to_all.42.lifted, f32[128,1024]{1,0:T(8,128)S(1)} %copy-done.15), custom_call_target="tpu_custom_call" | custom-call | flops 1610612736 | bytes 1572864 | tf_op jit(solution)/shard_map/pallas_call | solution.py:225
  211.6 6.9 %all-to-all-start.7 = ((bf16[16,192,256]{2,1,0:T(8,128)(2,1)}), bf16[16,192,256]{2,1,0:T(8,128)(2,1)S(1)}, u32[]{:S(2)}, u32[]{:S(2)}) async-start(bf16[16,192,256]{2,1,0:T(8,128)(2,1)} %shard_map.153), calls=%async_computation.7 | async-start | bytes 3145728 | tf_op jit(solution)/shard_map/all_to_all | solution.py:423
  218.5 8.2 %shard_map.150 = bf16[16,192,256]{2,1,0:T(8,128)(2,1)} custom-call(bf16[2,192,512]{2,1,0:T(8,128)(2,1)S(1)} %all-to-all-done.4.lifted, f32[128,1024]{1,0:T(8,128)S(1)} %copy-done.15), custom_call_target="tpu_custom_call" | custom-call | flops 1610612736 | bytes 1572864 | tf_op jit(solution)/shard_map/pallas_call | solution.py:225
  226.7 29.3 %all-to-all-done.7 = bf16[16,192,256]{2,1,0:T(8,128)(2,1)S(1)} async-done(((bf16[16,192,256]{2,1,0:T(8,128)(2,1)}), bf16[16,192,256]{2,1,0:T(8,128)(2,1)S(1)}, u32[]{:S(2)}, u32[]{:S(2)}) %all-to-all-start.7) | async-done | bytes 1572896 | tf_op jit(solution)/shard_map/all_to_all | solution.py:423
  257.2 5.2 %all-to-all-start.5 = ((bf16[16,192,256]{2,1,0:T(8,128)(2,1)}), bf16[16,192,256]{2,1,0:T(8,128)(2,1)}, u32[]{:S(2)}, u32[]{:S(2)}) async-start(bf16[16,192,256]{2,1,0:T(8,128)(2,1)} %shard_map.150), calls=%async_computation.5 | async-start | bytes 3145728 | tf_op jit(solution)/shard_map/all_to_all | solution.py:423
  262.4 3.6 %shard_map.151.tall = bf16[6144,256]{1,0:T(8,128)(2,1)S(1)} custom-call(f32[8]{0:T(128)S(1)} %pad_maximum_fusion.coef), custom_call_target="tpu_custom_call" | custom-call | flops 47185920 | bytes 3145728 | tf_op jit(solution)/shard_map/pallas_call | solution.py:75
  266.0 1.6 reduce
  267.6 1.6 reduce.1
  269.8 1.4 copy-done.7
  271.2 8.7 %shard_map.154.rest_0_ = f32[2,256,3072]{2,1,0:T(8,128)} custom-call(bf16[3072,256]{1,0:T(8,128)(2,1)S(1)} %bitcast.71, bf16[6144,256]{1,0:T(8,128)(2,1)S(1)} %shard_map.151.tall), custom_call_target="tpu_custom_call" | custom-call | flops 4831838208 | bytes 9437184 | tf_op jit(solution)/shard_map/pallas_call | solution.py:143
  279.9 19.5 %all-to-all-done.5 = bf16[16,192,256]{2,1,0:T(8,128)(2,1)} async-done(((bf16[16,192,256]{2,1,0:T(8,128)(2,1)}), bf16[16,192,256]{2,1,0:T(8,128)(2,1)}, u32[]{:S(2)}, u32[]{:S(2)}) %all-to-all-start.5) | async-done | bytes 1572896 | tf_op jit(solution)/shard_map/all_to_all | solution.py:423
  299.4 10.2 %shard_map.155 = f32[2,256,3072]{2,1,0:T(8,128)} custom-call(bf16[3072,256]{1,0:T(8,128)(2,1)} %bitcast.31.lines, bf16[6144,256]{1,0:T(8,128)(2,1)S(1)} %shard_map.151.tall, f32[2,256,3072]{2,1,0:T(8,128)} %shard_map.154.rest_0_), custom_call_target="tpu_custom_call", output_to_operand_aliasing={{}: (2, {})} | custom-call | flops 4831838208 | bytes 9437184 | tf_op jit(solution)/shard_map/pallas_call | solution.py:143
  (69 shorter events, 12.8 us)
Async XLA Ops:
  1.4 5.3 %copy-start.11 = (bf16[2,32,8,3072]{3,2,1,0:T(8,128)(2,1)S(1)}, bf16[2,32,8,3072]{3,2,1,0:T(8,128)(2,1)}, u32[]{:S(2)}) copy-start(bf16[2,32,8,3072]{3,2,1,0:T(8,128)(2,1)} %param.13) | copy-start | bytes 9437188
  5.0 1.7 copy-start.4
  17.1 7.3 %copy-start.22 = (s32[1,1,2,2]{3,2,1,0:T(2,128)S(1)}, s32[1,1,2,2]{3,2,1,0:T(2,128)}, u32[]{:S(2)}) copy-start(s32[1,1,2,2]{3,2,1,0:T(2,128)} %param.19) | copy-start | bytes 52
  17.1 9.5 %copy-start.23 = (f32[4]{0:T(128)S(1)}, f32[4]{0:T(128)}, u32[]{:S(2)}) copy-start(f32[4]{0:T(128)} %param.17) | copy-start | bytes 52
  17.1 9.5 %copy-start.24 = (f32[4]{0:T(128)S(1)}, f32[4]{0:T(128)}, u32[]{:S(2)}) copy-start(f32[4]{0:T(128)} %param.16) | copy-start | bytes 52
  17.1 44.5 %all-to-all-start = ((bf16[16,192,256]{2,1,0:T(8,128)(2,1)}), bf16[16,192,256]{2,1,0:T(8,128)(2,1)S(1)}, u32[]{:S(2)}, u32[]{:S(2)}) async-start(bf16[16,192,256]{2,1,0:T(8,128)(2,1)} %bitcast.8), calls=%async_computation | async-start | bytes 3145728 | tf_op jit(solution)/shard_map/all_to_all | solution.py:380
  32.7 1.9 copy-start.12
  34.6 27.0 %copy-start.13 = (f32[128,1024]{1,0:T(8,128)}, f32[128,1024]{1,0:T(8,128)S(1)}, u32[]{:S(2)}) copy-start(f32[128,1024]{1,0:T(8,128)S(1)} %fusion.4.spread) | copy-start | bytes 1572868
  72.1 4.8 %copy-start.21 = (s32[1,1,2048]{2,1,0:T(1,128)S(1)}, s32[1,1,2048]{2,1,0:T(1,128)}, u32[]{:S(2)}) copy-start(s32[1,1,2048]{2,1,0:T(1,128)} %param.20) | copy-start | bytes 24580
  72.1 4.8 %copy-start.16 = (s32[1,1,4,2048]{3,2,1,0:T(4,128)S(1)}, s32[1,1,4,2048]{3,2,1,0:T(4,128)}, u32[]{:S(2)}) copy-start(s32[1,1,4,2048]{3,2,1,0:T(4,128)} %param.22) | copy-start | bytes 98308
  72.1 5.3 %copy-start.10 = (f32[1,1,4,2048]{3,2,1,0:T(4,128)S(1)}, f32[1,1,4,2048]{3,2,1,0:T(4,128)}, u32[]{:S(2)}) copy-start(f32[1,1,4,2048]{3,2,1,0:T(4,128)} %param.23) | copy-start | bytes 98308
  72.1 49.9 %all-to-all-start.2 = ((bf16[16,192,256]{2,1,0:T(8,128)(2,1)}), bf16[16,192,256]{2,1,0:T(8,128)(2,1)}, u32[]{:S(2)}, u32[]{:S(2)}) async-start(bf16[16,192,256]{2,1,0:T(8,128)(2,1)} %bitcast.25), calls=%async_computation.2 | async-start | bytes 3145728 | tf_op jit(solution)/shard_map/all_to_all | solution.py:380
  76.8 1.9 copy-start.19
  77.0 2.1 copy-start.20
  79.4 1.2 copy-start
  101.3 11.2 %copy-start.17 = (s32[1,1,2048]{2,1,0:T(1,128)S(1)}, s32[1,1,2048]{2,1,0:T(1,128)}, u32[]{:S(2)}) copy-start(s32[1,1,2048]{2,1,0:T(1,128)} %param.21) | copy-start | bytes 24580
  101.3 11.5 %copy-start.18 = (bf16[2,64,64]{2,1,0:T(8,128)(2,1)S(1)}, bf16[2,64,64]{2,1,0:T(8,128)(2,1)}, u32[]{:S(2)}) copy-start(bf16[2,64,64]{2,1,0:T(8,128)(2,1)} %param.18) | copy-start | bytes 49156
  122.0 1.0 copy-start.14
  145.6 1.2 copy-start.1
  146.9 1.1 copy-start.3
  157.7 1.0 copy-start.8
  165.7 0.9 copy-start.5
  174.5 1.1 copy-start.2
  185.3 1.0 copy-start.9
  194.4 9.0 %copy-start.15 = (f32[128,1024]{1,0:T(8,128)S(1)}, f32[128,1024]{1,0:T(8,128)}, u32[]{:S(2)}) copy-start(f32[128,1024]{1,0:T(8,128)} %copy-done.13) | copy-start | bytes 1572868
  199.9 11.7 %all-to-all-start.4 = ((bf16[2,192,512]{2,1,0:T(8,128)(2,1)}), bf16[2,192,512]{2,1,0:T(8,128)(2,1)S(1)}, u32[]{:S(2)}, u32[]{:S(2)}) async-start(bf16[2,192,512]{2,1,0:T(8,128)(2,1)} %reshape.108), calls=%async_computation.4 | async-start | bytes 786432 | tf_op jit(solution)/shard_map/all_to_all | solution.py:419
  211.6 44.4 %all-to-all-start.7 = ((bf16[16,192,256]{2,1,0:T(8,128)(2,1)}), bf16[16,192,256]{2,1,0:T(8,128)(2,1)S(1)}, u32[]{:S(2)}, u32[]{:S(2)}) async-start(bf16[16,192,256]{2,1,0:T(8,128)(2,1)} %shard_map.153), calls=%async_computation.7 | async-start | bytes 3145728 | tf_op jit(solution)/shard_map/all_to_all | solution.py:423
  256.1 1.1 copy-start.6
  257.2 42.2 %all-to-all-start.5 = ((bf16[16,192,256]{2,1,0:T(8,128)(2,1)}), bf16[16,192,256]{2,1,0:T(8,128)(2,1)}, u32[]{:S(2)}, u32[]{:S(2)}) async-start(bf16[16,192,256]{2,1,0:T(8,128)(2,1)} %shard_map.150), calls=%async_computation.5 | async-start | bytes 3145728 | tf_op jit(solution)/shard_map/all_to_all | solution.py:423
  269.8 1.4 copy-start.7

commit v2 on v1

v2 whole, which is shorter than its diff:
```python
import functools
import math

import jax
import jax.numpy as jnp
from jax import lax
from jax.experimental import pallas as pl
from jax.experimental.pallas import tpu as pltpu
from jax.sharding import PartitionSpec as P

SLOTS = 2
BR = 4
TILE = 256
F32 = jnp.float32
BF16 = jnp.bfloat16


def coefficients(scales, heights):
    rate = -1.0 / (2.0 * scales * scales)
    gain = heights / jnp.sqrt(math.sqrt(math.pi) * scales)
    return jnp.concatenate([rate, gain]).astype(F32)


def gaussians(distance, coef):
    square = distance * distance
    total = coef[4] * jnp.exp(square * coef[0])
    for member in range(1, 4):
        total = total + coef[4 + member] * jnp.exp(square * coef[member])
    return total


def params(mib=48):
    return pltpu.CompilerParams(vmem_limit_bytes=mib * 1024 * 1024)


def cost(flops, nbytes):
    return pl.CostEstimate(flops=int(flops), bytes_accessed=int(nbytes), transcendentals=0)


def wide_table_kernel(width, coef, out):
    step = 512

    def piece(at, carry):
        start = pl.multiple_of(at * step, step)
        lane = lax.broadcasted_iota(jnp.int32, (TILE, step), 1) + start
        row = lax.broadcasted_iota(jnp.int32, (TILE, step), 0)
        offset = jnp.abs(lane - row)
        distance = jnp.minimum(offset, width - offset).astype(F32)
        value = gaussians(distance, coef).astype(BF16)
        out[:, pl.ds(start, step)] = value
        out[:, pl.ds(start + width, step)] = value
        return carry

    lax.fori_loop(0, width // step, piece, 0)


def tall_table_kernel(width, coef, out):
    step = 512

    def piece(at, carry):
        start = pl.multiple_of(at * step, step)
        row = lax.broadcasted_iota(jnp.int32, (step, TILE), 0) + start
        lane = lax.broadcasted_iota(jnp.int32, (step, TILE), 1)
        offset = jnp.abs(lane - row)
        distance = jnp.minimum(offset, width - offset).astype(F32)
        value = gaussians(distance, coef).astype(BF16)
        out[pl.ds(start, step), :] = value
        out[pl.ds(start + width, step), :] = value
        return carry

    lax.fori_loop(0, width // step, piece, 0)


def table(kernel, shape, width, coef):
    return pl.pallas_call(
        functools.partial(kernel, width),
        out_shape=jax.ShapeDtypeStruct(shape, BF16),
        in_specs=[pl.BlockSpec(memory_space=pltpu.SMEM)],
        out_specs=pl.BlockSpec(memory_space=pltpu.VMEM),
        compiler_params=params(),
        cost_estimate=cost(shape[0] * shape[1] * 30, shape[0] * shape[1] * 2),
    )(coef)


def zonal_forward_kernel(width, control, wide, out, turned):
    at = pl.program_id(0)

    @pl.when(at == 0)
    def _():
        for part in range(width // TILE):
            cells = slice(part * TILE, (part + 1) * TILE)
            turned[cells, :] = control[0, :, cells].T

    start = pl.multiple_of(width - at * TILE, TILE)
    out[...] = jnp.dot(
        wide[:, pl.ds(start, width)], turned[...], preferred_element_type=F32
    ).astype(BF16)


def zonal_forward(control, wide, variable):
    _, rows, width = control.shape
    return pl.pallas_call(
        functools.partial(zonal_forward_kernel, width),
        out_shape=jax.ShapeDtypeStruct((width, rows), BF16),
        grid=(width // TILE,),
        in_specs=[
            pl.BlockSpec((1, rows, width), lambda at: (variable, 0, 0)),
            pl.BlockSpec((TILE, 2 * width), lambda at: (0, 0)),
        ],
        out_specs=pl.BlockSpec((TILE, rows), lambda at: (at, 0)),
        scratch_shapes=[pltpu.VMEM((width, rows), BF16)],
        compiler_params=params(),
        cost_estimate=cost(2 * rows * width * width, 10 * rows * width),
    )(control, wide)


def zonal_backward_kernel(width, lines, tall, *rest):
    out, turned = rest[-2:]
    at = pl.program_id(0)

    @pl.when(at == 0)
    def _():
        for part in range(width // TILE):
            cells = slice(part * TILE, (part + 1) * TILE)
            turned[:, cells] = lines[cells, :].T

    start = pl.multiple_of(width - at * TILE, TILE)
    out[0] = jnp.dot(turned[...], tall[pl.ds(start, width), :], preferred_element_type=F32)


def zonal_backward(lines, tall, variables, variable, gradient):
    width, rows = lines.shape
    operands = [lines, tall]
    in_specs = [
        pl.BlockSpec((width, rows), lambda at: (0, 0)),
        pl.BlockSpec((2 * width, TILE), lambda at: (0, 0)),
    ]
    aliases = {}
    if gradient is not None:
        operands.append(gradient)
        in_specs.append(pl.BlockSpec(memory_space=pl.ANY))
        aliases = {2: 0}
    return pl.pallas_call(
        functools.partial(zonal_backward_kernel, width),
        out_shape=jax.ShapeDtypeStruct((variables, rows, width), F32),
        grid=(width // TILE,),
        in_specs=in_specs,
        out_specs=pl.BlockSpec((1, rows, TILE), lambda at: (variable, 0, at)),
        scratch_shapes=[pltpu.VMEM((rows, width), BF16)],
        input_output_aliases=aliases,
        compiler_params=params(),
        cost_estimate=cost(2 * rows * width * width, 12 * rows * width),
    )(*operands)


def band_kernel(levels, spread, out):
    rows, columns = spread.shape
    full = jnp.broadcast_to(spread[...][None], (levels, rows, columns))
    level = lax.broadcasted_iota(jnp.int32, full.shape, 0)
    lane = lax.broadcasted_iota(jnp.int32, (1, 1, columns), 2) % levels
    full = jnp.where(lane == level, full, 0.0)
    out[0] = full.reshape(levels * rows, columns).astype(BF16)


def band_matrices(spread, levels, bands):
    all_rows, columns = spread.shape
    band_rows = all_rows // bands
    rows = levels * band_rows
    return pl.pallas_call(
        functools.partial(band_kernel, levels),
        out_shape=jax.ShapeDtypeStruct((bands, rows, columns), BF16),
        grid=(bands,),
        in_specs=[pl.BlockSpec((band_rows, columns), lambda at: (at, 0))],
        out_specs=pl.BlockSpec((1, rows, columns), lambda at: (at, 0, 0)),
        compiler_params=params(),
        cost_estimate=cost(10 * bands * rows * columns, 2 * bands * rows * columns),
    )(spread)


def meridional_forward_kernel(lines, matrix, out, total):
    at = pl.program_id(0)
    product = jnp.dot(lines[0], matrix[0], preferred_element_type=F32)

    @pl.when(at == 0)
    def _():
        total[...] = product

    @pl.when(at > 0)
    def _():
        total[...] += product

    @pl.when(at == pl.num_programs(0) - 1)
    def _():
        owners, _, share = out.shape
        for owner in range(owners):
            out[owner] = total[:, owner * share : (owner + 1) * share].astype(BF16)


def meridional_forward(lines, matrices, owners):
    bands, strip, rows = lines.shape
    columns = matrices.shape[2]
    return pl.pallas_call(
        meridional_forward_kernel,
        out_shape=jax.ShapeDtypeStruct((owners, strip, columns // owners), BF16),
        grid=(bands,),
        in_specs=[
            pl.BlockSpec((1, strip, rows), lambda at: (at, 0, 0)),
            pl.BlockSpec((1, rows, columns), lambda at: (at, 0, 0)),
        ],
        out_specs=pl.BlockSpec((owners, strip, columns // owners), lambda at: (0, 0, 0)),
        scratch_shapes=[pltpu.VMEM((strip, columns), F32)],
        compiler_params=params(),
        cost_estimate=cost(2 * bands * strip * rows * columns, 2 * bands * strip * rows),
    )(lines, matrices)


def meridional_backward_kernel(own, other, matrix, out):
    share = own.shape[1]
    transposed = (((1,), (1,)), ((), ()))
    total = lax.dot_general(
        own[...], matrix[0, :, :share], transposed, preferred_element_type=F32
    ) + lax.dot_general(other[...], matrix[0, :, share:], transposed, preferred_element_type=F32)
    out[0] = total.astype(BF16)


def meridional_backward(own, other, matrices):
    bands, rows, columns = matrices.shape
    strip, share = own.shape
    half = pl.BlockSpec((strip, share), lambda at: (0, 0))
    return pl.pallas_call(
        meridional_backward_kernel,
        out_shape=jax.ShapeDtypeStruct((bands, strip, rows), BF16),
        grid=(bands,),
        in_specs=[half, half, pl.BlockSpec((1, rows, columns), lambda at: (at, 0, 0))],
        out_specs=pl.BlockSpec((1, strip, rows), lambda at: (at, 0, 0)),
        compiler_params=params(),
        cost_estimate=cost(2 * bands * strip * rows * columns, 2 * bands * strip * rows),
    )(own, other, matrices)


def reports_kernel(variable, share, own, other, ids, numbers, cells, weights, maps, departure, lifted, total):
    at = pl.program_id(0)
    strip, columns = own.shape
    block = ids.shape[0]
    levels = maps.shape[2]
    across = lax.broadcasted_iota(jnp.int32, (block, strip), 1)
    cell = ids[:, 0:1]
    down = lax.broadcasted_iota(jnp.int32, (strip, block), 0)
    place = cells[...]
    sides = []
    turned = []
    for side in range(2):
        value = jnp.where(across == cell, numbers[:, 2 * side : 2 * side + 1], 0.0)
        value = jnp.where(across == cell + 1, numbers[:, 2 * side + 1 : 2 * side + 2], value)
        sides.append(value.astype(BF16))
        value = jnp.where(down == place, weights[2 * side : 2 * side + 1, :], 0.0)
        value = jnp.where(down == place + 1, weights[2 * side + 1 : 2 * side + 2, :], value)
        turned.append(value.astype(BF16))
    level = ids[:, 2:3] - variable * levels
    chosen = jnp.where(lax.broadcasted_iota(jnp.int32, (block, levels), 1) == level, 1.0, 0.0)
    chosen = chosen.astype(BF16)
    lane = lax.broadcasted_iota(jnp.int32, (block, columns), 1) // share
    hits = [lane == ids[:, 1:2], lane == ids[:, 1:2] + 1]
    fields = (own, other)
    model = jnp.zeros((block, 1), F32)
    kept = []
    for half in range(2):
        mapped = jnp.dot(chosen, maps[0, half], preferred_element_type=F32)
        found = jnp.zeros((block, columns), F32)
        for side in range(2):
            picked = jnp.where(hits[side], mapped, 0.0)
            kept.append(picked)
            values = jnp.dot(sides[side], fields[half][...], preferred_element_type=F32)
            found = found + values * picked
        model = model + jnp.sum(found, axis=1, keepdims=True)
    result = numbers[:, 5:6] * (model - numbers[:, 4:5])
    departure[...] = jnp.broadcast_to(result, (block, 128)).T[0:1, :]
    for half in range(2):
        product = jnp.zeros((strip, columns), F32)
        for side in range(2):
            pushes = (kept[2 * half + side] * result).astype(BF16)
            product = product + jnp.dot(turned[side], pushes, preferred_element_type=F32)

        @pl.when(at == 0)
        def _():
            total[half] = product

        @pl.when(at > 0)
        def _():
            total[half] += product

    @pl.when(at == pl.num_programs(0) - 1)
    def _():
        lifted[...] = total[...].astype(BF16)


def at_reports(variable, share, own, other, ids, numbers, cells, weights, maps):
    strip, columns = own.shape
    reports = ids.shape[0]
    block = math.gcd(reports, 256)
    half = pl.BlockSpec((strip, columns), lambda at: (0, 0))
    return pl.pallas_call(
        functools.partial(reports_kernel, variable, share),
        out_shape=(
            jax.ShapeDtypeStruct((1, reports), F32),
            jax.ShapeDtypeStruct((2, strip, columns), BF16),
        ),
        grid=(reports // block,),
        in_specs=[
            half,
            half,
            pl.BlockSpec((block, ids.shape[1]), lambda at: (at, 0)),
            pl.BlockSpec((block, numbers.shape[1]), lambda at: (at, 0)),
            pl.BlockSpec((1, block), lambda at: (0, at)),
            pl.BlockSpec((4, block), lambda at: (0, at)),
            pl.BlockSpec((1,) + maps.shape[1:], lambda at: (variable, 0, 0, 0)),
        ],
        out_specs=(
            pl.BlockSpec((1, block), lambda at: (0, at)),
            pl.BlockSpec((2, strip, columns), lambda at: (0, 0, 0)),
        ),
        scratch_shapes=[pltpu.VMEM((2, strip, columns), F32)],
        compiler_params=params(),
        cost_estimate=cost(16 * reports * 256 * columns, 4 * reports * 128),
    )(own, other, ids, numbers, cells, weights, maps)


def on_device(
    control,
    zonal_scales,
    zonal_heights,
    meridional_scales,
    meridional_heights,
    vertical_map,
    send_blocks,
    report_slot,
    report_level,
    report_corner,
    report_weight,
    innovation,
    report_precision,
):
    lat_count = lax.axis_size("lat")
    owners = lax.axis_size("obs")
    variables, share, band_rows, width = control.shape
    strip = width // lat_count
    all_rows = band_rows * lat_count
    levels = share * owners
    slots = owners * SLOTS
    kept = slots * BR
    points = strip * kept
    reports = report_slot.shape[-1]

    zonal = coefficients(zonal_scales, zonal_heights)
    wide = table(wide_table_kernel, (TILE, 2 * width), width, zonal)
    fields = control.reshape(variables, share * band_rows, width)
    sent = []
    for variable in range(variables):
        smooth = zonal_forward(fields, wide, variable).reshape(lat_count, strip, -1)
        sent.append(lax.all_to_all(smooth, "lat", split_axis=0, concat_axis=0, tiled=True))

    tall = table(tall_table_kernel, (2 * width, TILE), width, zonal)

    me = lax.axis_index("obs")
    partner = [(0, 1), (1, 0)]
    blocks = lax.all_gather(send_blocks.reshape(owners, SLOTS), "obs", axis=0)
    source = jnp.arange(owners)[:, None, None]
    starts = jnp.transpose(source * (all_rows // owners) + blocks * BR, (1, 0, 2))
    starts = jnp.where(me == 0, starts, starts[::-1])
    rows = starts[..., None] + jnp.arange(BR)
    lanes = jnp.repeat(rows.reshape(-1), share)
    apart = jnp.abs(jnp.arange(all_rows)[:, None] - lanes[None, :]).astype(F32)
    meridional = coefficients(meridional_scales, meridional_heights)
    spread = gaussians(apart, meridional).astype(BF16).astype(F32)
    matrices = band_matrices(spread, share, lat_count)

    slot = report_slot.reshape(1, reports)
    code = report_level.reshape(1, reports)
    first = report_corner.reshape(4, reports)[0:1]
    weight = report_weight.reshape(4, reports)
    cells = first % strip
    ids = jnp.concatenate([cells, slot * BR + first // strip, code], axis=0).T
    numbers = jnp.concatenate(
        [weight, innovation.reshape(1, reports), report_precision.reshape(1, reports)], axis=0
    ).T
    maps = vertical_map.reshape(variables, levels, owners, share).transpose(0, 2, 1, 3)
    maps = jnp.where(me == 0, maps, maps[:, ::-1])
    maps = jnp.tile(maps, (1, 1, 1, kept))

    departures = []
    lines = []
    for variable in range(variables):
        mixed = meridional_forward(sent[variable], matrices, owners)
        theirs = lax.ppermute(mixed[1], "obs", partner)
        departure, lifted = at_reports(
            variable, share, mixed[0], theirs, ids, numbers, cells, weight, maps
        )
        departures.append(departure)
        theirs = lax.ppermute(lifted[1], "obs", partner)
        back = meridional_backward(lifted[0], theirs, matrices)
        lines.append(lax.all_to_all(back, "lat", split_axis=0, concat_axis=0, tiled=True))

    gradient = None
    for variable in range(variables):
        gradient = zonal_backward(
            lines[variable].reshape(width, -1), tall, variables, variable, gradient
        )
    departure = departures[0]
    for variable in range(1, variables):
        departure = jnp.where(code >= variable * levels, departures[variable], departure)
    return (departure.reshape(report_slot.shape), gradient.reshape(control.shape))


def solution(mesh):
    in_specs = (
        P(None, "obs", "lat", None),
        P(),
        P(),
        P(),
        P(),
        P(),
        P("lat", "obs", None, None),
        P("lat", "obs", None),
        P("lat", "obs", None),
        P("lat", "obs", None, None),
        P("lat", "obs", None, None),
        P("lat", "obs", None),
        P("lat", "obs", None),
    )
    out_specs = (P("lat", "obs", None), P(None, "obs", "lat", None))
    return jax.shard_map(
        on_device, mesh=mesh, in_specs=in_specs, out_specs=out_specs, check_vma=False
    )
```

time: 312 us -> 232 us (0.74)
  local copies, waits for them, and re-layouts: 43.4 us -> 13.8 us
  Pallas kernels: 145 us -> 129 us
  waiting for transfers between devices: 65.2 us -> 50.5 us
  blocking collectives: 15.4 us -> 1.79 us
    all_to_all x2, waiting for transfers between devices: 48.8 us -> 24.4 us  [on_device(): lax.all_to_all(back, 'lat', split_axis=0, concat_axis=0, tiled=True)]
    reshape x8 -> x0, local copies, waits for them, and re-layouts: 15.7 us -> none  [the longest x4 10.1 us: on_device(): taken.reshape(owners, points, share).transpose(1, 0, 2)]
    pallas_call x10 -> x7, Pallas kernels: 97.5 us -> 82.4 us  [the longest x2 25.8 us: at_reports(): pl.pallas_call(functools.partial(reports_kernel, variable, share), out_sh...]
    all_to_all x3 -> x0, blocking collectives: 13.6 us -> none  [the longest x2 9.58 us: on_device(): lax.all_to_all(mixed, 'obs', split_axis=0, concat_axis=0, tiled=True)]
    unnamed x50 -> x39, local copies, waits for them, and re-layouts: 14.8 us -> 7.21 us
    transpose x7 -> x2, local copies, waits for them, and re-layouts: 9.55 us -> 2.72 us  [the longest x1 1.37 us: on_device(): numbers = jnp.concatenate([weight, innovation.reshape(1, reports), report...]
    all_to_all x2, waiting for transfers between devices: 16.4 us -> 22.3 us  [on_device(): lax.all_to_all(smooth, 'lat', split_axis=0, concat_axis=0, tiled=True)]
    ppermute x0 -> x4, waiting for transfers between devices: none -> 3.8 us  [the longest x2 2.37 us: on_device(): theirs = lax.ppermute(lifted[1], 'obs', partner)]
  transfers between devices with their start and end apart: 5 -> 8, of which waited for: 3 -> 5; matrix products, arithmetic and copies ran while one was open for 7% -> 6% of each run, Pallas kernels for 23% -> 45%
where the time goes in v2:
time: 232 us; the launch traced here: 230 us
  Pallas kernels  129 us (56%)
  waiting for transfers between devices  50.5 us (22%)
  starting transfers between devices  26.8 us (12%)
  local copies, waits for them, and re-layouts  13.8 us (6%)
  other arithmetic  7.88 us (3%)
    pallas_call x2, Pallas kernels, at_reports(): pl.pallas_call(functools.partial(reports_kernel, variable, share), out_sh...  25.8 us
    pallas_call x2, Pallas kernels, meridional_backward(): pl.pallas_call(meridional_backward_kernel, out_shape=jax.ShapeDtypeStruct...  25.5 us
    all_to_all x2, waiting for transfers between devices, on_device(): lax.all_to_all(back, 'lat', split_axis=0, concat_axis=0, tiled=True)  24.4 us
    pallas_call x2, Pallas kernels, meridional_forward(): pl.pallas_call(meridional_forward_kernel, out_shape=jax.ShapeDtypeStruct(...  23.7 us
    all_to_all x2, waiting for transfers between devices, on_device(): lax.all_to_all(smooth, 'lat', split_axis=0, concat_axis=0, tiled=True)  22.3 us
    pallas_call x2, Pallas kernels, zonal_forward(): pl.pallas_call(functools.partial(zonal_forward_kernel, width), out_shape=...  20 us
    pallas_call x2, Pallas kernels, zonal_backward(): pl.pallas_call(functools.partial(zonal_backward_kernel, width), out_shape...  18.9 us
    all_to_all x2, starting transfers between devices, on_device(): lax.all_to_all(back, 'lat', split_axis=0, concat_axis=0, tiled=True)  13.8 us
  transfers between devices with their start and end apart: 8, of which 5 were waited for; matrix products, arithmetic and copies ran while one was open for 6% of the time, Pallas kernels for 45%

profile of v2, /device:TPU:12, one launch (start us, length us, event | category | flops | bytes accessed | tf_op | source)
XLA Modules:
  0.0 230.2 jit_solution(7638867859551859404)
XLA Ops:
  0.6 0.7 fusion.4
  1.3 0.1 pad_maximum_fusion.coef
  1.4 3.6 %shard_map.140.wide = bf16[256,6144]{1,0:T(8,128)(2,1)S(1)} custom-call(f32[8]{0:T(128)S(1)} %pad_maximum_fusion.coef), custom_call_target="tpu_custom_call" | custom-call | flops 47185920 | bytes 3145728 | tf_op jit(solution)/shard_map/pallas_call | solution.py:75
  5.0 1.7 copy-done
  6.7 10.5 %shard_map.145 = bf16[3072,256]{1,0:T(8,128)(2,1)} custom-call(bf16[2,256,3072]{2,1,0:T(8,128)(2,1)S(1)} %bitcast.77, bf16[256,6144]{1,0:T(8,128)(2,1)} %copy-done), custom_call_target="tpu_custom_call" | custom-call | flops 4831838208 | bytes 7864320 | tf_op jit(solution)/shard_map/pallas_call | solution.py:102
  17.1 7.3 %all-to-all-start.1 = ((bf16[16,192,256]{2,1,0:T(8,128)(2,1)}), bf16[16,192,256]{2,1,0:T(8,128)(2,1)S(1)}, u32[]{:S(2)}, u32[]{:S(2)}) async-start(bf16[16,192,256]{2,1,0:T(8,128)(2,1)} %bitcast.28), calls=%async_computation.1 | async-start | bytes 3145728 | tf_op jit(solution)/shard_map/all_to_all | solution.py:360
  24.4 1.8 all-gather
  26.2 0.1 fusion.3
  26.3 0.1 broadcast_select_fusion
  26.4 0.1 iota_add_fusion
  26.5 0.1 add.73
  26.6 0.1 broadcast_in_dim.2
  26.6 0.1 sub.22
  26.7 1.9 copy-done.10
  28.6 9.5 %shard_map.141 = bf16[3072,256]{1,0:T(8,128)(2,1)S(1)} custom-call(bf16[2,256,3072]{2,1,0:T(8,128)(2,1)S(1)} %bitcast.78, bf16[256,6144]{1,0:T(8,128)(2,1)} %copy-done), custom_call_target="tpu_custom_call" | custom-call | flops 4831838208 | bytes 7864320 | tf_op jit(solution)/shard_map/pallas_call | solution.py:102
  38.2 1.1 copy-done.1
  39.3 22.3 %all-to-all-done.1.lines = bf16[16,192,256]{2,1,0:T(8,128)(2,1)S(1)} async-done(((bf16[16,192,256]{2,1,0:T(8,128)(2,1)}), bf16[16,192,256]{2,1,0:T(8,128)(2,1)S(1)}, u32[]{:S(2)}, u32[]{:S(2)}) %all-to-all-start.1) | async-done | bytes 1572896 | tf_op jit(solution)/shard_map/all_to_all | solution.py:360
  61.6 4.8 %all-to-all-start = ((bf16[16,192,256]{2,1,0:T(8,128)(2,1)}), bf16[16,192,256]{2,1,0:T(8,128)(2,1)S(1)}, u32[]{:S(2)}, u32[]{:S(2)}) async-start(bf16[16,192,256]{2,1,0:T(8,128)(2,1)} %bitcast.72), calls=%async_computation | async-start | bytes 3145728 | tf_op jit(solution)/shard_map/all_to_all | solution.py:360
  66.5 0.8 and_select_fusion
  67.3 1.4 copy.32.ids
  68.7 1.4 copy.33.numbers
  70.1 0.1 copy.31
  70.2 0.7 fusion.6
  70.9 5.4 %fusion.spread = f32[128,1024]{1,0:T(8,128)S(1)} fusion(f32[]{:T(128)} %bitcast.12, f32[]{:T(128)} %bitcast.11, f32[]{:T(128)} %bitcast.10, f32[]{:T(128)} %bitcast.9, f32[]{:T(128)} %bitcast.8, f32[]{:T(128)} %bitcast.7, f32[]{:T(128)} %bitcast.6, s32[1024]{0:T(1024)S(1)} %sub.22, f32[]{:T(128)} %bitcast.3), kind=kLoop, calls=%fused_computation.1 | loop fusion | flops 2228224 | bytes 528416 | tf_op jit(solution)/shard_map/convert_element_type | solution.py:374
  76.3 7.4 %shard_map.142.matrix = bf16[16,256,1024]{2,1,0:T(8,128)(2,1)} custom-call(f32[128,1024]{1,0:T(8,128)S(1)} %fusion.spread), custom_call_target="tpu_custom_call" | custom-call | flops 41943040 | bytes 8388608 | tf_op jit(solution)/shard_map/pallas_call | solution.py:169
  83.7 11.8 %shard_map.146 = bf16[2,192,512]{2,1,0:T(8,128)(2,1)S(1)} custom-call(bf16[16,192,256]{2,1,0:T(8,128)(2,1)S(1)} %all-to-all-done.1.lines, bf16[16,256,1024]{2,1,0:T(8,128)(2,1)} %shard_map.142.matrix), custom_call_target="tpu_custom_call" | custom-call | flops 1610612736 | bytes 1572864 | tf_op jit(solution)/shard_map/pallas_call | solution.py:202
  95.5 0.7 slice_bitcast_fusion
  96.2 0.9 tile.4
  97.1 1.2 copy.34.maps
  98.4 1.2 copy-done.6
  99.6 12.9 %shard_map.147 = (f32[1,2048]{1,0:T(1,128)S(1)}, bf16[2,192,512]{2,1,0:T(8,128)(2,1)S(1)}) custom-call(bf16[192,512]{1,0:T(8,128)(2,1)S(1)} %get-tuple-element.15.own, bf16[192,512]{1,0:T(8,128)(2,1)S(1)} %collective-permute-done.1.other, s32[2048,3]{1,0:T(8,128)S(1)} %copy-done.4, f32[2048,6]{1,0:T(8,128)S(1)} %copy-done.6, ...), custom_call_target="tpu_custom_call" | custom-call | flops 4294967296 | bytes 1048576 | tf_op jit(solution)/shard_map/pallas_call | solution.py:302
  112.6 0.6 collective-permute-start.3
  113.1 1.1 collective-permute-done.3.other
  114.2 12.8 %shard_map.150 = bf16[16,192,256]{2,1,0:T(8,128)(2,1)} custom-call(bf16[192,512]{1,0:T(8,128)(2,1)S(1)} %get-tuple-element.11.own, bf16[192,512]{1,0:T(8,128)(2,1)S(1)} %collective-permute-done.3.other, bf16[16,256,1024]{2,1,0:T(8,128)(2,1)} %shard_map.142.matrix), custom_call_target="tpu_custom_call" | custom-call | flops 1610612736 | bytes 1572864 | tf_op jit(solution)/shard_map/pallas_call | solution.py:230
  127.0 6.9 %all-to-all-start.3 = ((bf16[16,192,256]{2,1,0:T(8,128)(2,1)}), bf16[16,192,256]{2,1,0:T(8,128)(2,1)S(1)}, u32[]{:S(2)}, u32[]{:S(2)}) async-start(bf16[16,192,256]{2,1,0:T(8,128)(2,1)} %shard_map.150), calls=%async_computation.3 | async-start | bytes 3145728 | tf_op jit(solution)/shard_map/all_to_all | solution.py:401
  133.9 11.9 %shard_map.143 = bf16[2,192,512]{2,1,0:T(8,128)(2,1)S(1)} custom-call(bf16[16,192,256]{2,1,0:T(8,128)(2,1)S(1)} %all-to-all-done.lines, bf16[16,256,1024]{2,1,0:T(8,128)(2,1)} %shard_map.142.matrix), custom_call_target="tpu_custom_call" | custom-call | flops 1610612736 | bytes 1572864 | tf_op jit(solution)/shard_map/pallas_call | solution.py:202
  145.9 1.4 collective-permute-done.other
  147.4 12.9 %shard_map.144 = (f32[1,2048]{1,0:T(1,128)S(1)}, bf16[2,192,512]{2,1,0:T(8,128)(2,1)S(1)}) custom-call(bf16[192,512]{1,0:T(8,128)(2,1)S(1)} %get-tuple-element.17.own, bf16[192,512]{1,0:T(8,128)(2,1)S(1)} %collective-permute-done.other, s32[2048,3]{1,0:T(8,128)S(1)} %copy-done.5, f32[2048,6]{1,0:T(8,128)S(1)} %copy-done.7, ...), custom_call_target="tpu_custom_call" | custom-call | flops 4294967296 | bytes 1048576 | tf_op jit(solution)/shard_map/pallas_call | solution.py:302
  160.3 0.2 collective-permute-start.2
  160.5 1.3 collective-permute-done.2.other
  161.8 12.7 %shard_map.148 = bf16[16,192,256]{2,1,0:T(8,128)(2,1)} custom-call(bf16[192,512]{1,0:T(8,128)(2,1)S(1)} %get-tuple-element.13.own, bf16[192,512]{1,0:T(8,128)(2,1)S(1)} %collective-permute-done.2.other, bf16[16,256,1024]{2,1,0:T(8,128)(2,1)} %shard_map.142.matrix), custom_call_target="tpu_custom_call" | custom-call | flops 1610612736 | bytes 1572864 | tf_op jit(solution)/shard_map/pallas_call | solution.py:230
  174.6 1.1 copy-done.2
  175.7 6.9 %all-to-all-start.2 = ((bf16[16,192,256]{2,1,0:T(8,128)(2,1)}), bf16[16,192,256]{2,1,0:T(8,128)(2,1)}, u32[]{:S(2)}, u32[]{:S(2)}) async-start(bf16[16,192,256]{2,1,0:T(8,128)(2,1)} %shard_map.148), calls=%async_computation.2 | async-start | bytes 3145728 | tf_op jit(solution)/shard_map/all_to_all | solution.py:401
  182.6 3.6 %shard_map.149.tall = bf16[6144,256]{1,0:T(8,128)(2,1)S(1)} custom-call(f32[8]{0:T(128)S(1)} %pad_maximum_fusion.coef), custom_call_target="tpu_custom_call" | custom-call | flops 47185920 | bytes 3145728 | tf_op jit(solution)/shard_map/pallas_call | solution.py:75
  186.3 0.6 fusion.2
  186.9 8.7 %shard_map.151.rest_0_ = f32[2,256,3072]{2,1,0:T(8,128)} custom-call(bf16[3072,256]{1,0:T(8,128)(2,1)S(1)} %bitcast.73, bf16[6144,256]{1,0:T(8,128)(2,1)S(1)} %shard_map.149.tall), custom_call_target="tpu_custom_call" | custom-call | flops 4831838208 | bytes 9437184 | tf_op jit(solution)/shard_map/pallas_call | solution.py:143
  195.7 24.4 %all-to-all-done.2 = bf16[16,192,256]{2,1,0:T(8,128)(2,1)} async-done(((bf16[16,192,256]{2,1,0:T(8,128)(2,1)}), bf16[16,192,256]{2,1,0:T(8,128)(2,1)}, u32[]{:S(2)}, u32[]{:S(2)}) %all-to-all-start.2) | async-done | bytes 1572896 | tf_op jit(solution)/shard_map/all_to_all | solution.py:401
  220.1 10.2 %shard_map.152 = f32[2,256,3072]{2,1,0:T(8,128)} custom-call(bf16[3072,256]{1,0:T(8,128)(2,1)} %bitcast.34.lines, bf16[6144,256]{1,0:T(8,128)(2,1)S(1)} %shard_map.149.tall, f32[2,256,3072]{2,1,0:T(8,128)} %shard_map.151.rest_0_), custom_call_target="tpu_custom_call", output_to_operand_aliasing={{}: (2, {})} | custom-call | flops 4831838208 | bytes 9437184 | tf_op jit(solution)/shard_map/pallas_call | solution.py:143
  (48 shorter events, 0.4 us)
Async XLA Ops:
  1.4 5.3 %copy-start.9 = (bf16[2,32,8,3072]{3,2,1,0:T(8,128)(2,1)S(1)}, bf16[2,32,8,3072]{3,2,1,0:T(8,128)(2,1)}, u32[]{:S(2)}) copy-start(bf16[2,32,8,3072]{3,2,1,0:T(8,128)(2,1)} %param.13) | copy-start | bytes 9437188
  5.0 1.7 copy-start
  17.1 7.3 %copy-start.16 = (s32[1,1,2,2]{3,2,1,0:T(2,128)S(1)}, s32[1,1,2,2]{3,2,1,0:T(2,128)}, u32[]{:S(2)}) copy-start(s32[1,1,2,2]{3,2,1,0:T(2,128)} %param.19) | copy-start | bytes 52
  17.1 44.5 %all-to-all-start.1 = ((bf16[16,192,256]{2,1,0:T(8,128)(2,1)}), bf16[16,192,256]{2,1,0:T(8,128)(2,1)S(1)}, u32[]{:S(2)}, u32[]{:S(2)}) async-start(bf16[16,192,256]{2,1,0:T(8,128)(2,1)} %bitcast.28), calls=%async_computation.1 | async-start | bytes 3145728 | tf_op jit(solution)/shard_map/all_to_all | solution.py:360
  26.7 1.9 copy-start.10
  38.2 1.1 copy-start.1
  61.6 4.8 %copy-start.15 = (s32[1,1,2048]{2,1,0:T(1,128)S(1)}, s32[1,1,2048]{2,1,0:T(1,128)}, u32[]{:S(2)}) copy-start(s32[1,1,2048]{2,1,0:T(1,128)} %param.20) | copy-start | bytes 24580
  61.6 5.7 %copy-start.12 = (s32[1,1,2048]{2,1,0:T(1,128)S(1)}, s32[1,1,2048]{2,1,0:T(1,128)}, u32[]{:S(2)}) copy-start(s32[1,1,2048]{2,1,0:T(1,128)} %param.21) | copy-start | bytes 24580
  61.6 7.1 %copy-start.8 = (f32[1,1,4,2048]{3,2,1,0:T(4,128)S(1)}, f32[1,1,4,2048]{3,2,1,0:T(4,128)}, u32[]{:S(2)}) copy-start(f32[1,1,4,2048]{3,2,1,0:T(4,128)} %param.23) | copy-start | bytes 98308
  61.6 7.1 %copy-start.13 = (f32[1,1,2048]{2,1,0:T(1,128)S(1)}, f32[1,1,2048]{2,1,0:T(1,128)}, u32[]{:S(2)}) copy-start(f32[1,1,2048]{2,1,0:T(1,128)} %param.25) | copy-start | bytes 24580
  61.6 7.1 %copy-start.14 = (f32[1,1,2048]{2,1,0:T(1,128)S(1)}, f32[1,1,2048]{2,1,0:T(1,128)}, u32[]{:S(2)}) copy-start(f32[1,1,2048]{2,1,0:T(1,128)} %param.24) | copy-start | bytes 24580
  61.6 65.3 %all-to-all-start = ((bf16[16,192,256]{2,1,0:T(8,128)(2,1)}), bf16[16,192,256]{2,1,0:T(8,128)(2,1)S(1)}, u32[]{:S(2)}, u32[]{:S(2)}) async-start(bf16[16,192,256]{2,1,0:T(8,128)(2,1)} %bitcast.72), calls=%async_computation | async-start | bytes 3145728 | tf_op jit(solution)/shard_map/all_to_all | solution.py:360
  66.4 3.7 %copy-start.11 = (bf16[2,64,64]{2,1,0:T(8,128)(2,1)S(1)}, bf16[2,64,64]{2,1,0:T(8,128)(2,1)}, u32[]{:S(2)}) copy-start(bf16[2,64,64]{2,1,0:T(8,128)(2,1)} %param.18) | copy-start | bytes 49156
  66.4 3.8 %copy-start.17 = (f32[4]{0:T(128)S(1)}, f32[4]{0:T(128)}, u32[]{:S(2)}) copy-start(f32[4]{0:T(128)} %param.17) | copy-start | bytes 52
  66.4 3.8 %copy-start.18 = (f32[4]{0:T(128)S(1)}, f32[4]{0:T(128)}, u32[]{:S(2)}) copy-start(f32[4]{0:T(128)} %param.16) | copy-start | bytes 52
  95.5 2.9 %copy-start.4 = (s32[2048,3]{1,0:T(8,128)S(1)}, s32[2048,3]{1,0:T(8,128)}, u32[]{:S(2)}) copy-start(s32[2048,3]{1,0:T(8,128)} %copy.32.ids) | copy-start | bytes 73732
  96.2 2.2 collective-permute-start.1
  98.4 1.2 copy-start.6
  112.6 1.6 collective-permute-start.3
  127.0 47.6 %all-to-all-start.3 = ((bf16[16,192,256]{2,1,0:T(8,128)(2,1)}), bf16[16,192,256]{2,1,0:T(8,128)(2,1)S(1)}, u32[]{:S(2)}, u32[]{:S(2)}) async-start(bf16[16,192,256]{2,1,0:T(8,128)(2,1)} %shard_map.150), calls=%async_computation.3 | async-start | bytes 3145728 | tf_op jit(solution)/shard_map/all_to_all | solution.py:401
  133.9 13.5 %copy-start.5 = (s32[2048,3]{1,0:T(8,128)S(1)}, s32[2048,3]{1,0:T(8,128)}, u32[]{:S(2)}) copy-start(s32[2048,3]{1,0:T(8,128)} %copy.32.ids) | copy-start | bytes 73732
  133.9 13.5 %copy-start.7 = (f32[2048,6]{1,0:T(8,128)S(1)}, f32[2048,6]{1,0:T(8,128)}, u32[]{:S(2)}) copy-start(f32[2048,6]{1,0:T(8,128)} %copy.33.numbers) | copy-start | bytes 147460
  145.9 1.5 collective-permute-start
  160.3 1.5 collective-permute-start.2
  174.6 1.1 copy-start.2
  175.7 44.3 %all-to-all-start.2 = ((bf16[16,192,256]{2,1,0:T(8,128)(2,1)}), bf16[16,192,256]{2,1,0:T(8,128)(2,1)}, u32[]{:S(2)}, u32[]{:S(2)}) async-start(bf16[16,192,256]{2,1,0:T(8,128)(2,1)} %shard_map.148), calls=%async_computation.2 | async-start | bytes 3145728 | tf_op jit(solution)/shard_map/all_to_all | solution.py:401
  182.6 4.3 %copy-start.3 = (bf16[16,192,256]{2,1,0:T(8,128)(2,1)S(1)}, bf16[16,192,256]{2,1,0:T(8,128)(2,1)}, u32[]{:S(2)}) copy-start(bf16[16,192,256]{2,1,0:T(8,128)(2,1)} %copy-done.2) | copy-start | bytes 4718596

commit v3 on v2

--- a/solution.py
+++ b/solution.py
@@ -153,92 +153,116 @@
     )(*operands)
 
 
-def band_kernel(levels, spread, out):
-    rows, columns = spread.shape
-    full = jnp.broadcast_to(spread[...][None], (levels, rows, columns))
-    level = lax.broadcasted_iota(jnp.int32, full.shape, 0)
-    lane = lax.broadcasted_iota(jnp.int32, (1, 1, columns), 2) % levels
+def band_kernel(group, coef, lanes, out):
+    pair, band_rows = 2, out.shape[1] // (2 * group)
+    columns = out.shape[2]
+    base = pl.program_id(0) * pair * band_rows
+    row = lax.broadcasted_iota(jnp.int32, (pair * band_rows, columns), 0) + base
+    apart = jnp.abs(row - lanes[...]).astype(F32)
+    value = gaussians(apart, coef).reshape(pair, 1, band_rows, columns)
+    full = jnp.broadcast_to(value, (pair, group, band_rows, columns))
+    level = lax.broadcasted_iota(jnp.int32, full.shape, 1)
+    lane = lax.broadcasted_iota(jnp.int32, (1, 1, 1, columns), 3) % group
     full = jnp.where(lane == level, full, 0.0)
-    out[0] = full.reshape(levels * rows, columns).astype(BF16)
-
-
-def band_matrices(spread, levels, bands):
-    all_rows, columns = spread.shape
-    band_rows = all_rows // bands
-    rows = levels * band_rows
-    return pl.pallas_call(
-        functools.partial(band_kernel, levels),
-        out_shape=jax.ShapeDtypeStruct((bands, rows, columns), BF16),
-        grid=(bands,),
-        in_specs=[pl.BlockSpec((band_rows, columns), lambda at: (at, 0))],
+    out[0] = full.reshape(pair * group * band_rows, columns).astype(BF16)
+
+
+def band_matrices(coef, lanes, group, band_rows, bands):
+    columns = lanes.shape[1]
+    rows = 2 * group * band_rows
+    return pl.pallas_call(
+        functools.partial(band_kernel, group),
+        out_shape=jax.ShapeDtypeStruct((bands // 2, rows, columns), BF16),
+        grid=(bands // 2,),
+        in_specs=[
+            pl.BlockSpec(memory_space=pltpu.SMEM),
+            pl.BlockSpec((1, columns), lambda at: (0, 0)),
+        ],
         out_specs=pl.BlockSpec((1, rows, columns), lambda at: (at, 0, 0)),
         compiler_params=params(),
-        cost_estimate=cost(10 * bands * rows * columns, 2 * bands * rows * columns),
-    )(spread)
+        cost_estimate=cost(5 * bands * rows * columns, bands * rows * columns),
+    )(coef, lanes)
 
 
 def meridional_forward_kernel(lines, matrix, out, total):
     at = pl.program_id(0)
-    product = jnp.dot(lines[0], matrix[0], preferred_element_type=F32)
-
-    @pl.when(at == 0)
-    def _():
-        total[...] = product
-
-    @pl.when(at > 0)
-    def _():
-        total[...] += product
+    groups, strip, columns = total.shape
+    part = lines.shape[2] // groups
+    owners, share = out.shape[0], columns // out.shape[0]
+    for group in range(groups):
+        cells = slice(group * part, (group + 1) * part)
+        both = jnp.concatenate([lines[0, :, cells], lines[1, :, cells]], axis=1)
+        product = jnp.dot(both, matrix[0], preferred_element_type=F32)
+
+        @pl.when(at == 0)
+        def _():
+            total[group] = product
+
+        @pl.when(at > 0)
+        def _():
+            total[group] += product
 
     @pl.when(at == pl.num_programs(0) - 1)
     def _():
-        owners, _, share = out.shape
         for owner in range(owners):
-            out[owner] = total[:, owner * share : (owner + 1) * share].astype(BF16)
-
-
-def meridional_forward(lines, matrices, owners):
+            for group in range(groups):
+                out[owner, :, group * share : (group + 1) * share] = total[
+                    group, :, owner * share : (owner + 1) * share
+                ].astype(BF16)
+
+
+def meridional_forward(lines, matrices, owners, groups):
     bands, strip, rows = lines.shape
-    columns = matrices.shape[2]
+    pairs, depth, columns = matrices.shape
     return pl.pallas_call(
         meridional_forward_kernel,
-        out_shape=jax.ShapeDtypeStruct((owners, strip, columns // owners), BF16),
-        grid=(bands,),
+        out_shape=jax.ShapeDtypeStruct((owners, strip, groups * columns // owners), BF16),
+        grid=(pairs,),
         in_specs=[
-            pl.BlockSpec((1, strip, rows), lambda at: (at, 0, 0)),
-            pl.BlockSpec((1, rows, columns), lambda at: (at, 0, 0)),
+            pl.BlockSpec((2, strip, rows), lambda at: (at, 0, 0)),
+            pl.BlockSpec((1, depth, columns), lambda at: (at, 0, 0)),
         ],
-        out_specs=pl.BlockSpec((owners, strip, columns // owners), lambda at: (0, 0, 0)),
-        scratch_shapes=[pltpu.VMEM((strip, columns), F32)],
+        out_specs=pl.BlockSpec(
+            (owners, strip, groups * columns // owners), lambda at: (0, 0, 0)
+        ),
+        scratch_shapes=[pltpu.VMEM((groups, strip, columns), F32)],
         compiler_params=params(),
         cost_estimate=cost(2 * bands * strip * rows * columns, 2 * bands * strip * rows),
     )(lines, matrices)
 
 
-def meridional_backward_kernel(own, other, matrix, out):
-    share = own.shape[1]
-    transposed = (((1,), (1,)), ((), ()))
-    total = lax.dot_general(
-        own[...], matrix[0, :, :share], transposed, preferred_element_type=F32
-    ) + lax.dot_general(other[...], matrix[0, :, share:], transposed, preferred_element_type=F32)
-    out[0] = total.astype(BF16)
-
-
-def meridional_backward(own, other, matrices):
-    bands, rows, columns = matrices.shape
+def meridional_backward_kernel(groups, own, other, matrix, out):
+    share = own.shape[1] // groups
+    part = out.shape[2] // groups
+    for group in range(groups):
+        cells = slice(group * share, (group + 1) * share)
+        both = jnp.concatenate([own[:, cells], other[:, cells]], axis=1)
+        product = lax.dot_general(
+            both, matrix[0], (((1,), (1,)), ((), ())), preferred_element_type=F32
+        ).astype(BF16)
+        for band in range(2):
+            out[band, :, group * part : (group + 1) * part] = product[
+                :, band * part : (band + 1) * part
+            ]
+
+
+def meridional_backward(own, other, matrices, groups):
+    pairs, depth, columns = matrices.shape
     strip, share = own.shape
+    rows = depth * groups // 2
     half = pl.BlockSpec((strip, share), lambda at: (0, 0))
     return pl.pallas_call(
-        meridional_backward_kernel,
-        out_shape=jax.ShapeDtypeStruct((bands, strip, rows), BF16),
-        grid=(bands,),
-        in_specs=[half, half, pl.BlockSpec((1, rows, columns), lambda at: (at, 0, 0))],
-        out_specs=pl.BlockSpec((1, strip, rows), lambda at: (at, 0, 0)),
-        compiler_params=params(),
-        cost_estimate=cost(2 * bands * strip * rows * columns, 2 * bands * strip * rows),
+        functools.partial(meridional_backward_kernel, groups),
+        out_shape=jax.ShapeDtypeStruct((2 * pairs, strip, rows), BF16),
+        grid=(pairs,),
+        in_specs=[half, half, pl.BlockSpec((1, depth, columns), lambda at: (at, 0, 0))],
+        out_specs=pl.BlockSpec((2, strip, rows), lambda at: (at, 0, 0)),
+        compiler_params=params(),
+        cost_estimate=cost(4 * pairs * strip * rows * columns, 4 * pairs * strip * rows),
     )(own, other, matrices)
 
 
-def reports_kernel(variable, share, own, other, ids, numbers, cells, weights, maps, departure, lifted, total):
+def reports_kernel(variable, group, kept_rows, own, other, ids, numbers, cells, weights, maps, departure, lifted, total):
     at = pl.program_id(0)
     strip, columns = own.shape
     block = ids.shape[0]
@@ -259,7 +283,7 @@
     level = ids[:, 2:3] - variable * levels
     chosen = jnp.where(lax.broadcasted_iota(jnp.int32, (block, levels), 1) == level, 1.0, 0.0)
     chosen = chosen.astype(BF16)
-    lane = lax.broadcasted_iota(jnp.int32, (block, columns), 1) // share
+    lane = lax.broadcasted_iota(jnp.int32, (block, columns), 1) // group % kept_rows
     hits = [lane == ids[:, 1:2], lane == ids[:, 1:2] + 1]
     fields = (own, other)
     model = jnp.zeros((block, 1), F32)
@@ -274,12 +298,11 @@
             found = found + values * picked
         model = model + jnp.sum(found, axis=1, keepdims=True)
     result = numbers[:, 5:6] * (model - numbers[:, 4:5])
+    both = jnp.concatenate(turned, axis=1)
     departure[...] = jnp.broadcast_to(result, (block, 128)).T[0:1, :]
     for half in range(2):
-        product = jnp.zeros((strip, columns), F32)
-        for side in range(2):
-            pushes = (kept[2 * half + side] * result).astype(BF16)
-            product = product + jnp.dot(turned[side], pushes, preferred_element_type=F32)
+        pushes = [(kept[2 * half + side] * result).astype(BF16) for side in range(2)]
+        product = jnp.dot(both, jnp.concatenate(pushes, axis=0), preferred_element_type=F32)
 
         @pl.when(at == 0)
         def _():
@@ -294,13 +317,13 @@
         lifted[...] = total[...].astype(BF16)
 
 
-def at_reports(variable, share, own, other, ids, numbers, cells, weights, maps):
+def at_reports(variable, group, kept_rows, own, other, ids, numbers, cells, weights, maps):
     strip, columns = own.shape
     reports = ids.shape[0]
     block = math.gcd(reports, 256)
     half = pl.BlockSpec((strip, columns), lambda at: (0, 0))
     return pl.pallas_call(
-        functools.partial(reports_kernel, variable, share),
+        functools.partial(reports_kernel, variable, group, kept_rows),
         out_shape=(
             jax.ShapeDtypeStruct((1, reports), F32),
             jax.ShapeDtypeStruct((2, strip, columns), BF16),
@@ -354,13 +377,13 @@
     zonal = coefficients(zonal_scales, zonal_heights)
     wide = table(wide_table_kernel, (TILE, 2 * width), width, zonal)
     fields = control.reshape(variables, share * band_rows, width)
-    sent = []
-    for variable in range(variables):
-        smooth = zonal_forward(fields, wide, variable).reshape(lat_count, strip, -1)
-        sent.append(lax.all_to_all(smooth, "lat", split_axis=0, concat_axis=0, tiled=True))
-
-    tall = table(tall_table_kernel, (2 * width, TILE), width, zonal)
-
+    smooth = [
+        zonal_forward(fields, wide, variable).reshape(lat_count, strip, -1)
+        for variable in range(variables)
+    ]
+
+    group = 128 // band_rows
+    groups = share // group
     me = lax.axis_index("obs")
     partner = [(0, 1), (1, 0)]
     blocks = lax.all_gather(send_blocks.reshape(owners, SLOTS), "obs", axis=0)
@@ -368,11 +391,9 @@
     starts = jnp.transpose(source * (all_rows // owners) + blocks * BR, (1, 0, 2))
     starts = jnp.where(me == 0, starts, starts[::-1])
     rows = starts[..., None] + jnp.arange(BR)
-    lanes = jnp.repeat(rows.reshape(-1), share)
-    apart = jnp.abs(jnp.arange(all_rows)[:, None] - lanes[None, :]).astype(F32)
+    lanes = jnp.repeat(rows.reshape(-1), group).reshape(1, -1).astype(jnp.int32)
     meridional = coefficients(meridional_scales, meridional_heights)
-    spread = gaussians(apart, meridional).astype(BF16).astype(F32)
-    matrices = band_matrices(spread, share, lat_count)
+    matrices = band_matrices(meridional, lanes, group, band_rows, lat_count)
 
     slot = report_slot.reshape(1, reports)
     code = report_level.reshape(1, reports)
@@ -383,21 +404,32 @@
     numbers = jnp.concatenate(
         [weight, innovation.reshape(1, reports), report_precision.reshape(1, reports)], axis=0
     ).T
-    maps = vertical_map.reshape(variables, levels, owners, share).transpose(0, 2, 1, 3)
+    maps = vertical_map.reshape(variables, levels, owners, groups, 1, group)
+    maps = maps.transpose(0, 2, 1, 3, 4, 5)
     maps = jnp.where(me == 0, maps, maps[:, ::-1])
-    maps = jnp.tile(maps, (1, 1, 1, kept))
+    maps = jnp.broadcast_to(maps, (variables, owners, levels, groups, kept, group))
+    maps = maps.reshape(variables, owners, levels, groups * kept * group)
+    tall = table(tall_table_kernel, (2 * width, TILE), width, zonal)
+
+    last, matrices, ids, numbers, cells, maps, tall = lax.optimization_barrier(
+        (smooth[-1], matrices, ids, numbers, cells, maps, tall)
+    )
+    smooth[-1] = last
+    sent = [
+        lax.all_to_all(part, "lat", split_axis=0, concat_axis=0, tiled=True) for part in smooth
+    ]
 
     departures = []
     lines = []
     for variable in range(variables):
-        mixed = meridional_forward(sent[variable], matrices, owners)
+        mixed = meridional_forward(sent[variable], matrices, owners, groups)
         theirs = lax.ppermute(mixed[1], "obs", partner)
         departure, lifted = at_reports(
-            variable, share, mixed[0], theirs, ids, numbers, cells, weight, maps
+            variable, group, kept, mixed[0], theirs, ids, numbers, cells, weight, maps
         )
         departures.append(departure)
         theirs = lax.ppermute(lifted[1], "obs", partner)
-        back = meridional_backward(lifted[0], theirs, matrices)
+        back = meridional_backward(lifted[0], theirs, matrices, groups)
         lines.append(lax.all_to_all(back, "lat", split_axis=0, concat_axis=0, tiled=True))
 
     gradient = None

time: 232 us -> 196 us (0.84)
  Pallas kernels: 129 us -> 93.7 us
  waiting for transfers between devices: 50.5 us -> 62.3 us
  starting transfers between devices: 26.8 us -> 21.4 us
  other arithmetic: 7.88 us -> 2.57 us
    pallas_call x5, Pallas kernels: 58.7 us -> 33.5 us  [the longest x2 26.9 us: at_reports(): pl.pallas_call(functools.partial(reports_kernel, variable, group, kept_ro...]
    all_to_all x2, waiting for transfers between devices: 24.4 us -> 36.2 us  [on_device(): lax.all_to_all(back, 'lat', split_axis=0, concat_axis=0, tiled=True)]
    pallas_call x2, Pallas kernels: 23.7 us -> 12.6 us  [meridional_forward(): pl.pallas_call(meridional_forward_kernel, out_shape=jax.ShapeDtypeStruct(...]
    convert_element_type x1 -> x0, other arithmetic: 5.37 us -> none  [on_device(): spread = gaussians(apart, meridional).astype(BF16).astype(F32)]
    all_to_all x2, starting transfers between devices: 13.8 us -> 8.61 us  [on_device(): lax.all_to_all(back, 'lat', split_axis=0, concat_axis=0, tiled=True)]
    transpose x2 -> x0, local copies, waits for them, and re-layouts: 2.72 us -> none  [the longest x1 1.37 us: on_device(): numbers = jnp.concatenate([weight, innovation.reshape(1, reports), report...]
    unnamed x39 -> x41, local copies, waits for them, and re-layouts: 7.21 us -> 9.02 us
  transfers between devices with their start and end apart: 8 -> 8, of which waited for: 5 -> 7; matrix products, arithmetic and copies ran while one was open for 6% -> 3% of each run, Pallas kernels for 45% -> 36%
where the time goes in v3:
time: 196 us; the launch traced here: 195 us
  Pallas kernels  93.7 us (48%)
  waiting for transfers between devices  62.3 us (32%)
  starting transfers between devices  21.4 us (11%)
  local copies, waits for them, and re-layouts  12.2 us (6%)
  other arithmetic  2.57 us (1%)
    all_to_all x2, waiting for transfers between devices, on_device(): lax.all_to_all(back, 'lat', split_axis=0, concat_axis=0, tiled=True)  36.2 us
    pallas_call x2, Pallas kernels, at_reports(): pl.pallas_call(functools.partial(reports_kernel, variable, group, kept_ro...  26.9 us
    all_to_all x2, waiting for transfers between devices, on_device(): lax.all_to_all(part, 'lat', split_axis=0, concat_axis=0, tiled=True)  22.3 us
    pallas_call x2, Pallas kernels, zonal_backward(): pl.pallas_call(functools.partial(zonal_backward_kernel, width), out_shape...  20.3 us
    pallas_call x2, Pallas kernels, zonal_forward(): pl.pallas_call(functools.partial(zonal_forward_kernel, width), out_shape=...  20 us
    pallas_call x2, Pallas kernels, meridional_forward(): pl.pallas_call(meridional_forward_kernel, out_shape=jax.ShapeDtypeStruct(...  12.6 us
    all_to_all x2, starting transfers between devices, on_device(): lax.all_to_all(part, 'lat', split_axis=0, concat_axis=0, tiled=True)  12 us
    unnamed x41, local copies, waits for them, and re-layouts  9.02 us
  transfers between devices with their start and end apart: 8, of which 7 were waited for; matrix products, arithmetic and copies ran while one was open for 3% of the time, Pallas kernels for 36%

profile of v3, /device:TPU:12, one launch (start us, length us, event | category | flops | bytes accessed | tf_op | source)
XLA Modules:
  0.0 194.9 jit_solution(9075816153534597174)
XLA Ops:
  0.6 0.7 fusion.4
  1.3 0.1 pad_maximum_fusion.coef
  1.4 3.6 %shard_map.140.wide = bf16[256,6144]{1,0:T(8,128)(2,1)S(1)} custom-call(f32[8]{0:T(128)S(1)} %pad_maximum_fusion.coef), custom_call_target="tpu_custom_call" | custom-call | flops 47185920 | bytes 3145728 | tf_op jit(solution)/shard_map/pallas_call | solution.py:75
  5.0 1.7 copy-done.4
  6.7 10.4 %shard_map.146 = bf16[3072,256]{1,0:T(8,128)(2,1)} custom-call(bf16[2,256,3072]{2,1,0:T(8,128)(2,1)S(1)} %bitcast.70, bf16[256,6144]{1,0:T(8,128)(2,1)} %copy-done.4), custom_call_target="tpu_custom_call" | custom-call | flops 4831838208 | bytes 7864320 | tf_op jit(solution)/shard_map/pallas_call | solution.py:102
  17.1 7.3 %all-to-all-start.1 = ((bf16[16,192,256]{2,1,0:T(8,128)(2,1)}), bf16[16,192,256]{2,1,0:T(8,128)(2,1)}, u32[]{:S(2)}, u32[]{:S(2)}) async-start(bf16[16,192,256]{2,1,0:T(8,128)(2,1)} %bitcast.21), calls=%async_computation.1 | async-start | bytes 3145728 | tf_op jit(solution)/shard_map/all_to_all | solution.py:419
  24.4 1.8 all-gather
  26.2 0.1 fusion.3
  26.3 0.1 broadcast_select_fusion
  26.5 0.1 add.64
  26.6 0.1 reshape_reshape.3.lanes
  26.7 0.1 copy.31
  26.9 0.1 pad_maximum_fusion.1.coef
  26.9 1.3 shard_map.142.matrix
  28.3 3.6 %shard_map.143.tall = bf16[6144,256]{1,0:T(8,128)(2,1)S(1)} custom-call(f32[8]{0:T(128)S(1)} %pad_maximum_fusion.coef), custom_call_target="tpu_custom_call" | custom-call | flops 47185920 | bytes 3145728 | tf_op jit(solution)/shard_map/pallas_call | solution.py:75
  32.0 1.6 copy-done.2
  33.6 0.8 and_select_fusion
  34.6 9.6 %shard_map.141 = bf16[3072,256]{1,0:T(8,128)(2,1)S(1)} custom-call(bf16[2,256,3072]{2,1,0:T(8,128)(2,1)S(1)} %bitcast.71, bf16[256,6144]{1,0:T(8,128)(2,1)} %copy-done.4), custom_call_target="tpu_custom_call" | custom-call | flops 4831838208 | bytes 7864320 | tf_op jit(solution)/shard_map/pallas_call | solution.py:102
  44.2 1.1 copy-done.5
  45.4 16.3 %all-to-all-done.1.lines = bf16[16,192,256]{2,1,0:T(8,128)(2,1)} async-done(((bf16[16,192,256]{2,1,0:T(8,128)(2,1)}), bf16[16,192,256]{2,1,0:T(8,128)(2,1)}, u32[]{:S(2)}, u32[]{:S(2)}) %all-to-all-start.1) | async-done | bytes 1572896 | tf_op jit(solution)/shard_map/all_to_all | solution.py:419
  61.7 4.6 %all-to-all-start = ((bf16[16,192,256]{2,1,0:T(8,128)(2,1)}), bf16[16,192,256]{2,1,0:T(8,128)(2,1)}, u32[]{:S(2)}, u32[]{:S(2)}) async-start(bf16[16,192,256]{2,1,0:T(8,128)(2,1)} %bitcast.66), calls=%async_computation | async-start | bytes 3145728 | tf_op jit(solution)/shard_map/all_to_all | solution.py:419
  66.3 6.3 %shard_map.147 = bf16[2,192,512]{2,1,0:T(8,128)(2,1)S(1)} custom-call(bf16[16,192,256]{2,1,0:T(8,128)(2,1)} %all-to-all-done.1.lines, bf16[8,256,512]{2,1,0:T(8,128)(2,1)S(1)} %shard_map.142.matrix), custom_call_target="tpu_custom_call" | custom-call | flops 805306368 | bytes 1572864 | tf_op jit(solution)/shard_map/pallas_call | solution.py:217
  72.6 0.8 slice_bitcast_fusion
  73.4 0.2 copy.34.maps
  73.6 0.4 copy.32.ids
  74.0 1.4 copy.33.numbers
  75.4 1.2 copy-done.6
  76.7 0.9 copy-done.8
  77.6 13.9 %shard_map.148 = (f32[1,2048]{1,0:T(1,128)S(1)}, bf16[2,192,512]{2,1,0:T(8,128)(2,1)S(1)}) custom-call(bf16[192,512]{1,0:T(8,128)(2,1)S(1)} %copy-done.8, bf16[192,512]{1,0:T(8,128)(2,1)} %collective-permute-done.1.other, s32[2048,3]{1,0:T(8,128)S(1)} %copy.32.ids, f32[2048,6]{1,0:T(8,128)S(1)} %copy-done.6, s32[1,2048]{1,0:T(1,128)S(1)} %get-tuple-element.17.cells, ...), custom_call_target="tpu_custom_call" | custom-call | flops 4294967296 | bytes 1048576 | tf_op jit(solution)/shard_map/pallas_call | solution.py:325
  91.5 0.6 collective-permute-start.3
  92.1 1.1 collective-permute-done.3.other
  93.2 2.6 %shard_map.150 = bf16[16,192,256]{2,1,0:T(8,128)(2,1)S(1)} custom-call(bf16[192,512]{1,0:T(8,128)(2,1)S(1)} %get-tuple-element.25.own, bf16[192,512]{1,0:T(8,128)(2,1)S(1)} %collective-permute-done.3.other, bf16[8,256,512]{2,1,0:T(8,128)(2,1)S(1)} %shard_map.142.matrix), custom_call_target="tpu_custom_call" | custom-call | flops 805306368 | bytes 1572864 | tf_op jit(solution)/shard_map/pallas_call | solution.py:254
  95.8 1.2 copy-done
  97.0 6.0 %all-to-all-done.lines = bf16[16,192,256]{2,1,0:T(8,128)(2,1)} async-done(((bf16[16,192,256]{2,1,0:T(8,128)(2,1)}), bf16[16,192,256]{2,1,0:T(8,128)(2,1)}, u32[]{:S(2)}, u32[]{:S(2)}) %all-to-all-start) | async-done | bytes 1572896 | tf_op jit(solution)/shard_map/all_to_all | solution.py:419
  102.9 4.3 %all-to-all-start.3 = ((bf16[16,192,256]{2,1,0:T(8,128)(2,1)}), bf16[16,192,256]{2,1,0:T(8,128)(2,1)}, u32[]{:S(2)}, u32[]{:S(2)}) async-start(bf16[16,192,256]{2,1,0:T(8,128)(2,1)} %copy-done), calls=%async_computation.3 | async-start | bytes 3145728 | tf_op jit(solution)/shard_map/all_to_all | solution.py:433
  107.3 6.4 %shard_map.144 = bf16[2,192,512]{2,1,0:T(8,128)(2,1)S(1)} custom-call(bf16[16,192,256]{2,1,0:T(8,128)(2,1)} %all-to-all-done.lines, bf16[8,256,512]{2,1,0:T(8,128)(2,1)S(1)} %shard_map.142.matrix), custom_call_target="tpu_custom_call" | custom-call | flops 805306368 | bytes 1572864 | tf_op jit(solution)/shard_map/pallas_call | solution.py:217
  113.8 1.4 collective-permute-done.other
  115.2 13.0 %shard_map.145 = (f32[1,2048]{1,0:T(1,128)S(1)}, bf16[2,192,512]{2,1,0:T(8,128)(2,1)S(1)}) custom-call(bf16[192,512]{1,0:T(8,128)(2,1)S(1)} %get-tuple-element.31.own, bf16[192,512]{1,0:T(8,128)(2,1)S(1)} %collective-permute-done.other, s32[2048,3]{1,0:T(8,128)S(1)} %copy.32.ids, f32[2048,6]{1,0:T(8,128)S(1)} %copy-done.7, ...), custom_call_target="tpu_custom_call" | custom-call | flops 4294967296 | bytes 1048576 | tf_op jit(solution)/shard_map/pallas_call | solution.py:325
  128.2 0.2 collective-permute-start.2
  128.4 1.3 collective-permute-done.2.other
  129.7 2.6 %shard_map.149 = bf16[16,192,256]{2,1,0:T(8,128)(2,1)S(1)} custom-call(bf16[192,512]{1,0:T(8,128)(2,1)S(1)} %get-tuple-element.27.own, bf16[192,512]{1,0:T(8,128)(2,1)S(1)} %collective-permute-done.2.other, bf16[8,256,512]{2,1,0:T(8,128)(2,1)S(1)} %shard_map.142.matrix), custom_call_target="tpu_custom_call" | custom-call | flops 805306368 | bytes 1572864 | tf_op jit(solution)/shard_map/pallas_call | solution.py:254
  132.4 1.1 copy-done.1
  133.5 10.3 %all-to-all-done.3 = bf16[16,192,256]{2,1,0:T(8,128)(2,1)} async-done(((bf16[16,192,256]{2,1,0:T(8,128)(2,1)}), bf16[16,192,256]{2,1,0:T(8,128)(2,1)}, u32[]{:S(2)}, u32[]{:S(2)}) %all-to-all-start.3) | async-done | bytes 1572896 | tf_op jit(solution)/shard_map/all_to_all | solution.py:433
  143.9 4.3 %all-to-all-start.2 = ((bf16[16,192,256]{2,1,0:T(8,128)(2,1)}), bf16[16,192,256]{2,1,0:T(8,128)(2,1)}, u32[]{:S(2)}, u32[]{:S(2)}) async-start(bf16[16,192,256]{2,1,0:T(8,128)(2,1)} %copy-done.1), calls=%async_computation.2 | async-start | bytes 3145728 | tf_op jit(solution)/shard_map/all_to_all | solution.py:433
  148.2 0.6 fusion.2
  148.8 10.2 %shard_map.151.rest_0_ = f32[2,256,3072]{2,1,0:T(8,128)} custom-call(bf16[3072,256]{1,0:T(8,128)(2,1)} %bitcast.30.lines, bf16[6144,256]{1,0:T(8,128)(2,1)S(1)} %copy-done.3), custom_call_target="tpu_custom_call" | custom-call | flops 4831838208 | bytes 9437184 | tf_op jit(solution)/shard_map/pallas_call | solution.py:143
  158.9 25.8 %all-to-all-done.2 = bf16[16,192,256]{2,1,0:T(8,128)(2,1)} async-done(((bf16[16,192,256]{2,1,0:T(8,128)(2,1)}), bf16[16,192,256]{2,1,0:T(8,128)(2,1)}, u32[]{:S(2)}, u32[]{:S(2)}) %all-to-all-start.2) | async-done | bytes 1572896 | tf_op jit(solution)/shard_map/all_to_all | solution.py:433
  184.8 10.2 %shard_map.152 = f32[2,256,3072]{2,1,0:T(8,128)} custom-call(bf16[3072,256]{1,0:T(8,128)(2,1)} %bitcast.27.lines, bf16[6144,256]{1,0:T(8,128)(2,1)S(1)} %copy-done.3, f32[2,256,3072]{2,1,0:T(8,128)} %shard_map.151.rest_0_), custom_call_target="tpu_custom_call", output_to_operand_aliasing={{}: (2, {})} | custom-call | flops 4831838208 | bytes 9437184 | tf_op jit(solution)/shard_map/pallas_call | solution.py:143
  (49 shorter events, 0.6 us)
Async XLA Ops:
  1.4 5.3 %copy-start.10 = (bf16[2,32,8,3072]{3,2,1,0:T(8,128)(2,1)S(1)}, bf16[2,32,8,3072]{3,2,1,0:T(8,128)(2,1)}, u32[]{:S(2)}) copy-start(bf16[2,32,8,3072]{3,2,1,0:T(8,128)(2,1)} %param.13) | copy-start | bytes 9437188
  5.0 1.7 copy-start.4
  17.1 7.3 %copy-start.17 = (s32[1,1,2,2]{3,2,1,0:T(2,128)S(1)}, s32[1,1,2,2]{3,2,1,0:T(2,128)}, u32[]{:S(2)}) copy-start(s32[1,1,2,2]{3,2,1,0:T(2,128)} %param.19) | copy-start | bytes 52
  17.1 9.6 %copy-start.12 = (bf16[2,64,64]{2,1,0:T(8,128)(2,1)S(1)}, bf16[2,64,64]{2,1,0:T(8,128)(2,1)}, u32[]{:S(2)}) copy-start(bf16[2,64,64]{2,1,0:T(8,128)(2,1)} %param.18) | copy-start | bytes 49156
  17.1 9.7 %copy-start.18 = (f32[4]{0:T(128)S(1)}, f32[4]{0:T(128)}, u32[]{:S(2)}) copy-start(f32[4]{0:T(128)} %param.16) | copy-start | bytes 52
  17.1 9.7 %copy-start.19 = (f32[4]{0:T(128)S(1)}, f32[4]{0:T(128)}, u32[]{:S(2)}) copy-start(f32[4]{0:T(128)} %param.17) | copy-start | bytes 52
  17.1 44.6 %all-to-all-start.1 = ((bf16[16,192,256]{2,1,0:T(8,128)(2,1)}), bf16[16,192,256]{2,1,0:T(8,128)(2,1)}, u32[]{:S(2)}, u32[]{:S(2)}) async-start(bf16[16,192,256]{2,1,0:T(8,128)(2,1)} %bitcast.21), calls=%async_computation.1 | async-start | bytes 3145728 | tf_op jit(solution)/shard_map/all_to_all | solution.py:419
  26.9 6.7 %copy-start.16 = (s32[1,1,2048]{2,1,0:T(1,128)S(1)}, s32[1,1,2048]{2,1,0:T(1,128)}, u32[]{:S(2)}) copy-start(s32[1,1,2048]{2,1,0:T(1,128)} %param.20) | copy-start | bytes 24580
  26.9 7.5 %copy-start.13 = (s32[1,1,2048]{2,1,0:T(1,128)S(1)}, s32[1,1,2048]{2,1,0:T(1,128)}, u32[]{:S(2)}) copy-start(s32[1,1,2048]{2,1,0:T(1,128)} %param.21) | copy-start | bytes 24580
  28.3 6.2 %copy-start.9 = (f32[1,1,4,2048]{3,2,1,0:T(4,128)S(1)}, f32[1,1,4,2048]{3,2,1,0:T(4,128)}, u32[]{:S(2)}) copy-start(f32[1,1,4,2048]{3,2,1,0:T(4,128)} %param.23) | copy-start | bytes 98308
  28.3 6.2 %copy-start.14 = (f32[1,1,2048]{2,1,0:T(1,128)S(1)}, f32[1,1,2048]{2,1,0:T(1,128)}, u32[]{:S(2)}) copy-start(f32[1,1,2048]{2,1,0:T(1,128)} %param.25) | copy-start | bytes 24580
  28.3 6.2 %copy-start.15 = (f32[1,1,2048]{2,1,0:T(1,128)S(1)}, f32[1,1,2048]{2,1,0:T(1,128)}, u32[]{:S(2)}) copy-start(f32[1,1,2048]{2,1,0:T(1,128)} %param.24) | copy-start | bytes 24580
  28.3 6.3 %copy-start.11 = (bf16[2,32,8,3072]{3,2,1,0:T(8,128)(2,1)S(1)}, bf16[2,32,8,3072]{3,2,1,0:T(8,128)(2,1)}, u32[]{:S(2)}) copy-start(bf16[2,32,8,3072]{3,2,1,0:T(8,128)(2,1)} %param.13) | copy-start | bytes 9437188
  32.0 1.6 copy-start.2
  44.2 1.1 copy-start.5
  61.7 41.2 %all-to-all-start = ((bf16[16,192,256]{2,1,0:T(8,128)(2,1)}), bf16[16,192,256]{2,1,0:T(8,128)(2,1)}, u32[]{:S(2)}, u32[]{:S(2)}) async-start(bf16[16,192,256]{2,1,0:T(8,128)(2,1)} %bitcast.66), calls=%async_computation | async-start | bytes 3145728 | tf_op jit(solution)/shard_map/all_to_all | solution.py:419
  73.4 2.0 %collective-permute-start.1 = (bf16[192,512]{1,0:T(8,128)(2,1)}, bf16[192,512]{1,0:T(8,128)(2,1)}, u32[]{:S(2)}, u32[]{:S(2)}) collective-permute-start(bf16[192,512]{1,0:T(8,128)(2,1)} %get-tuple-element.28), channel_id=1, source_target_pairs={{0,1},{1,0},{2,3},{3,2},{4,5},{5,4},{6,7},{7,6},{8,9},{9,8},{10,11... | collective-permute-start | bytes 589832 | tf_op jit(solution)/shard_map/ppermute | solution.py:426
  75.4 1.2 copy-start.6
  76.7 0.9 copy-start.8
  91.5 1.7 collective-permute-start.3
  95.8 1.2 copy-start
  102.9 40.9 %all-to-all-start.3 = ((bf16[16,192,256]{2,1,0:T(8,128)(2,1)}), bf16[16,192,256]{2,1,0:T(8,128)(2,1)}, u32[]{:S(2)}, u32[]{:S(2)}) async-start(bf16[16,192,256]{2,1,0:T(8,128)(2,1)} %copy-done), calls=%async_computation.3 | async-start | bytes 3145728 | tf_op jit(solution)/shard_map/all_to_all | solution.py:433
  107.3 7.9 %copy-start.7 = (f32[2048,6]{1,0:T(8,128)S(1)}, f32[2048,6]{1,0:T(8,128)}, u32[]{:S(2)}) copy-start(f32[2048,6]{1,0:T(8,128)} %copy.33.numbers) | copy-start | bytes 147460
  113.7 1.5 collective-permute-start
  128.2 1.5 collective-permute-start.2
  132.4 1.1 copy-start.1
  133.5 15.3 %copy-start.3 = (bf16[6144,256]{1,0:T(8,128)(2,1)S(1)}, bf16[6144,256]{1,0:T(8,128)(2,1)}, u32[]{:S(2)}) copy-start(bf16[6144,256]{1,0:T(8,128)(2,1)} %copy-done.2) | copy-start | bytes 9437188
  143.9 40.9 %all-to-all-start.2 = ((bf16[16,192,256]{2,1,0:T(8,128)(2,1)}), bf16[16,192,256]{2,1,0:T(8,128)(2,1)}, u32[]{:S(2)}, u32[]{:S(2)}) async-start(bf16[16,192,256]{2,1,0:T(8,128)(2,1)} %copy-done.1), calls=%async_computation.2 | async-start | bytes 3145728 | tf_op jit(solution)/shard_map/all_to_all | solution.py:433

commit v4 on v3

--- a/solution.py
+++ b/solution.py
@@ -13,6 +13,7 @@
 TILE = 256
 F32 = jnp.float32
 BF16 = jnp.bfloat16
+MESH = pl.DeviceIdType.MESH
 
 
 def coefficients(scales, heights):
@@ -82,36 +83,132 @@
     )(coef)
 
 
-def zonal_forward_kernel(width, control, wide, out, turned):
-    at = pl.program_id(0)
-
-    @pl.when(at == 0)
-    def _():
+def zonal_forward_kernel(count, coef, fields, lines, smooth, wide, turned, made, send, recv, keep):
+    variables, rows, width = fields.shape
+    strip = width // count
+    batch = 3 * TILE
+    me = lax.axis_index("lat")
+    barrier = pltpu.get_barrier_semaphore()
+
+    def greet(other, carry):
+        @pl.when(other != me)
+        def _():
+            pl.semaphore_signal(barrier, inc=1, device_id={"lat": other}, device_id_type=MESH)
+
+        return carry
+
+    lax.fori_loop(0, count, greet, 0)
+    wide_table_kernel(width, coef, wide)
+
+    def turn(variable):
         for part in range(width // TILE):
             cells = slice(part * TILE, (part + 1) * TILE)
-            turned[cells, :] = control[0, :, cells].T
-
-    start = pl.multiple_of(width - at * TILE, TILE)
-    out[...] = jnp.dot(
-        wide[:, pl.ds(start, width)], turned[...], preferred_element_type=F32
-    ).astype(BF16)
-
-
-def zonal_forward(control, wide, variable):
-    _, rows, width = control.shape
-    return pl.pallas_call(
-        functools.partial(zonal_forward_kernel, width),
-        out_shape=jax.ShapeDtypeStruct((width, rows), BF16),
-        grid=(width // TILE,),
+            turned[cells, :] = fields[variable, :, cells].T
+
+    def block(at):
+        start = pl.multiple_of(width - at * TILE, TILE)
+        return jnp.dot(
+            wide[:, pl.ds(start, width)], turned[...], preferred_element_type=F32
+        ).astype(BF16)
+
+    def strip_copy(other):
+        return pltpu.make_async_remote_copy(
+            src_ref=made.at[other],
+            dst_ref=lines.at[me],
+            send_sem=send.at[other],
+            recv_sem=recv.at[me],
+            device_id={"lat": other},
+            device_id_type=MESH,
+        )
+
+    own = pltpu.make_async_copy(made.at[me], lines.at[me], keep)
+    turn(0)
+    pl.semaphore_wait(barrier, count - 1)
+    batches = width // batch
+    each = batch // strip
+
+    def one_batch(step, carry):
+        which = (me // each + batches // 2 + step) % batches
+        product = jnp.concatenate([block(which * 3 + part) for part in range(3)], axis=0)
+        made[pl.ds(which * each, each)] = product.reshape(each, strip, rows)
+
+        def one_strip(at, inner):
+            other = which * each + at
+
+            @pl.when(other != me)
+            def _():
+                strip_copy(other).start()
+
+            @pl.when(other == me)
+            def _():
+                own.start()
+
+            return inner
+
+        return lax.fori_loop(0, each, one_strip, carry)
+
+    lax.fori_loop(0, batches, one_batch, 0)
+
+    for variable in range(1, variables):
+        turn(variable)
+
+        def one_block(at, carry):
+            start = pl.multiple_of(at * TILE, TILE)
+            smooth[variable - 1, pl.ds(start, TILE), :] = block(at)
+            return carry
+
+        lax.fori_loop(0, width // TILE, one_block, 0)
+
+    own.wait()
+
+    def finish(other, carry):
+        @pl.when(other != me)
+        def _():
+            strip_copy(other).wait_send()
+            pltpu.make_async_remote_copy(
+                src_ref=made.at[other],
+                dst_ref=lines.at[other],
+                send_sem=send.at[other],
+                recv_sem=recv.at[other],
+                device_id={"lat": other},
+                device_id_type=MESH,
+            ).wait_recv()
+
+        return carry
+
+    lax.fori_loop(0, count, finish, 0)
+
+
+def zonal_forward(fields, coef, count):
+    variables, rows, width = fields.shape
+    strip = width // count
+    return pl.pallas_call(
+        functools.partial(zonal_forward_kernel, count),
+        out_shape=(
+            jax.ShapeDtypeStruct((count, strip, rows), BF16),
+            jax.ShapeDtypeStruct((variables - 1, width, rows), BF16),
+        ),
         in_specs=[
-            pl.BlockSpec((1, rows, width), lambda at: (variable, 0, 0)),
-            pl.BlockSpec((TILE, 2 * width), lambda at: (0, 0)),
+            pl.BlockSpec(memory_space=pltpu.SMEM),
+            pl.BlockSpec(memory_space=pltpu.VMEM),
         ],
-        out_specs=pl.BlockSpec((TILE, rows), lambda at: (at, 0)),
-        scratch_shapes=[pltpu.VMEM((width, rows), BF16)],
-        compiler_params=params(),
-        cost_estimate=cost(2 * rows * width * width, 10 * rows * width),
-    )(control, wide)
+        out_specs=(
+            pl.BlockSpec(memory_space=pl.ANY),
+            pl.BlockSpec(memory_space=pltpu.VMEM),
+        ),
+        scratch_shapes=[
+            pltpu.VMEM((TILE, 2 * width), BF16),
+            pltpu.VMEM((width, rows), BF16),
+            pltpu.VMEM((count, strip, rows), BF16),
+            pltpu.SemaphoreType.DMA((count,)),
+            pltpu.SemaphoreType.DMA((count,)),
+            pltpu.SemaphoreType.DMA,
+        ],
+        compiler_params=pltpu.CompilerParams(
+            vmem_limit_bytes=48 * 1024 * 1024, collective_id=0, has_side_effects=True
+        ),
+        cost_estimate=cost(2 * variables * rows * width * width, 10 * rows * width),
+    )(coef, fields)
 
 
 def zonal_backward_kernel(width, lines, tall, *rest):
@@ -375,12 +472,8 @@
     reports = report_slot.shape[-1]
 
     zonal = coefficients(zonal_scales, zonal_heights)
-    wide = table(wide_table_kernel, (TILE, 2 * width), width, zonal)
     fields = control.reshape(variables, share * band_rows, width)
-    smooth = [
-        zonal_forward(fields, wide, variable).reshape(lat_count, strip, -1)
-        for variable in range(variables)
-    ]
+    arrived, smooth = zonal_forward(fields, zonal, lat_count)
 
     group = 128 // band_rows
     groups = share // group
@@ -411,13 +504,10 @@
     maps = maps.reshape(variables, owners, levels, groups * kept * group)
     tall = table(tall_table_kernel, (2 * width, TILE), width, zonal)
 
-    last, matrices, ids, numbers, cells, maps, tall = lax.optimization_barrier(
-        (smooth[-1], matrices, ids, numbers, cells, maps, tall)
-    )
-    smooth[-1] = last
-    sent = [
-        lax.all_to_all(part, "lat", split_axis=0, concat_axis=0, tiled=True) for part in smooth
-    ]
+    sent = [arrived]
+    for variable in range(1, variables):
+        part = smooth[variable - 1].reshape(lat_count, strip, -1)
+        sent.append(lax.all_to_all(part, "lat", split_axis=0, concat_axis=0, tiled=True))
 
     departures = []
     lines = []

time: 196 us -> 186 us (0.949)
  waiting for transfers between devices: 62.3 us -> 39.7 us
  Pallas kernels: 93.7 us -> 112 us
  starting transfers between devices: 21.4 us -> 17.6 us
  local copies, waits for them, and re-layouts: 12.2 us -> 10.2 us
    pallas_call x2 -> x1, Pallas kernels: 20 us -> 44.2 us  [zonal_forward(): pl.pallas_call(functools.partial(zonal_forward_kernel, count), out_shape=...]
    all_to_all x2 -> x1, waiting for transfers between devices: 22.3 us -> 2.74 us  [on_device(): lax.all_to_all(part, 'lat', split_axis=0, concat_axis=0, tiled=True)]
    all_to_all x2 -> x1, starting transfers between devices: 12 us -> 7.34 us  [on_device(): lax.all_to_all(part, 'lat', split_axis=0, concat_axis=0, tiled=True)]
    pallas_call x2 -> x1, Pallas kernels: 7.25 us -> 3.64 us  [table(): pl.pallas_call(functools.partial(kernel, width), out_shape=jax.ShapeDtype...]
    all_to_all x2, waiting for transfers between devices: 36.2 us -> 33.2 us  [on_device(): lax.all_to_all(back, 'lat', split_axis=0, concat_axis=0, tiled=True)]
    pallas_call x2, Pallas kernels: 12.6 us -> 10.3 us  [meridional_forward(): pl.pallas_call(meridional_forward_kernel, out_shape=jax.ShapeDtypeStruct(...]
    optimization_barrier x3 -> x0, local copies, waits for them, and re-layouts: 1.99 us -> none  [on_device(): lax.optimization_barrier((smooth[-1], matrices, ids, numbers, cells, maps...]
    unnamed x41 -> x33, local copies, waits for them, and re-layouts: 9.02 us -> 7.12 us
  transfers between devices with their start and end apart: 8 -> 7, of which waited for: 7 -> 6; matrix products, arithmetic and copies ran while one was open for 3% -> 3% of each run, Pallas kernels for 36% -> 31%
where the time goes in v4:
time: 186 us; the launch traced here: 185 us
  Pallas kernels  112 us (60%)
  waiting for transfers between devices  39.7 us (21%)
  starting transfers between devices  17.6 us (9%)
  local copies, waits for them, and re-layouts  10.2 us (5%)
  other arithmetic  2.57 us (1%)
    pallas_call x1, Pallas kernels, zonal_forward(): pl.pallas_call(functools.partial(zonal_forward_kernel, count), out_shape=...  44.2 us
    all_to_all x2, waiting for transfers between devices, on_device(): lax.all_to_all(back, 'lat', split_axis=0, concat_axis=0, tiled=True)  33.2 us
    pallas_call x2, Pallas kernels, at_reports(): pl.pallas_call(functools.partial(reports_kernel, variable, group, kept_ro...  26.9 us
    pallas_call x2, Pallas kernels, zonal_backward(): pl.pallas_call(functools.partial(zonal_backward_kernel, width), out_shape...  20.3 us
    pallas_call x2, Pallas kernels, meridional_forward(): pl.pallas_call(meridional_forward_kernel, out_shape=jax.ShapeDtypeStruct(...  10.3 us
    all_to_all x2, starting transfers between devices, on_device(): lax.all_to_all(back, 'lat', split_axis=0, concat_axis=0, tiled=True)  9.37 us
    all_to_all x1, starting transfers between devices, on_device(): lax.all_to_all(part, 'lat', split_axis=0, concat_axis=0, tiled=True)  7.34 us
    unnamed x33, local copies, waits for them, and re-layouts  7.12 us
  transfers between devices with their start and end apart: 7, of which 6 were waited for; matrix products, arithmetic and copies ran while one was open for 3% of the time, Pallas kernels for 31%

profile of v4, /device:TPU:12, one launch (start us, length us, event | category | flops | bytes accessed | tf_op | source)
XLA Modules:
  0.0 184.8 jit_solution(11190543126814558454)
XLA Ops:
  0.6 0.7 fusion.4
  1.3 0.1 pad_maximum_fusion.coef
  1.4 44.2 %shard_map.140 = (bf16[16,192,256]{2,1,0:T(8,128)(2,1)S(1)}, bf16[1,3072,256]{2,1,0:T(8,128)(2,1)}) custom-call(f32[8]{0:T(128)S(1)} %pad_maximum_fusion.coef, bf16[2,256,3072]{2,1,0:T(8,128)(2,1)} %bitcast.73), custom_call_target="tpu_custom_call" | custom-call | flops 9663676416 | bytes 7864320 | tf_op jit(solution)/shard_map/pallas_call | solution.py:185
  45.6 1.1 copy-done.2
  46.7 7.3 %all-to-all-start = ((bf16[16,192,256]{2,1,0:T(8,128)(2,1)}), bf16[16,192,256]{2,1,0:T(8,128)(2,1)}, u32[]{:S(2)}, u32[]{:S(2)}) async-start(bf16[16,192,256]{2,1,0:T(8,128)(2,1)} %bitcast.2), calls=%async_computation | async-start | bytes 3145728 | tf_op jit(solution)/shard_map/all_to_all | solution.py:510
  54.1 1.8 all-gather
  55.9 0.1 fusion.3
  56.0 0.1 broadcast_select_fusion
  56.1 0.1 iota_add_fusion
  56.1 0.1 add.64
  56.2 0.1 broadcast_in_dim.6
  56.3 0.1 reshape_reshape.3.lanes
  56.4 0.1 pad_maximum_fusion.1.coef
  56.5 1.3 shard_map.141.matrix
  57.8 1.4 copy-done.3
  59.2 4.0 %shard_map.144 = bf16[2,192,512]{2,1,0:T(8,128)(2,1)S(1)} custom-call(bf16[16,192,256]{2,1,0:T(8,128)(2,1)S(1)} %copy-done.3, bf16[8,256,512]{2,1,0:T(8,128)(2,1)S(1)} %shard_map.141.matrix), custom_call_target="tpu_custom_call" | custom-call | flops 805306368 | bytes 1572864 | tf_op jit(solution)/shard_map/pallas_call | solution.py:314
  63.3 0.8 slice_bitcast_fusion
  64.0 0.2 collective-permute-start.1
  64.2 0.1 copy.31
  64.4 0.1 broadcast_in_dim.15
  64.4 0.2 copy.34.maps
  64.7 0.4 copy.33.numbers
  65.1 0.8 and_select_fusion
  66.0 1.3 copy.32.ids
  67.3 1.2 copy-done.4
  68.5 0.9 copy-done.6
  69.5 13.9 %shard_map.145 = (f32[1,2048]{1,0:T(1,128)S(1)}, bf16[2,192,512]{2,1,0:T(8,128)(2,1)S(1)}) custom-call(bf16[192,512]{1,0:T(8,128)(2,1)S(1)} %copy-done.6, bf16[192,512]{1,0:T(8,128)(2,1)} %collective-permute-done.1.other, s32[2048,3]{1,0:T(8,128)S(1)} %copy-done.4, f32[2048,6]{1,0:T(8,128)S(1)} %copy.33.numbers, s32[1,2048]{1,0:T(1,128)S(1)} %get-tuple-element.22.cells, ...), custom_call_target="tpu_custom_call" | custom-call | flops 4294967296 | bytes 1048576 | tf_op jit(solution)/shard_map/pallas_call | solution.py:422
  83.4 0.4 collective-permute-start.3
  83.8 1.1 collective-permute-done.3.other
  84.9 2.6 %shard_map.148 = bf16[16,192,256]{2,1,0:T(8,128)(2,1)S(1)} custom-call(bf16[192,512]{1,0:T(8,128)(2,1)S(1)} %get-tuple-element.15.own, bf16[192,512]{1,0:T(8,128)(2,1)S(1)} %collective-permute-done.3.other, bf16[8,256,512]{2,1,0:T(8,128)(2,1)S(1)} %shard_map.141.matrix), custom_call_target="tpu_custom_call" | custom-call | flops 805306368 | bytes 1572864 | tf_op jit(solution)/shard_map/pallas_call | solution.py:351
  87.6 1.1 copy-done
  88.7 2.7 %all-to-all-done.lines = bf16[16,192,256]{2,1,0:T(8,128)(2,1)} async-done(((bf16[16,192,256]{2,1,0:T(8,128)(2,1)}), bf16[16,192,256]{2,1,0:T(8,128)(2,1)}, u32[]{:S(2)}, u32[]{:S(2)}) %all-to-all-start) | async-done | bytes 1572896 | tf_op jit(solution)/shard_map/all_to_all | solution.py:510
  91.4 4.9 %all-to-all-start.2 = ((bf16[16,192,256]{2,1,0:T(8,128)(2,1)}), bf16[16,192,256]{2,1,0:T(8,128)(2,1)}, u32[]{:S(2)}, u32[]{:S(2)}) async-start(bf16[16,192,256]{2,1,0:T(8,128)(2,1)} %copy-done), calls=%async_computation.2 | async-start | bytes 3145728 | tf_op jit(solution)/shard_map/all_to_all | solution.py:523
  96.3 6.4 %shard_map.142 = bf16[2,192,512]{2,1,0:T(8,128)(2,1)S(1)} custom-call(bf16[16,192,256]{2,1,0:T(8,128)(2,1)} %all-to-all-done.lines, bf16[8,256,512]{2,1,0:T(8,128)(2,1)S(1)} %shard_map.141.matrix), custom_call_target="tpu_custom_call" | custom-call | flops 805306368 | bytes 1572864 | tf_op jit(solution)/shard_map/pallas_call | solution.py:314
  102.7 0.1 collective-permute-start
  102.8 1.4 collective-permute-done.other
  104.2 13.0 %shard_map.143 = (f32[1,2048]{1,0:T(1,128)S(1)}, bf16[2,192,512]{2,1,0:T(8,128)(2,1)S(1)}) custom-call(bf16[192,512]{1,0:T(8,128)(2,1)S(1)} %get-tuple-element.21.own, bf16[192,512]{1,0:T(8,128)(2,1)S(1)} %collective-permute-done.other, s32[2048,3]{1,0:T(8,128)S(1)} %copy-done.5, f32[2048,6]{1,0:T(8,128)S(1)} %copy.33.numbers, ...), custom_call_target="tpu_custom_call" | custom-call | flops 4294967296 | bytes 1048576 | tf_op jit(solution)/shard_map/pallas_call | solution.py:422
  117.3 0.2 collective-permute-start.2
  117.5 1.3 collective-permute-done.2.other
  118.8 2.6 %shard_map.146 = bf16[16,192,256]{2,1,0:T(8,128)(2,1)S(1)} custom-call(bf16[192,512]{1,0:T(8,128)(2,1)S(1)} %get-tuple-element.17.own, bf16[192,512]{1,0:T(8,128)(2,1)S(1)} %collective-permute-done.2.other, bf16[8,256,512]{2,1,0:T(8,128)(2,1)S(1)} %shard_map.141.matrix), custom_call_target="tpu_custom_call" | custom-call | flops 805306368 | bytes 1572864 | tf_op jit(solution)/shard_map/pallas_call | solution.py:351
  121.4 1.1 copy-done.1
  122.6 10.9 %all-to-all-done.2 = bf16[16,192,256]{2,1,0:T(8,128)(2,1)} async-done(((bf16[16,192,256]{2,1,0:T(8,128)(2,1)}), bf16[16,192,256]{2,1,0:T(8,128)(2,1)}, u32[]{:S(2)}, u32[]{:S(2)}) %all-to-all-start.2) | async-done | bytes 1572896 | tf_op jit(solution)/shard_map/all_to_all | solution.py:523
  133.5 4.5 %all-to-all-start.1 = ((bf16[16,192,256]{2,1,0:T(8,128)(2,1)}), bf16[16,192,256]{2,1,0:T(8,128)(2,1)}, u32[]{:S(2)}, u32[]{:S(2)}) async-start(bf16[16,192,256]{2,1,0:T(8,128)(2,1)} %copy-done.1), calls=%async_computation.1 | async-start | bytes 3145728 | tf_op jit(solution)/shard_map/all_to_all | solution.py:523
  138.0 3.6 %shard_map.147.tall = bf16[6144,256]{1,0:T(8,128)(2,1)S(1)} custom-call(f32[8]{0:T(128)S(1)} %pad_maximum_fusion.coef), custom_call_target="tpu_custom_call" | custom-call | flops 47185920 | bytes 3145728 | tf_op jit(solution)/shard_map/pallas_call | solution.py:76
  141.6 0.6 fusion.2
  142.2 10.2 %shard_map.149.rest_0_ = f32[2,256,3072]{2,1,0:T(8,128)} custom-call(bf16[3072,256]{1,0:T(8,128)(2,1)} %bitcast.29.lines, bf16[6144,256]{1,0:T(8,128)(2,1)S(1)} %shard_map.147.tall), custom_call_target="tpu_custom_call" | custom-call | flops 4831838208 | bytes 9437184 | tf_op jit(solution)/shard_map/pallas_call | solution.py:240
  152.4 22.3 %all-to-all-done.1 = bf16[16,192,256]{2,1,0:T(8,128)(2,1)} async-done(((bf16[16,192,256]{2,1,0:T(8,128)(2,1)}), bf16[16,192,256]{2,1,0:T(8,128)(2,1)}, u32[]{:S(2)}, u32[]{:S(2)}) %all-to-all-start.1) | async-done | bytes 1572896 | tf_op jit(solution)/shard_map/all_to_all | solution.py:523
  174.7 10.2 %shard_map.150 = f32[2,256,3072]{2,1,0:T(8,128)} custom-call(bf16[3072,256]{1,0:T(8,128)(2,1)} %bitcast.26.lines, bf16[6144,256]{1,0:T(8,128)(2,1)S(1)} %shard_map.147.tall, f32[2,256,3072]{2,1,0:T(8,128)} %shard_map.149.rest_0_), custom_call_target="tpu_custom_call", output_to_operand_aliasing={{}: (2, {})} | custom-call | flops 4831838208 | bytes 9437184 | tf_op jit(solution)/shard_map/pallas_call | solution.py:240
  (37 shorter events, 0.3 us)
Async XLA Ops:
  45.6 1.1 copy-start.2
  46.7 7.4 %copy-start.13 = (s32[1,1,2,2]{3,2,1,0:T(2,128)S(1)}, s32[1,1,2,2]{3,2,1,0:T(2,128)}, u32[]{:S(2)}) copy-start(s32[1,1,2,2]{3,2,1,0:T(2,128)} %param.19) | copy-start | bytes 52
  46.7 9.6 %copy-start.14 = (f32[4]{0:T(128)S(1)}, f32[4]{0:T(128)}, u32[]{:S(2)}) copy-start(f32[4]{0:T(128)} %param.16) | copy-start | bytes 52
  46.7 9.7 %copy-start.15 = (f32[4]{0:T(128)S(1)}, f32[4]{0:T(128)}, u32[]{:S(2)}) copy-start(f32[4]{0:T(128)} %param.17) | copy-start | bytes 52
  46.7 44.7 %all-to-all-start = ((bf16[16,192,256]{2,1,0:T(8,128)(2,1)}), bf16[16,192,256]{2,1,0:T(8,128)(2,1)}, u32[]{:S(2)}, u32[]{:S(2)}) async-start(bf16[16,192,256]{2,1,0:T(8,128)(2,1)} %bitcast.2), calls=%async_computation | async-start | bytes 3145728 | tf_op jit(solution)/shard_map/all_to_all | solution.py:510
  57.8 1.4 copy-start.3
  59.2 5.0 %copy-start.8 = (bf16[2,64,64]{2,1,0:T(8,128)(2,1)S(1)}, bf16[2,64,64]{2,1,0:T(8,128)(2,1)}, u32[]{:S(2)}) copy-start(bf16[2,64,64]{2,1,0:T(8,128)(2,1)} %param.18) | copy-start | bytes 49156
  63.2 1.4 copy-start.7
  63.2 1.4 copy-start.10
  63.3 1.4 copy-start.11
  63.3 1.8 copy-start.12
  64.0 1.9 %copy-start.9 = (s32[1,1,2048]{2,1,0:T(1,128)S(1)}, s32[1,1,2048]{2,1,0:T(1,128)}, u32[]{:S(2)}) copy-start(s32[1,1,2048]{2,1,0:T(1,128)} %param.21) | copy-start | bytes 24580
  64.0 3.3 %collective-permute-start.1 = (bf16[192,512]{1,0:T(8,128)(2,1)}, bf16[192,512]{1,0:T(8,128)(2,1)}, u32[]{:S(2)}, u32[]{:S(2)}) collective-permute-start(bf16[192,512]{1,0:T(8,128)(2,1)} %get-tuple-element.18), channel_id=1, source_target_pairs={{0,1},{1,0},{2,3},{3,2},{4,5},{5,4},{6,7},{7,6},{8,9},{9,8},{10,11... | collective-permute-start | bytes 589832 | tf_op jit(solution)/shard_map/ppermute | solution.py:516
  67.3 1.2 copy-start.4
  68.5 0.9 copy-start.6
  83.4 1.5 collective-permute-start.3
  87.6 1.1 copy-start
  91.4 42.0 %all-to-all-start.2 = ((bf16[16,192,256]{2,1,0:T(8,128)(2,1)}), bf16[16,192,256]{2,1,0:T(8,128)(2,1)}, u32[]{:S(2)}, u32[]{:S(2)}) async-start(bf16[16,192,256]{2,1,0:T(8,128)(2,1)} %copy-done), calls=%async_computation.2 | async-start | bytes 3145728 | tf_op jit(solution)/shard_map/all_to_all | solution.py:523
  96.3 7.9 %copy-start.5 = (s32[2048,3]{1,0:T(8,128)S(1)}, s32[2048,3]{1,0:T(8,128)}, u32[]{:S(2)}) copy-start(s32[2048,3]{1,0:T(8,128)} %copy.32.ids) | copy-start | bytes 73732
  102.7 1.5 collective-permute-start
  117.3 1.5 collective-permute-start.2
  121.4 1.2 copy-start.1
  133.5 41.2 %all-to-all-start.1 = ((bf16[16,192,256]{2,1,0:T(8,128)(2,1)}), bf16[16,192,256]{2,1,0:T(8,128)(2,1)}, u32[]{:S(2)}, u32[]{:S(2)}) async-start(bf16[16,192,256]{2,1,0:T(8,128)(2,1)} %copy-done.1), calls=%async_computation.1 | async-start | bytes 3145728 | tf_op jit(solution)/shard_map/all_to_all | solution.py:523

commit v5 on v4

--- a/solution.py
+++ b/solution.py
@@ -281,168 +281,226 @@
     )(coef, lanes)
 
 
-def meridional_forward_kernel(lines, matrix, out, total):
-    at = pl.program_id(0)
-    groups, strip, columns = total.shape
-    part = lines.shape[2] // groups
-    owners, share = out.shape[0], columns // out.shape[0]
-    for group in range(groups):
-        cells = slice(group * part, (group + 1) * part)
-        both = jnp.concatenate([lines[0, :, cells], lines[1, :, cells]], axis=1)
-        product = jnp.dot(both, matrix[0], preferred_element_type=F32)
-
-        @pl.when(at == 0)
-        def _():
-            total[group] = product
-
-        @pl.when(at > 0)
-        def _():
-            total[group] += product
-
-    @pl.when(at == pl.num_programs(0) - 1)
-    def _():
-        for owner in range(owners):
-            for group in range(groups):
-                out[owner, :, group * share : (group + 1) * share] = total[
-                    group, :, owner * share : (owner + 1) * share
-                ].astype(BF16)
-
-
-def meridional_forward(lines, matrices, owners, groups):
-    bands, strip, rows = lines.shape
-    pairs, depth, columns = matrices.shape
-    return pl.pallas_call(
-        meridional_forward_kernel,
-        out_shape=jax.ShapeDtypeStruct((owners, strip, groups * columns // owners), BF16),
-        grid=(pairs,),
-        in_specs=[
-            pl.BlockSpec((2, strip, rows), lambda at: (at, 0, 0)),
-            pl.BlockSpec((1, depth, columns), lambda at: (at, 0, 0)),
-        ],
-        out_specs=pl.BlockSpec(
-            (owners, strip, groups * columns // owners), lambda at: (0, 0, 0)
-        ),
-        scratch_shapes=[pltpu.VMEM((groups, strip, columns), F32)],
-        compiler_params=params(),
-        cost_estimate=cost(2 * bands * strip * rows * columns, 2 * bands * strip * rows),
-    )(lines, matrices)
-
-
-def meridional_backward_kernel(groups, own, other, matrix, out):
-    share = own.shape[1] // groups
-    part = out.shape[2] // groups
-    for group in range(groups):
-        cells = slice(group * share, (group + 1) * share)
-        both = jnp.concatenate([own[:, cells], other[:, cells]], axis=1)
-        product = lax.dot_general(
-            both, matrix[0], (((1,), (1,)), ((), ())), preferred_element_type=F32
-        ).astype(BF16)
-        for band in range(2):
-            out[band, :, group * part : (group + 1) * part] = product[
-                :, band * part : (band + 1) * part
-            ]
-
-
-def meridional_backward(own, other, matrices, groups):
-    pairs, depth, columns = matrices.shape
-    strip, share = own.shape
-    rows = depth * groups // 2
-    half = pl.BlockSpec((strip, share), lambda at: (0, 0))
-    return pl.pallas_call(
-        functools.partial(meridional_backward_kernel, groups),
-        out_shape=jax.ShapeDtypeStruct((2 * pairs, strip, rows), BF16),
-        grid=(pairs,),
-        in_specs=[half, half, pl.BlockSpec((1, depth, columns), lambda at: (at, 0, 0))],
-        out_specs=pl.BlockSpec((2, strip, rows), lambda at: (at, 0, 0)),
-        compiler_params=params(),
-        cost_estimate=cost(4 * pairs * strip * rows * columns, 4 * pairs * strip * rows),
-    )(own, other, matrices)
-
-
-def reports_kernel(variable, group, kept_rows, own, other, ids, numbers, cells, weights, maps, departure, lifted, total):
-    at = pl.program_id(0)
-    strip, columns = own.shape
-    block = ids.shape[0]
-    levels = maps.shape[2]
-    across = lax.broadcasted_iota(jnp.int32, (block, strip), 1)
-    cell = ids[:, 0:1]
-    down = lax.broadcasted_iota(jnp.int32, (strip, block), 0)
-    place = cells[...]
-    sides = []
-    turned = []
-    for side in range(2):
-        value = jnp.where(across == cell, numbers[:, 2 * side : 2 * side + 1], 0.0)
-        value = jnp.where(across == cell + 1, numbers[:, 2 * side + 1 : 2 * side + 2], value)
-        sides.append(value.astype(BF16))
-        value = jnp.where(down == place, weights[2 * side : 2 * side + 1, :], 0.0)
-        value = jnp.where(down == place + 1, weights[2 * side + 1 : 2 * side + 2, :], value)
-        turned.append(value.astype(BF16))
-    level = ids[:, 2:3] - variable * levels
-    chosen = jnp.where(lax.broadcasted_iota(jnp.int32, (block, levels), 1) == level, 1.0, 0.0)
-    chosen = chosen.astype(BF16)
-    lane = lax.broadcasted_iota(jnp.int32, (block, columns), 1) // group % kept_rows
-    hits = [lane == ids[:, 1:2], lane == ids[:, 1:2] + 1]
-    fields = (own, other)
-    model = jnp.zeros((block, 1), F32)
-    kept = []
-    for half in range(2):
-        mapped = jnp.dot(chosen, maps[0, half], preferred_element_type=F32)
-        found = jnp.zeros((block, columns), F32)
-        for side in range(2):
-            picked = jnp.where(hits[side], mapped, 0.0)
-            kept.append(picked)
-            values = jnp.dot(sides[side], fields[half][...], preferred_element_type=F32)
-            found = found + values * picked
-        model = model + jnp.sum(found, axis=1, keepdims=True)
-    result = numbers[:, 5:6] * (model - numbers[:, 4:5])
-    both = jnp.concatenate(turned, axis=1)
-    departure[...] = jnp.broadcast_to(result, (block, 128)).T[0:1, :]
-    for half in range(2):
-        pushes = [(kept[2 * half + side] * result).astype(BF16) for side in range(2)]
-        product = jnp.dot(both, jnp.concatenate(pushes, axis=0), preferred_element_type=F32)
-
-        @pl.when(at == 0)
-        def _():
-            total[half] = product
-
-        @pl.when(at > 0)
-        def _():
-            total[half] += product
-
-    @pl.when(at == pl.num_programs(0) - 1)
-    def _():
-        lifted[...] = total[...].astype(BF16)
-
-
-def at_reports(variable, group, kept_rows, own, other, ids, numbers, cells, weights, maps):
-    strip, columns = own.shape
+def middle_kernel(
+    variable,
+    group,
+    kept_rows,
+    parcels,
+    lines,
+    matrices,
+    ids,
+    numbers,
+    cells,
+    weights,
+    maps,
+    landed,
+    back,
+    departure,
+    mixing,
+    mixed,
+    mixed_other,
+    total,
+    lifted,
+    lifted_other,
+    send,
+    recv,
+    keep,
+    pair_send,
+    pair_recv,
+):
+    count, strip, depth = lines.shape
+    groups = mixing.shape[0]
+    part = depth // groups
+    columns = mixed.shape[2]
+    share = columns // groups
+    levels = maps.shape[1]
     reports = ids.shape[0]
     block = math.gcd(reports, 256)
-    half = pl.BlockSpec((strip, columns), lambda at: (0, 0))
+    me = lax.axis_index("lat")
+    twin = 1 - lax.axis_index("obs")
+    barrier = pltpu.get_barrier_semaphore()
+    pl.semaphore_signal(barrier, inc=1, device_id={"obs": twin}, device_id_type=MESH)
+
+    def greet(other, carry):
+        @pl.when(other != me)
+        def _():
+            pl.semaphore_signal(barrier, inc=1, device_id={"lat": other}, device_id_type=MESH)
+
+        return carry
+
+    lax.fori_loop(0, count, greet, 0)
+    own = pltpu.make_async_copy(parcels.at[me], landed.at[me], keep)
+    own.start()
+    mixing[...] = jnp.zeros_like(mixing)
+    total[...] = jnp.zeros_like(total)
+    pl.semaphore_wait(barrier, count)
+
+    def parcel(other, slot):
+        return pltpu.make_async_remote_copy(
+            src_ref=parcels.at[other],
+            dst_ref=landed.at[slot],
+            send_sem=send.at[other],
+            recv_sem=recv.at[slot],
+            device_id={"lat": other},
+            device_id_type=MESH,
+        )
+
+    def begin(step, carry):
+        other = (me + count // 2 + step) % count
+
+        @pl.when(other != me)
+        def _():
+            parcel(other, me).start()
+
+        return carry
+
+    lax.fori_loop(0, count, begin, 0)
+
+    def mix(pair, carry):
+        for at in range(groups):
+            lane = slice(at * part, (at + 1) * part)
+            both = jnp.concatenate([lines[2 * pair, :, lane], lines[2 * pair + 1, :, lane]], axis=1)
+            mixing[at] += jnp.dot(both, matrices[pair], preferred_element_type=F32)
+        return carry
+
+    lax.fori_loop(0, count // 2, mix, 0)
+    for owner in (1, 0):
+        for at in range(groups):
+            mixed[owner, :, at * share : (at + 1) * share] = mixing[
+                at, :, owner * share : (owner + 1) * share
+            ].astype(BF16)
+    trade = pltpu.make_async_remote_copy(
+        src_ref=mixed.at[1],
+        dst_ref=mixed_other,
+        send_sem=pair_send.at[0],
+        recv_sem=pair_recv.at[0],
+        device_id={"obs": twin},
+        device_id_type=MESH,
+    )
+    trade.start()
+    trade.wait()
+
+    def observe(at, carry):
+        start = pl.multiple_of(at * block, block)
+        here = pl.ds(start, block)
+        across = lax.broadcasted_iota(jnp.int32, (block, strip), 1)
+        down = lax.broadcasted_iota(jnp.int32, (strip, block), 0)
+        cell = ids[here, 0:1]
+        row = ids[here, 1:2]
+        place = cells[0:1, here]
+        sides = []
+        turned = []
+        for side in range(2):
+            low, high = 2 * side, 2 * side + 1
+            value = jnp.where(across == cell, numbers[here, low : low + 1], 0.0)
+            value = jnp.where(across == cell + 1, numbers[here, high : high + 1], value)
+            sides.append(value.astype(BF16))
+            value = jnp.where(down == place, weights[low : low + 1, here], 0.0)
+            value = jnp.where(down == place + 1, weights[high : high + 1, here], value)
+            turned.append(value.astype(BF16))
+        both = jnp.concatenate(turned, axis=1)
+        level = ids[here, 2:3] - variable * levels
+        chosen = jnp.where(lax.broadcasted_iota(jnp.int32, (block, levels), 1) == level, 1.0, 0.0)
+        chosen = chosen.astype(BF16)
+        lane = lax.broadcasted_iota(jnp.int32, (block, columns), 1) // group % kept_rows
+        hits = [lane == row, lane == row + 1]
+        model = jnp.zeros((block, 1), F32)
+        kept = []
+        for half in range(2):
+            field = mixed[0] if half == 0 else mixed_other[...]
+            mapped = jnp.dot(chosen, maps[half], preferred_element_type=F32)
+            found = jnp.zeros((block, columns), F32)
+            for side in range(2):
+                picked = jnp.where(hits[side], mapped, 0.0)
+                kept.append(picked)
+                values = jnp.dot(sides[side], field, preferred_element_type=F32)
+                found = found + values * picked
+            model = model + jnp.sum(found, axis=1, keepdims=True)
+        result = numbers[here, 5:6] * (model - numbers[here, 4:5])
+        departure[0:1, here] = jnp.broadcast_to(result, (block, 128)).T[0:1, :]
+        for half in range(2):
+            pushes = [(kept[2 * half + side] * result).astype(BF16) for side in range(2)]
+            total[half] += jnp.dot(
+                both, jnp.concatenate(pushes, axis=0), preferred_element_type=F32
+            )
+        return carry
+
+    lax.fori_loop(0, reports // block, observe, 0)
+    lifted[...] = total[...].astype(BF16)
+    trade = pltpu.make_async_remote_copy(
+        src_ref=lifted.at[1],
+        dst_ref=lifted_other,
+        send_sem=pair_send.at[1],
+        recv_sem=pair_recv.at[1],
+        device_id={"obs": twin},
+        device_id_type=MESH,
+    )
+    trade.start()
+    trade.wait()
+
+    def unmix(pair, carry):
+        for at in range(groups):
+            lane = slice(at * share, (at + 1) * share)
+            both = jnp.concatenate([lifted[0, :, lane], lifted_other[:, lane]], axis=1)
+            product = lax.dot_general(
+                both, matrices[pair], (((1,), (1,)), ((), ())), preferred_element_type=F32
+            ).astype(BF16)
+            for band in range(2):
+                back[2 * pair + band, :, at * part : (at + 1) * part] = product[
+                    :, band * part : (band + 1) * part
+                ]
+        return carry
+
+    lax.fori_loop(0, count // 2, unmix, 0)
+    own.wait()
+
+    def finish(other, carry):
+        @pl.when(other != me)
+        def _():
+            parcel(other, me).wait_send()
+            parcel(other, other).wait_recv()
+
+        return carry
+
+    lax.fori_loop(0, count, finish, 0)
+
+
+def middle(variable, group, kept_rows, parcels, lines, matrices, ids, numbers, cells, weights, maps):
+    count, strip, depth = lines.shape
+    columns = matrices.shape[2]
+    groups = maps.shape[2] // columns * 2
+    reports = ids.shape[0]
+    width = maps.shape[2]
+    vmem = pl.BlockSpec(memory_space=pltpu.VMEM)
     return pl.pallas_call(
-        functools.partial(reports_kernel, variable, group, kept_rows),
+        functools.partial(middle_kernel, variable, group, kept_rows),
         out_shape=(
+            jax.ShapeDtypeStruct(lines.shape, BF16),
+            jax.ShapeDtypeStruct(lines.shape, BF16),
             jax.ShapeDtypeStruct((1, reports), F32),
-            jax.ShapeDtypeStruct((2, strip, columns), BF16),
         ),
-        grid=(reports // block,),
-        in_specs=[
-            half,
-            half,
-            pl.BlockSpec((block, ids.shape[1]), lambda at: (at, 0)),
-            pl.BlockSpec((block, numbers.shape[1]), lambda at: (at, 0)),
-            pl.BlockSpec((1, block), lambda at: (0, at)),
-            pl.BlockSpec((4, block), lambda at: (0, at)),
-            pl.BlockSpec((1,) + maps.shape[1:], lambda at: (variable, 0, 0, 0)),
+        in_specs=[pl.BlockSpec(memory_space=pl.ANY)] + [vmem] * 7,
+        out_specs=(pl.BlockSpec(memory_space=pl.ANY), vmem, vmem),
+        scratch_shapes=[
+            pltpu.VMEM((groups, strip, columns), F32),
+            pltpu.VMEM((2, strip, width), BF16),
+            pltpu.VMEM((strip, width), BF16),
+            pltpu.VMEM((2, strip, width), F32),
+            pltpu.VMEM((2, strip, width), BF16),
+            pltpu.VMEM((strip, width), BF16),
+            pltpu.SemaphoreType.DMA((count,)),
+            pltpu.SemaphoreType.DMA((count,)),
+            pltpu.SemaphoreType.DMA,
+            pltpu.SemaphoreType.DMA((2,)),
+            pltpu.SemaphoreType.DMA((2,)),
         ],
-        out_specs=(
-            pl.BlockSpec((1, block), lambda at: (0, at)),
-            pl.BlockSpec((2, strip, columns), lambda at: (0, 0, 0)),
+        compiler_params=pltpu.CompilerParams(
+            vmem_limit_bytes=48 * 1024 * 1024,
+            collective_id=1 + variable,
+            has_side_effects=True,
         ),
-        scratch_shapes=[pltpu.VMEM((2, strip, columns), F32)],
-        compiler_params=params(),
-        cost_estimate=cost(16 * reports * 256 * columns, 4 * reports * 128),
-    )(own, other, ids, numbers, cells, weights, maps)
+        cost_estimate=cost(20 * reports * 256 * width, 8 * count * strip * depth),
+    )(parcels, lines, matrices, ids, numbers, cells, weights, maps)
 
 
 def on_device(
@@ -478,7 +536,6 @@
     group = 128 // band_rows
     groups = share // group
     me = lax.axis_index("obs")
-    partner = [(0, 1), (1, 0)]
     blocks = lax.all_gather(send_blocks.reshape(owners, SLOTS), "obs", axis=0)
     source = jnp.arange(owners)[:, None, None]
     starts = jnp.transpose(source * (all_rows // owners) + blocks * BR, (1, 0, 2))
@@ -504,23 +561,31 @@
     maps = maps.reshape(variables, owners, levels, groups * kept * group)
     tall = table(tall_table_kernel, (2 * width, TILE), width, zonal)
 
-    sent = [arrived]
-    for variable in range(1, variables):
-        part = smooth[variable - 1].reshape(lat_count, strip, -1)
-        sent.append(lax.all_to_all(part, "lat", split_axis=0, concat_axis=0, tiled=True))
-
+    parcels = [
+        smooth[variable].reshape(lat_count, strip, -1) for variable in range(variables - 1)
+    ]
+    landed = [arrived]
     departures = []
-    lines = []
     for variable in range(variables):
-        mixed = meridional_forward(sent[variable], matrices, owners, groups)
-        theirs = lax.ppermute(mixed[1], "obs", partner)
-        departure, lifted = at_reports(
-            variable, group, kept, mixed[0], theirs, ids, numbers, cells, weight, maps
+        there, back, departure = middle(
+            variable,
+            group,
+            kept,
+            parcels[variable],
+            landed[variable],
+            matrices,
+            ids,
+            numbers,
+            cells,
+            weight,
+            maps[variable],
         )
+        parcels.append(back)
+        landed.append(there)
         departures.append(departure)
-        theirs = lax.ppermute(lifted[1], "obs", partner)
-        back = meridional_backward(lifted[0], theirs, matrices, groups)
-        lines.append(lax.all_to_all(back, "lat", split_axis=0, concat_axis=0, tiled=True))
+    lines = landed[variables:]
+    for part in parcels[variables:]:
+        lines.append(lax.all_to_all(part, "lat", split_axis=0, concat_axis=0, tiled=True))
 
     gradient = None
     for variable in range(variables):

time: 186 us -> 196 us (1.054)
  Pallas kernels: 112 us -> 150 us
  waiting for transfers between devices: 39.7 us -> 23.4 us
  starting transfers between devices: 17.6 us -> 7.86 us
    pallas_call x6 -> x2, Pallas kernels: 42.5 us -> 82.5 us  [middle(): pl.pallas_call(functools.partial(middle_kernel, variable, group, kept_row...]
    all_to_all x2 -> x0, waiting for transfers between devices: 33.2 us -> none  [on_device(): lax.all_to_all(back, 'lat', split_axis=0, concat_axis=0, tiled=True)]
    all_to_all x1, waiting for transfers between devices: 2.74 us -> 23.4 us  [on_device(): lax.all_to_all(part, 'lat', split_axis=0, concat_axis=0, tiled=True)]
    all_to_all x2 -> x0, starting transfers between devices: 9.37 us -> none  [on_device(): lax.all_to_all(back, 'lat', split_axis=0, concat_axis=0, tiled=True)]
    ppermute x4 -> x0, waiting for transfers between devices: 3.84 us -> none  [the longest x2 2.41 us: on_device(): theirs = lax.ppermute(lifted[1], 'obs', partner)]
  transfers between devices with their start and end apart: 7 -> 1, of which waited for: 6 -> 1; matrix products, arithmetic and copies ran while one was open for 3% -> 0% of each run, Pallas kernels for 31% -> 6%
where the time goes in v5:
time: 196 us
  Pallas kernels  150 us (77%)
  waiting for transfers between devices  23.4 us (12%)
  local copies, waits for them, and re-layouts  9.28 us (5%)
  starting transfers between devices  7.86 us (4%)
  blocking collectives  2.13 us (1%)
    pallas_call x2, Pallas kernels, middle(): pl.pallas_call(functools.partial(middle_kernel, variable, group, kept_row...  82.5 us
    pallas_call x1, Pallas kernels, zonal_forward(): pl.pallas_call(functools.partial(zonal_forward_kernel, count), out_shape=...  44.1 us
    all_to_all x1, waiting for transfers between devices, on_device(): lax.all_to_all(part, 'lat', split_axis=0, concat_axis=0, tiled=True)  23.4 us
    pallas_call x2, Pallas kernels, zonal_backward(): pl.pallas_call(functools.partial(zonal_backward_kernel, width), out_shape...  18.9 us
    unnamed x33, local copies, waits for them, and re-layouts  7.96 us
    all_to_all x1, starting transfers between devices, on_device(): lax.all_to_all(part, 'lat', split_axis=0, concat_axis=0, tiled=True)  7.86 us
  transfers between devices with their start and end apart: 1, of which 1 were waited for; matrix products, arithmetic and copies ran while one was open for 0% of the time, Pallas kernels for 6%

profile of v5, /device:TPU:12, one launch (start us, length us, event | category | flops | bytes accessed | tf_op | source)
XLA Modules:
  0.0 196.0 jit_solution(15101640196870007551)
XLA Ops:
  0.6 0.0 copy-start.9
  0.6 0.0 copy-start.10
  0.7 0.0 copy-start.1
  0.7 0.0 copy-start.11
  0.7 0.0 copy-start.8
  0.7 2.1 %all-gather = s32[2,1,2,2]{3,2,1,0:T(2,128)S(1)} all-gather(s32[1,1,2,2]{3,2,1,0:T(2,128)} %param.19), channel_id=2, replica_groups=mesh['lat'=16,'obs'=2] {'obs'}, dimensions={0}, use_global_device_ids=true | all-gather | bytes 48 | tf_op jit(solution)/shard_map/all_gather | solution.py:539
  2.8 0.1 fusion.2
  2.9 0.1 broadcast_select_fusion
  3.0 0.1 iota_add_fusion
  3.1 0.1 add.64
  3.2 0.1 broadcast_in_dim.17
  3.2 0.1 reshape_reshape.3.lanes
  3.3 0.9 copy.32
  4.3 0.1 copy.38.maps
  4.4 0.0 copy-start.12
  4.4 0.0 copy-start.13
  4.4 0.0 copy-start.14
  4.4 0.0 copy-start.15
  4.5 0.1 copy.35.maps
  4.6 0.0 copy-done.9
  4.6 0.0 copy-done.10
  4.6 0.0 copy-done.1
  4.7 0.4 copy.34.numbers
  5.1 0.0 copy-done.11
  5.1 0.8 and_select_fusion
  5.9 0.0 copy-done.8
  5.9 0.4 copy.33.ids
  6.3 0.1 pad_maximum_fusion.coef
  6.4 0.1 pad_maximum_fusion.1.coef
  6.5 1.4 shard_map.141.matrices
  7.9 0.0 copy-start
  7.9 1.3 copy-done
  9.2 44.1 %shard_map.140 = (bf16[16,192,256]{2,1,0:T(8,128)(2,1)S(1)}, bf16[1,3072,256]{2,1,0:T(8,128)(2,1)S(1)}) custom-call(f32[8]{0:T(128)S(1)} %pad_maximum_fusion.coef, bf16[2,256,3072]{2,1,0:T(8,128)(2,1)} %bitcast.63), custom_call_target="tpu_custom_call" | custom-call | flops 9663676416 | bytes 7864320 | tf_op jit(solution)/shard_map/pallas_call | solution.py:185
  53.3 1.1 copy-done.4
  54.5 1.1 copy-done.7
  55.6 40.9 %shard_map.142 = (bf16[16,192,256]{2,1,0:T(8,128)(2,1)S(1)}, bf16[16,192,256]{2,1,0:T(8,128)(2,1)S(1)}, f32[1,2048]{1,0:T(1,128)S(1)}) custom-call(bf16[16,192,256]{2,1,0:T(8,128)(2,1)} %bitcast.56, bf16[16,192,256]{2,1,0:T(8,128)(2,1)} %copy-done.7, bf16[8,256,512]{2,1,0:T(8,128)(2,1)} %copy-done, s32[2048,3]{1,0:T(8,128)S(1)} %copy.33.ids, ...), custom_call_target="tpu_custom_call" | custom-call | flops 5368709120 | bytes 6291456 | tf_op jit(solution)/shard_map/pallas_call | solution.py:475
  96.6 1.2 copy-done.5
  97.7 1.1 copy-done.6
  98.9 41.5 %shard_map.143 = (bf16[16,192,256]{2,1,0:T(8,128)(2,1)S(1)}, bf16[16,192,256]{2,1,0:T(8,128)(2,1)}, f32[1,2048]{1,0:T(1,128)S(1)}) custom-call(bf16[16,192,256]{2,1,0:T(8,128)(2,1)} %copy-done.6, bf16[16,192,256]{2,1,0:T(8,128)(2,1)} %copy-done.5, bf16[8,256,512]{2,1,0:T(8,128)(2,1)} %copy-done, s32[2048,3]{1,0:T(8,128)S(1)} %copy.33.ids, ...), custom_call_target="tpu_custom_call" | custom-call | flops 5368709120 | bytes 6291456 | tf_op jit(solution)/shard_map/pallas_call | solution.py:475
  140.4 0.0 copy-start.2
  140.4 1.1 copy-done.2
  141.6 7.9 %all-to-all-start = ((bf16[16,192,256]{2,1,0:T(8,128)(2,1)}), bf16[16,192,256]{2,1,0:T(8,128)(2,1)}, u32[]{:S(2)}, u32[]{:S(2)}) async-start(bf16[16,192,256]{2,1,0:T(8,128)(2,1)} %get-tuple-element.16), calls=%async_computation | async-start | bytes 3145728 | tf_op jit(solution)/shard_map/all_to_all | solution.py:588
  149.4 3.6 %shard_map.144.tall = bf16[6144,256]{1,0:T(8,128)(2,1)S(1)} custom-call(f32[8]{0:T(128)S(1)} %pad_maximum_fusion.coef), custom_call_target="tpu_custom_call" | custom-call | flops 47185920 | bytes 3145728 | tf_op jit(solution)/shard_map/pallas_call | solution.py:76
  153.1 0.6 fusion.1
  153.7 0.0 copy-done.3
  153.7 8.7 %shard_map.145.rest_0_ = f32[2,256,3072]{2,1,0:T(8,128)} custom-call(bf16[3072,256]{1,0:T(8,128)(2,1)S(1)} %bitcast.55, bf16[6144,256]{1,0:T(8,128)(2,1)S(1)} %shard_map.144.tall), custom_call_target="tpu_custom_call" | custom-call | flops 4831838208 | bytes 9437184 | tf_op jit(solution)/shard_map/pallas_call | solution.py:240
  162.4 23.4 %all-to-all-done = bf16[16,192,256]{2,1,0:T(8,128)(2,1)} async-done(((bf16[16,192,256]{2,1,0:T(8,128)(2,1)}), bf16[16,192,256]{2,1,0:T(8,128)(2,1)}, u32[]{:S(2)}, u32[]{:S(2)}) %all-to-all-start) | async-done | bytes 1572896 | tf_op jit(solution)/shard_map/all_to_all | solution.py:588
  185.8 10.2 %shard_map.146 = f32[2,256,3072]{2,1,0:T(8,128)} custom-call(bf16[3072,256]{1,0:T(8,128)(2,1)} %bitcast.22.lines, bf16[6144,256]{1,0:T(8,128)(2,1)S(1)} %shard_map.144.tall, f32[2,256,3072]{2,1,0:T(8,128)} %shard_map.145.rest_0_), custom_call_target="tpu_custom_call", output_to_operand_aliasing={{}: (2, {})} | custom-call | flops 4831838208 | bytes 9437184 | tf_op jit(solution)/shard_map/pallas_call | solution.py:240
  (20 shorter events, 0.2 us)
Async XLA Ops:
  0.6 4.0 %copy-start.9 = (f32[1,1,2048]{2,1,0:T(1,128)S(1)}, f32[1,1,2048]{2,1,0:T(1,128)}, u32[]{:S(2)}) copy-start(f32[1,1,2048]{2,1,0:T(1,128)} %param.25) | copy-start | bytes 24580
  0.6 4.0 %copy-start.10 = (f32[1,1,2048]{2,1,0:T(1,128)S(1)}, f32[1,1,2048]{2,1,0:T(1,128)}, u32[]{:S(2)}) copy-start(f32[1,1,2048]{2,1,0:T(1,128)} %param.24) | copy-start | bytes 24580
  0.7 4.0 %copy-start.1 = (f32[1,1,4,2048]{3,2,1,0:T(4,128)S(1)}, f32[1,1,4,2048]{3,2,1,0:T(4,128)}, u32[]{:S(2)}) copy-start(f32[1,1,4,2048]{3,2,1,0:T(4,128)} %param.23) | copy-start | bytes 98308
  0.7 4.4 %copy-start.11 = (s32[1,1,2048]{2,1,0:T(1,128)S(1)}, s32[1,1,2048]{2,1,0:T(1,128)}, u32[]{:S(2)}) copy-start(s32[1,1,2048]{2,1,0:T(1,128)} %param.20) | copy-start | bytes 24580
  0.7 5.2 %copy-start.8 = (s32[1,1,2048]{2,1,0:T(1,128)S(1)}, s32[1,1,2048]{2,1,0:T(1,128)}, u32[]{:S(2)}) copy-start(s32[1,1,2048]{2,1,0:T(1,128)} %param.21) | copy-start | bytes 24580
  4.4 1.9 copy-start.12
  4.4 1.9 copy-start.13
  4.4 2.0 %copy-start.14 = (f32[4]{0:T(128)S(1)}, f32[4]{0:T(128)}, u32[]{:S(2)}) copy-start(f32[4]{0:T(128)} %param.16) | copy-start | bytes 52
  4.4 2.0 %copy-start.15 = (f32[4]{0:T(128)S(1)}, f32[4]{0:T(128)}, u32[]{:S(2)}) copy-start(f32[4]{0:T(128)} %param.17) | copy-start | bytes 52
  7.9 1.3 copy-start
  53.3 1.2 copy-start.4
  54.5 1.1 copy-start.7
  96.6 1.2 copy-start.5
  97.7 1.1 copy-start.6
  140.4 1.1 copy-start.2
  141.6 44.3 %all-to-all-start = ((bf16[16,192,256]{2,1,0:T(8,128)(2,1)}), bf16[16,192,256]{2,1,0:T(8,128)(2,1)}, u32[]{:S(2)}, u32[]{:S(2)}) async-start(bf16[16,192,256]{2,1,0:T(8,128)(2,1)} %get-tuple-element.16), calls=%async_computation | async-start | bytes 3145728 | tf_op jit(solution)/shard_map/all_to_all | solution.py:588
  149.4 4.3 %copy-start.3 = (bf16[16,192,256]{2,1,0:T(8,128)(2,1)S(1)}, bf16[16,192,256]{2,1,0:T(8,128)(2,1)}, u32[]{:S(2)}) copy-start(bf16[16,192,256]{2,1,0:T(8,128)(2,1)} %copy-done.2) | copy-start | bytes 4718596

commit v6 on v4

--- a/solution.py
+++ b/solution.py
@@ -221,12 +221,17 @@
             cells = slice(part * TILE, (part + 1) * TILE)
             turned[:, cells] = lines[cells, :].T
 
-    start = pl.multiple_of(width - at * TILE, TILE)
-    out[0] = jnp.dot(turned[...], tall[pl.ds(start, width), :], preferred_element_type=F32)
+    blocks = out.shape[2] // TILE
+    for part in range(blocks):
+        start = pl.multiple_of(width - (at * blocks + part) * TILE, TILE)
+        out[0, :, part * TILE : (part + 1) * TILE] = jnp.dot(
+            turned[...], tall[pl.ds(start, width), :], preferred_element_type=F32
+        )
 
 
 def zonal_backward(lines, tall, variables, variable, gradient):
     width, rows = lines.shape
+    batch = 3 * TILE
     operands = [lines, tall]
     in_specs = [
         pl.BlockSpec((width, rows), lambda at: (0, 0)),
@@ -240,9 +245,9 @@
     return pl.pallas_call(
         functools.partial(zonal_backward_kernel, width),
         out_shape=jax.ShapeDtypeStruct((variables, rows, width), F32),
-        grid=(width // TILE,),
+        grid=(width // batch,),
         in_specs=in_specs,
-        out_specs=pl.BlockSpec((1, rows, TILE), lambda at: (variable, 0, at)),
+        out_specs=pl.BlockSpec((1, rows, batch), lambda at: (variable, 0, at)),
         scratch_shapes=[pltpu.VMEM((rows, width), BF16)],
         input_output_aliases=aliases,
         compiler_params=params(),

time: 186 us -> 184 us (0.989)
  Pallas kernels: 112 us -> 108 us
    pallas_call x2, Pallas kernels: 20.3 us -> 16.7 us  [zonal_backward(): pl.pallas_call(functools.partial(zonal_backward_kernel, width), out_shape...]
where the time goes in v6:
time: 184 us; the launch traced here: 183 us
  Pallas kernels  108 us (59%)
  waiting for transfers between devices  41.5 us (23%)
  starting transfers between devices  17.6 us (10%)
  local copies, waits for them, and re-layouts  10.2 us (6%)
  other arithmetic  2.57 us (1%)
    pallas_call x1, Pallas kernels, zonal_forward(): pl.pallas_call(functools.partial(zonal_forward_kernel, count), out_shape=...  44.2 us
    all_to_all x2, waiting for transfers between devices, on_device(): lax.all_to_all(back, 'lat', split_axis=0, concat_axis=0, tiled=True)  34.9 us
    pallas_call x2, Pallas kernels, at_reports(): pl.pallas_call(functools.partial(reports_kernel, variable, group, kept_ro...  26.9 us
    pallas_call x2, Pallas kernels, zonal_backward(): pl.pallas_call(functools.partial(zonal_backward_kernel, width), out_shape...  16.7 us
    pallas_call x2, Pallas kernels, meridional_forward(): pl.pallas_call(meridional_forward_kernel, out_shape=jax.ShapeDtypeStruct(...  10.4 us
    all_to_all x2, starting transfers between devices, on_device(): lax.all_to_all(back, 'lat', split_axis=0, concat_axis=0, tiled=True)  9.37 us
    all_to_all x1, starting transfers between devices, on_device(): lax.all_to_all(part, 'lat', split_axis=0, concat_axis=0, tiled=True)  7.37 us
    unnamed x33, local copies, waits for them, and re-layouts  7.12 us
  transfers between devices with their start and end apart: 7, of which 6 were waited for; matrix products, arithmetic and copies ran while one was open for 3% of the time, Pallas kernels for 31%

profile of v6, /device:TPU:12, one launch (start us, length us, event | category | flops | bytes accessed | tf_op | source)
XLA Modules:
  0.0 183.1 jit_solution(13092009106432579477)
XLA Ops:
  0.6 0.7 fusion.4
  1.3 0.1 pad_maximum_fusion.coef
  1.4 44.2 %shard_map.140 = (bf16[16,192,256]{2,1,0:T(8,128)(2,1)S(1)}, bf16[1,3072,256]{2,1,0:T(8,128)(2,1)}) custom-call(f32[8]{0:T(128)S(1)} %pad_maximum_fusion.coef, bf16[2,256,3072]{2,1,0:T(8,128)(2,1)} %bitcast.73), custom_call_target="tpu_custom_call" | custom-call | flops 9663676416 | bytes 7864320 | tf_op jit(solution)/shard_map/pallas_call | solution.py:185
  45.6 1.1 copy-done.2
  46.7 7.4 %all-to-all-start = ((bf16[16,192,256]{2,1,0:T(8,128)(2,1)}), bf16[16,192,256]{2,1,0:T(8,128)(2,1)}, u32[]{:S(2)}, u32[]{:S(2)}) async-start(bf16[16,192,256]{2,1,0:T(8,128)(2,1)} %bitcast.2), calls=%async_computation | async-start | bytes 3145728 | tf_op jit(solution)/shard_map/all_to_all | solution.py:515
  54.1 1.8 all-gather
  55.9 0.1 fusion.3
  56.0 0.1 broadcast_select_fusion
  56.1 0.1 iota_add_fusion
  56.2 0.1 add.64
  56.2 0.1 broadcast_in_dim.6
  56.3 0.1 reshape_reshape.3.lanes
  56.4 0.1 pad_maximum_fusion.1.coef
  56.5 1.3 shard_map.141.matrix
  57.9 1.4 copy-done.3
  59.3 4.0 %shard_map.144 = bf16[2,192,512]{2,1,0:T(8,128)(2,1)S(1)} custom-call(bf16[16,192,256]{2,1,0:T(8,128)(2,1)S(1)} %copy-done.3, bf16[8,256,512]{2,1,0:T(8,128)(2,1)S(1)} %shard_map.141.matrix), custom_call_target="tpu_custom_call" | custom-call | flops 805306368 | bytes 1572864 | tf_op jit(solution)/shard_map/pallas_call | solution.py:319
  63.3 0.8 slice_bitcast_fusion
  64.1 0.2 collective-permute-start.1
  64.3 0.1 copy.31
  64.4 0.1 broadcast_in_dim.15
  64.5 0.2 copy.34.maps
  64.7 0.4 copy.33.numbers
  65.1 0.8 and_select_fusion
  66.0 1.3 copy.32.ids
  67.3 1.2 copy-done.4
  68.6 0.9 copy-done.6
  69.5 13.9 %shard_map.145 = (f32[1,2048]{1,0:T(1,128)S(1)}, bf16[2,192,512]{2,1,0:T(8,128)(2,1)S(1)}) custom-call(bf16[192,512]{1,0:T(8,128)(2,1)S(1)} %copy-done.6, bf16[192,512]{1,0:T(8,128)(2,1)} %collective-permute-done.1.other, s32[2048,3]{1,0:T(8,128)S(1)} %copy-done.4, f32[2048,6]{1,0:T(8,128)S(1)} %copy.33.numbers, s32[1,2048]{1,0:T(1,128)S(1)} %get-tuple-element.22.cells, ...), custom_call_target="tpu_custom_call" | custom-call | flops 4294967296 | bytes 1048576 | tf_op jit(solution)/shard_map/pallas_call | solution.py:427
  83.5 0.4 collective-permute-start.3
  83.8 1.1 collective-permute-done.3.other
  85.0 2.6 %shard_map.148 = bf16[16,192,256]{2,1,0:T(8,128)(2,1)S(1)} custom-call(bf16[192,512]{1,0:T(8,128)(2,1)S(1)} %get-tuple-element.15.own, bf16[192,512]{1,0:T(8,128)(2,1)S(1)} %collective-permute-done.3.other, bf16[8,256,512]{2,1,0:T(8,128)(2,1)S(1)} %shard_map.141.matrix), custom_call_target="tpu_custom_call" | custom-call | flops 805306368 | bytes 1572864 | tf_op jit(solution)/shard_map/pallas_call | solution.py:356
  87.6 1.1 copy-done
  88.8 2.7 %all-to-all-done.lines = bf16[16,192,256]{2,1,0:T(8,128)(2,1)} async-done(((bf16[16,192,256]{2,1,0:T(8,128)(2,1)}), bf16[16,192,256]{2,1,0:T(8,128)(2,1)}, u32[]{:S(2)}, u32[]{:S(2)}) %all-to-all-start) | async-done | bytes 1572896 | tf_op jit(solution)/shard_map/all_to_all | solution.py:515
  91.5 4.9 %all-to-all-start.2 = ((bf16[16,192,256]{2,1,0:T(8,128)(2,1)}), bf16[16,192,256]{2,1,0:T(8,128)(2,1)}, u32[]{:S(2)}, u32[]{:S(2)}) async-start(bf16[16,192,256]{2,1,0:T(8,128)(2,1)} %copy-done), calls=%async_computation.2 | async-start | bytes 3145728 | tf_op jit(solution)/shard_map/all_to_all | solution.py:528
  96.4 6.4 %shard_map.142 = bf16[2,192,512]{2,1,0:T(8,128)(2,1)S(1)} custom-call(bf16[16,192,256]{2,1,0:T(8,128)(2,1)} %all-to-all-done.lines, bf16[8,256,512]{2,1,0:T(8,128)(2,1)S(1)} %shard_map.141.matrix), custom_call_target="tpu_custom_call" | custom-call | flops 805306368 | bytes 1572864 | tf_op jit(solution)/shard_map/pallas_call | solution.py:319
  102.8 0.1 collective-permute-start
  102.9 1.4 collective-permute-done.other
  104.3 13.0 %shard_map.143 = (f32[1,2048]{1,0:T(1,128)S(1)}, bf16[2,192,512]{2,1,0:T(8,128)(2,1)S(1)}) custom-call(bf16[192,512]{1,0:T(8,128)(2,1)S(1)} %get-tuple-element.21.own, bf16[192,512]{1,0:T(8,128)(2,1)S(1)} %collective-permute-done.other, s32[2048,3]{1,0:T(8,128)S(1)} %copy-done.5, f32[2048,6]{1,0:T(8,128)S(1)} %copy.33.numbers, ...), custom_call_target="tpu_custom_call" | custom-call | flops 4294967296 | bytes 1048576 | tf_op jit(solution)/shard_map/pallas_call | solution.py:427
  117.3 0.2 collective-permute-start.2
  117.5 1.3 collective-permute-done.2.other
  118.8 2.6 %shard_map.146 = bf16[16,192,256]{2,1,0:T(8,128)(2,1)S(1)} custom-call(bf16[192,512]{1,0:T(8,128)(2,1)S(1)} %get-tuple-element.17.own, bf16[192,512]{1,0:T(8,128)(2,1)S(1)} %collective-permute-done.2.other, bf16[8,256,512]{2,1,0:T(8,128)(2,1)S(1)} %shard_map.141.matrix), custom_call_target="tpu_custom_call" | custom-call | flops 805306368 | bytes 1572864 | tf_op jit(solution)/shard_map/pallas_call | solution.py:356
  121.5 1.1 copy-done.1
  122.6 10.9 %all-to-all-done.2 = bf16[16,192,256]{2,1,0:T(8,128)(2,1)} async-done(((bf16[16,192,256]{2,1,0:T(8,128)(2,1)}), bf16[16,192,256]{2,1,0:T(8,128)(2,1)}, u32[]{:S(2)}, u32[]{:S(2)}) %all-to-all-start.2) | async-done | bytes 1572896 | tf_op jit(solution)/shard_map/all_to_all | solution.py:528
  133.5 4.5 %all-to-all-start.1 = ((bf16[16,192,256]{2,1,0:T(8,128)(2,1)}), bf16[16,192,256]{2,1,0:T(8,128)(2,1)}, u32[]{:S(2)}, u32[]{:S(2)}) async-start(bf16[16,192,256]{2,1,0:T(8,128)(2,1)} %copy-done.1), calls=%async_computation.1 | async-start | bytes 3145728 | tf_op jit(solution)/shard_map/all_to_all | solution.py:528
  138.0 3.6 %shard_map.147.tall = bf16[6144,256]{1,0:T(8,128)(2,1)S(1)} custom-call(f32[8]{0:T(128)S(1)} %pad_maximum_fusion.coef), custom_call_target="tpu_custom_call" | custom-call | flops 47185920 | bytes 3145728 | tf_op jit(solution)/shard_map/pallas_call | solution.py:76
  141.7 0.6 fusion.2
  142.3 8.4 %shard_map.149.rest_0_ = f32[2,256,3072]{2,1,0:T(8,128)} custom-call(bf16[3072,256]{1,0:T(8,128)(2,1)} %bitcast.29.lines, bf16[6144,256]{1,0:T(8,128)(2,1)S(1)} %shard_map.147.tall), custom_call_target="tpu_custom_call" | custom-call | flops 4831838208 | bytes 9437184 | tf_op jit(solution)/shard_map/pallas_call | solution.py:245
  150.6 24.1 %all-to-all-done.1 = bf16[16,192,256]{2,1,0:T(8,128)(2,1)} async-done(((bf16[16,192,256]{2,1,0:T(8,128)(2,1)}), bf16[16,192,256]{2,1,0:T(8,128)(2,1)}, u32[]{:S(2)}, u32[]{:S(2)}) %all-to-all-start.1) | async-done | bytes 1572896 | tf_op jit(solution)/shard_map/all_to_all | solution.py:528
  174.7 8.4 %shard_map.150 = f32[2,256,3072]{2,1,0:T(8,128)} custom-call(bf16[3072,256]{1,0:T(8,128)(2,1)} %bitcast.26.lines, bf16[6144,256]{1,0:T(8,128)(2,1)S(1)} %shard_map.147.tall, f32[2,256,3072]{2,1,0:T(8,128)} %shard_map.149.rest_0_), custom_call_target="tpu_custom_call", output_to_operand_aliasing={{}: (2, {})} | custom-call | flops 4831838208 | bytes 9437184 | tf_op jit(solution)/shard_map/pallas_call | solution.py:245
  (37 shorter events, 0.3 us)
Async XLA Ops:
  45.6 1.1 copy-start.2
  46.7 7.4 %copy-start.13 = (s32[1,1,2,2]{3,2,1,0:T(2,128)S(1)}, s32[1,1,2,2]{3,2,1,0:T(2,128)}, u32[]{:S(2)}) copy-start(s32[1,1,2,2]{3,2,1,0:T(2,128)} %param.19) | copy-start | bytes 52
  46.7 9.7 %copy-start.14 = (f32[4]{0:T(128)S(1)}, f32[4]{0:T(128)}, u32[]{:S(2)}) copy-start(f32[4]{0:T(128)} %param.16) | copy-start | bytes 52
  46.7 9.7 %copy-start.15 = (f32[4]{0:T(128)S(1)}, f32[4]{0:T(128)}, u32[]{:S(2)}) copy-start(f32[4]{0:T(128)} %param.17) | copy-start | bytes 52
  46.7 44.8 %all-to-all-start = ((bf16[16,192,256]{2,1,0:T(8,128)(2,1)}), bf16[16,192,256]{2,1,0:T(8,128)(2,1)}, u32[]{:S(2)}, u32[]{:S(2)}) async-start(bf16[16,192,256]{2,1,0:T(8,128)(2,1)} %bitcast.2), calls=%async_computation | async-start | bytes 3145728 | tf_op jit(solution)/shard_map/all_to_all | solution.py:515
  57.9 1.4 copy-start.3
  59.3 5.0 %copy-start.8 = (bf16[2,64,64]{2,1,0:T(8,128)(2,1)S(1)}, bf16[2,64,64]{2,1,0:T(8,128)(2,1)}, u32[]{:S(2)}) copy-start(bf16[2,64,64]{2,1,0:T(8,128)(2,1)} %param.18) | copy-start | bytes 49156
  63.3 1.4 copy-start.7
  63.3 1.4 copy-start.10
  63.3 1.4 copy-start.11
  63.3 1.8 copy-start.12
  64.1 1.9 %copy-start.9 = (s32[1,1,2048]{2,1,0:T(1,128)S(1)}, s32[1,1,2048]{2,1,0:T(1,128)}, u32[]{:S(2)}) copy-start(s32[1,1,2048]{2,1,0:T(1,128)} %param.21) | copy-start | bytes 24580
  64.1 3.3 %collective-permute-start.1 = (bf16[192,512]{1,0:T(8,128)(2,1)}, bf16[192,512]{1,0:T(8,128)(2,1)}, u32[]{:S(2)}, u32[]{:S(2)}) collective-permute-start(bf16[192,512]{1,0:T(8,128)(2,1)} %get-tuple-element.18), channel_id=1, source_target_pairs={{0,1},{1,0},{2,3},{3,2},{4,5},{5,4},{6,7},{7,6},{8,9},{9,8},{10,11... | collective-permute-start | bytes 589832 | tf_op jit(solution)/shard_map/ppermute | solution.py:521
  67.3 1.2 copy-start.4
  68.6 0.9 copy-start.6
  83.5 1.5 collective-permute-start.3
  87.6 1.1 copy-start
  91.5 42.0 %all-to-all-start.2 = ((bf16[16,192,256]{2,1,0:T(8,128)(2,1)}), bf16[16,192,256]{2,1,0:T(8,128)(2,1)}, u32[]{:S(2)}, u32[]{:S(2)}) async-start(bf16[16,192,256]{2,1,0:T(8,128)(2,1)} %copy-done), calls=%async_computation.2 | async-start | bytes 3145728 | tf_op jit(solution)/shard_map/all_to_all | solution.py:528
  96.3 7.9 %copy-start.5 = (s32[2048,3]{1,0:T(8,128)S(1)}, s32[2048,3]{1,0:T(8,128)}, u32[]{:S(2)}) copy-start(s32[2048,3]{1,0:T(8,128)} %copy.32.ids) | copy-start | bytes 73732
  102.8 1.5 collective-permute-start
  117.3 1.5 collective-permute-start.2
  121.5 1.2 copy-start.1
  133.5 41.2 %all-to-all-start.1 = ((bf16[16,192,256]{2,1,0:T(8,128)(2,1)}), bf16[16,192,256]{2,1,0:T(8,128)(2,1)}, u32[]{:S(2)}, u32[]{:S(2)}) async-start(bf16[16,192,256]{2,1,0:T(8,128)(2,1)} %copy-done.1), calls=%async_computation.1 | async-start | bytes 3145728 | tf_op jit(solution)/shard_map/all_to_all | solution.py:528
